TPU v7x, 32 devices: a whole 2x2x4 slice. The times are simulated.
32 devices in a mesh: seq: 4 (over y, x), dp: 8 (over z, core).
Axes of the slice: x: 2, y: 2, z: 4, core: 2. Of those that a mesh axis runs over, the one named last changes fastest.
Arguments:
- tokens: bfloat16 [8, 2048, 1024], P('dp', 'seq'), may hold values from -6 to 6
- cotangent: bfloat16 [8, 2048, 1024], P('dp', 'seq'), may hold values from -6 to 6
- block_order: int32 [8, 4], P('dp'), may hold values from 0 to 3, each once within a row
- joint_weight: bfloat16 [1024, 3072], P(('seq', 'dp')), may hold values from -0.1875 to 0.1875
- query_bias: bfloat16 [1024], P(('seq', 'dp')), may hold values from -3 to 3
- value_bias: bfloat16 [1024], P(('seq', 'dp')), may hold values from -3 to 3
- projection: bfloat16 [1024, 1024], P(('seq', 'dp')), may hold values from -0.75 to 0.75
- offset: bfloat16 [1024], P(('seq', 'dp')), may hold values from -3 to 3
- first_gain: bfloat16 [1024], P(('seq', 'dp')), may hold values from 0.099609375 to 1.8984375
- first_shift: bfloat16 [1024], P(('seq', 'dp')), may hold values from -3 to 3
- upward_weight: bfloat16 [1024, 4096], P(('seq', 'dp')), may hold values from -0.1875 to 0.1875
- upward_bias: bfloat16 [4096], P(('seq', 'dp')), may hold values from -3 to 3
- downward_weight: bfloat16 [4096, 1024], P(('seq', 'dp')), may hold values from -0.09375 to 0.09375
- downward_bias: bfloat16 [1024], P(('seq', 'dp')), may hold values from -3 to 3
- second_gain: bfloat16 [1024], P(('seq', 'dp')), may hold values from 0.099609375 to 1.8984375
- second_shift: bfloat16 [1024], P(('seq', 'dp')), may hold values from -3 to 3
Outputs:
- output: bfloat16 [8, 2048, 1024], P('dp', 'seq')
- input_grad: bfloat16 [8, 2048, 1024], P('dp', 'seq')
- joint_grad: float32 [1024, 3072], P(('seq', 'dp'))
- query_grad: float32 [1024], P(('seq', 'dp'))
- value_grad: float32 [1024], P(('seq', 'dp'))
- projection_grad: float32 [1024, 1024], P(('seq', 'dp'))
- offset_grad: float32 [1024], P(('seq', 'dp'))
- firstgain_grad: float32 [1024], P(('seq', 'dp'))
- firstshift_grad: float32 [1024], P(('seq', 'dp'))
- upward_grad: float32 [1024, 4096], P(('seq', 'dp'))
- upwardbias_grad: float32 [4096], P(('seq', 'dp'))
- downward_grad: float32 [4096, 1024], P(('seq', 'dp'))
- downwardbias_grad: float32 [1024], P(('seq', 'dp'))
- secondgain_grad: float32 [1024], P(('seq', 'dp'))
- secondshift_grad: float32 [1024], P(('seq', 'dp'))
Inputs may be any that keep to these rules, and one draw needn't show every extreme that they name: Each row is an ordering of the 4 position blocks of one sequence: index j of seq holds block block_order[s, j].
All inputs are finite; a program needn't handle non-finite values.
Results may differ from a plain program's by a relative error of at most 0.02.
Values may be sent and summed in bfloat16 or wider, within the bound.
No kernel may reach another device: no remote copies, remote signals or barrier semaphores. Data moves between devices by JAX's collectives and lax.ppermute only.
A program may use at most 256 MiB of HBM per device.

v0:
```python
from functools import partial
import math

import jax
import jax.numpy as jnp
from jax import lax
from jax.sharding import PartitionSpec as P

HEADS = 16


epsilon = 1e-05
masked_score = -1e30


def passed_along(value, axis, by):
    count = lax.axis_size(axis)
    return lax.ppermute(value, axis, [(i, (i + by) % count) for i in range(count)])


def layer_norm(values, scaling, shifting):
    average = jnp.mean(values, -1, keepdims=True)
    centered = values - average
    variance = jnp.mean(centered * centered, -1, keepdims=True)
    return centered * lax.rsqrt(variance + epsilon) * scaling + shifting


def gelu_tanh(values):
    return jax.nn.gelu(values, approximate=True)


def head_slopes(number_heads, sequence_length):
    return 2.0 ** (-8.0 * (jnp.arange(number_heads, dtype=jnp.float32) + 1.0) / number_heads) * (
        4.0 / sequence_length
    )


def matmul(left, right):
    return jnp.dot(left, right, preferred_element_type=jnp.float32)


def left_transposed(left, right):
    return lax.dot_general(
        left, right, (((0,), (0,)), ((), ())), preferred_element_type=jnp.float32
    )


def right_transposed(left, right):
    return lax.dot_general(
        left, right, (((1,), (1,)), ((), ())), preferred_element_type=jnp.float32
    )


def score_block(block_queries, block_keys, query_place, key_place, slopes, factor):
    products = (
        jnp.einsum("qhe,khe->hqk", block_queries, block_keys, preferred_element_type=jnp.float32)
        * factor
    )
    distance = (key_place[None, :] - query_place[:, None]).astype(jnp.float32)
    allowed = key_place[None, :] <= query_place[:, None]
    scores = jnp.where(
        allowed[None], products + slopes[:, None, None] * distance[None], masked_score
    )
    return (scores, allowed)


def forward_block(
    carried, block_queries, block_keys, block_values, query_place, key_place, slopes, factor
):
    maximum, weight_sum, summed = carried
    scores, allowed = score_block(block_queries, block_keys, query_place, key_place, slopes, factor)
    new_maximum = jnp.maximum(maximum, jnp.max(scores, -1))
    weights = jnp.where(allowed[None], jnp.exp(scores - new_maximum[..., None]), 0.0)
    rescale = jnp.exp(maximum - new_maximum)
    weight_sum = weight_sum * rescale + jnp.sum(weights, -1)
    summed = summed * rescale[..., None] + jnp.einsum(
        "hqk,khe->hqe",
        weights.astype(jnp.bfloat16),
        block_values,
        preferred_element_type=jnp.float32,
    )
    return (new_maximum, weight_sum, summed)


def backward_block(
    carried,
    block_queries,
    block_keys,
    block_values,
    grad_attended,
    delta_rows,
    log_sums,
    query_place,
    key_place,
    slopes,
    factor,
):
    grad_queries, grad_keys, grad_values = carried
    scores, allowed = score_block(block_queries, block_keys, query_place, key_place, slopes, factor)
    weights = jnp.where(allowed[None], jnp.exp(scores - log_sums[..., None]), 0.0)
    grad_weights = jnp.einsum(
        "qhe,khe->hqk", grad_attended, block_values, preferred_element_type=jnp.float32
    )
    grad_scores = (weights * (grad_weights - delta_rows[..., None])).astype(jnp.bfloat16)
    grad_queries = (
        grad_queries
        + jnp.einsum("hqk,khe->qhe", grad_scores, block_keys, preferred_element_type=jnp.float32)
        * factor
    )
    grad_keys = (
        grad_keys
        + jnp.einsum("hqk,qhe->khe", grad_scores, block_queries, preferred_element_type=jnp.float32)
        * factor
    )
    grad_values = grad_values + jnp.einsum(
        "hqk,qhe->khe",
        weights.astype(jnp.bfloat16),
        grad_attended,
        preferred_element_type=jnp.float32,
    )
    return (grad_queries, grad_keys, grad_values)


def guarded(needed, update, carried, operands):
    return lax.cond(
        needed,
        lambda current, given: update(current, *given),
        lambda current, given: current,
        carried,
        operands,
    )


def body(
    tokens,
    cotangent,
    block_order,
    joint_weight,
    query_bias,
    value_bias,
    projection,
    offset,
    first_gain,
    first_shift,
    upward_weight,
    upward_bias,
    downward_weight,
    downward_bias,
    second_gain,
    second_shift,
):
    members, length, features = tokens.shape
    total_rows = members * length
    head_dim = features // HEADS
    cycle_size = lax.axis_size("seq")
    cycle_place = lax.axis_index("seq")
    factor = 1.0 / math.sqrt(head_dim)
    slopes = head_slopes(HEADS, length * cycle_size)
    attention_parts = (
        lax.all_gather(joint_weight, ("seq", "dp"), axis=0, tiled=True),
        lax.all_gather(query_bias, ("seq", "dp"), axis=0, tiled=True),
        lax.all_gather(value_bias, ("seq", "dp"), axis=0, tiled=True),
        lax.all_gather(projection, ("seq", "dp"), axis=0, tiled=True),
        lax.all_gather(offset, ("seq", "dp"), axis=0, tiled=True),
        lax.all_gather(first_gain, ("seq", "dp"), axis=0, tiled=True),
        lax.all_gather(first_shift, ("seq", "dp"), axis=0, tiled=True),
    )
    feedforward_parts = (
        lax.all_gather(upward_weight, ("seq", "dp"), axis=0, tiled=True),
        lax.all_gather(upward_bias, ("seq", "dp"), axis=0, tiled=True),
        lax.all_gather(downward_weight, ("seq", "dp"), axis=0, tiled=True),
        lax.all_gather(downward_bias, ("seq", "dp"), axis=0, tiled=True),
        lax.all_gather(second_gain, ("seq", "dp"), axis=0, tiled=True),
        lax.all_gather(second_shift, ("seq", "dp"), axis=0, tiled=True),
    )
    joint_full, query_add, value_add, projection_full, offset_add, gain_one, shift_one = (
        attention_parts
    )
    upward_full, upward_add, downward_full, downward_add, gain_two, shift_two = feedforward_parts
    inputs = tokens.reshape(total_rows, features).astype(jnp.float32)
    normed, first_pull = jax.vjp(
        layer_norm, inputs, gain_one.astype(jnp.float32), shift_one.astype(jnp.float32)
    )
    normed_low = normed.astype(jnp.bfloat16)
    mixture = matmul(normed_low, joint_full)
    queries = (mixture[:, :features] + query_add.astype(jnp.float32)).astype(jnp.bfloat16)
    queries = queries.reshape(members, length, HEADS, head_dim)
    keys_local = (
        mixture[:, features : 2 * features]
        .astype(jnp.bfloat16)
        .reshape(members, length, HEADS, head_dim)
    )
    values_local = (mixture[:, 2 * features :] + value_add.astype(jnp.float32)).astype(jnp.bfloat16)
    values_local = values_local.reshape(members, length, HEADS, head_dim)
    home_pair = jnp.stack((keys_local, values_local))
    block_offsets = jnp.arange(length, dtype=jnp.int32)
    query_blocks = lax.dynamic_index_in_dim(block_order, cycle_place, 1, keepdims=False)
    query_places = query_blocks[:, None] * length + block_offsets[None, :]
    forward_update = partial(forward_block, factor=factor)
    states = [
        (
            jnp.full((HEADS, length), masked_score, jnp.float32),
            jnp.zeros((HEADS, length), jnp.float32),
            jnp.zeros((HEADS, length, head_dim), jnp.float32),
        )
    ]
    moving = home_pair
    received = []
    for cycle_step in range(cycle_size):
        received.append(moving)
        source = (cycle_place - cycle_step) % cycle_size
        key_blocks = lax.dynamic_index_in_dim(block_order, source, 1, keepdims=False)
        member = 0
        key_places = key_blocks[member] * length + block_offsets
        operands = (
            queries[member],
            moving[0, member],
            moving[1, member],
            query_places[member],
            key_places,
            slopes,
        )
        states[member] = guarded(
            key_blocks[member] <= query_blocks[member], forward_update, states[member], operands
        )
        if cycle_step + 1 < cycle_size:
            moving = passed_along(moving, "seq", 1)
    member = 0
    maximum, weight_sum, summed = states[member]
    attended_list = [summed / weight_sum[..., None]]
    log_list = [maximum + jnp.log(weight_sum)]
    attended_full = jnp.stack(attended_list)
    attended_low = (
        attended_full.transpose(0, 2, 1, 3).reshape(total_rows, features).astype(jnp.bfloat16)
    )
    middle = inputs + matmul(attended_low, projection_full) + offset_add.astype(jnp.float32)
    second, second_pull = jax.vjp(
        layer_norm, middle, gain_two.astype(jnp.float32), shift_two.astype(jnp.float32)
    )
    second_low = second.astype(jnp.bfloat16)
    hidden = matmul(second_low, upward_full) + upward_add.astype(jnp.float32)
    active, gelu_pull = jax.vjp(gelu_tanh, hidden)
    active_low = active.astype(jnp.bfloat16)
    result = matmul(active_low, downward_full) + downward_add.astype(jnp.float32)
    output = (middle + result).astype(jnp.bfloat16).reshape(members, length, features)
    attention_parts = (
        lax.all_gather(joint_weight, ("seq", "dp"), axis=0, tiled=True),
        lax.all_gather(query_bias, ("seq", "dp"), axis=0, tiled=True),
        lax.all_gather(value_bias, ("seq", "dp"), axis=0, tiled=True),
        lax.all_gather(projection, ("seq", "dp"), axis=0, tiled=True),
        lax.all_gather(offset, ("seq", "dp"), axis=0, tiled=True),
        lax.all_gather(first_gain, ("seq", "dp"), axis=0, tiled=True),
        lax.all_gather(first_shift, ("seq", "dp"), axis=0, tiled=True),
    )
    feedforward_parts = (
        lax.all_gather(upward_weight, ("seq", "dp"), axis=0, tiled=True),
        lax.all_gather(upward_bias, ("seq", "dp"), axis=0, tiled=True),
        lax.all_gather(downward_weight, ("seq", "dp"), axis=0, tiled=True),
        lax.all_gather(downward_bias, ("seq", "dp"), axis=0, tiled=True),
        lax.all_gather(second_gain, ("seq", "dp"), axis=0, tiled=True),
        lax.all_gather(second_shift, ("seq", "dp"), axis=0, tiled=True),
    )
    joint_full = attention_parts[0]
    projection_full = attention_parts[3]
    upward_full = feedforward_parts[0]
    downward_full = feedforward_parts[2]
    grad_result = cotangent.reshape(total_rows, features)
    grad_result_full = grad_result.astype(jnp.float32)
    downward_grad = left_transposed(active_low, grad_result)
    downwardbias_grad = jnp.sum(grad_result_full, 0)
    (grad_hidden,) = gelu_pull(right_transposed(grad_result, downward_full))
    grad_hidden_low = grad_hidden.astype(jnp.bfloat16)
    upward_grad = left_transposed(second_low, grad_hidden_low)
    upwardbias_grad = jnp.sum(grad_hidden_low.astype(jnp.float32), 0)
    grad_second = right_transposed(grad_hidden_low, upward_full)
    middle_part, secondgain_grad, secondshift_grad = second_pull(grad_second)
    feedforward_sums = (
        lax.psum_scatter(upward_grad, ("seq", "dp"), scatter_dimension=0, tiled=True),
        lax.psum_scatter(upwardbias_grad, ("seq", "dp"), scatter_dimension=0, tiled=True),
        lax.psum_scatter(downward_grad, ("seq", "dp"), scatter_dimension=0, tiled=True),
        lax.psum_scatter(downwardbias_grad, ("seq", "dp"), scatter_dimension=0, tiled=True),
        lax.psum_scatter(secondgain_grad, ("seq", "dp"), scatter_dimension=0, tiled=True),
        lax.psum_scatter(secondshift_grad, ("seq", "dp"), scatter_dimension=0, tiled=True),
    )
    grad_middle = grad_result_full + middle_part
    grad_branch = grad_middle.astype(jnp.bfloat16)
    projection_grad = left_transposed(attended_low, grad_branch)
    offset_grad = jnp.sum(grad_branch.astype(jnp.float32), 0)
    grad_attended = right_transposed(grad_branch, projection_full).astype(jnp.bfloat16)
    grad_attended = grad_attended.reshape(members, length, HEADS, head_dim)
    delta_list = [jnp.einsum("qhe,hqe->hq", grad_attended[0].astype(jnp.float32), attended_full[0])]
    backward_update = partial(backward_block, factor=factor)
    query_grads = [jnp.zeros((length, HEADS, head_dim), jnp.float32)]
    travelling = jnp.zeros((2, members, length, HEADS, head_dim), jnp.float32)
    moving = home_pair
    for cycle_step in range(cycle_size):
        source = (cycle_place - cycle_step) % cycle_size
        key_blocks = lax.dynamic_index_in_dim(block_order, source, 1, keepdims=False)
        member = 0
        key_places = key_blocks[member] * length + block_offsets
        operands = (
            queries[member],
            moving[0, member],
            moving[1, member],
            grad_attended[member],
            delta_list[member],
            log_list[member],
            query_places[member],
            key_places,
            slopes,
        )
        carried = (query_grads[member], travelling[0, member], travelling[1, member])
        carried = guarded(
            key_blocks[member] <= query_blocks[member], backward_update, carried, operands
        )
        query_grads[member] = carried[0]
        key_list = [carried[1]]
        value_list = [carried[2]]
        travelling = jnp.stack((jnp.stack(key_list), jnp.stack(value_list)))
        travelling = passed_along(travelling.astype(jnp.bfloat16), "seq", 1).astype(
            travelling.dtype
        )
        if cycle_step + 1 < cycle_size:
            moving = passed_along(moving, "seq", 1)
    grad_queries = jnp.stack(query_grads).astype(jnp.bfloat16).reshape(total_rows, features)
    grad_keys = travelling[0].astype(jnp.bfloat16).reshape(total_rows, features)
    grad_values = travelling[1].astype(jnp.bfloat16).reshape(total_rows, features)
    grad_mixture = jnp.concatenate((grad_queries, grad_keys, grad_values), 1)
    joint_grad = left_transposed(normed_low, grad_mixture)
    query_grad = jnp.sum(grad_queries.astype(jnp.float32), 0)
    value_grad = jnp.sum(grad_values.astype(jnp.float32), 0)
    grad_normed = right_transposed(grad_mixture, joint_full)
    input_part, firstgain_grad, firstshift_grad = first_pull(grad_normed)
    input_grad = (grad_middle + input_part).astype(jnp.bfloat16).reshape(members, length, features)
    attention_sums = (
        lax.psum_scatter(joint_grad, ("seq", "dp"), scatter_dimension=0, tiled=True),
        lax.psum_scatter(query_grad, ("seq", "dp"), scatter_dimension=0, tiled=True),
        lax.psum_scatter(value_grad, ("seq", "dp"), scatter_dimension=0, tiled=True),
        lax.psum_scatter(projection_grad, ("seq", "dp"), scatter_dimension=0, tiled=True),
        lax.psum_scatter(offset_grad, ("seq", "dp"), scatter_dimension=0, tiled=True),
        lax.psum_scatter(firstgain_grad, ("seq", "dp"), scatter_dimension=0, tiled=True),
        lax.psum_scatter(firstshift_grad, ("seq", "dp"), scatter_dimension=0, tiled=True),
    )
    return (
        output,
        input_grad,
        attention_sums[0],
        attention_sums[1],
        attention_sums[2],
        attention_sums[3],
        attention_sums[4],
        attention_sums[5],
        attention_sums[6],
        feedforward_sums[0],
        feedforward_sums[1],
        feedforward_sums[2],
        feedforward_sums[3],
        feedforward_sums[4],
        feedforward_sums[5],
    )


def solution(mesh):
    in_specs = (
        P("dp", "seq", None),
        P("dp", "seq", None),
        P("dp", None),
        P(("seq", "dp"), None),
        P(("seq", "dp")),
        P(("seq", "dp")),
        P(("seq", "dp"), None),
        P(("seq", "dp")),
        P(("seq", "dp")),
        P(("seq", "dp")),
        P(("seq", "dp"), None),
        P(("seq", "dp")),
        P(("seq", "dp"), None),
        P(("seq", "dp")),
        P(("seq", "dp")),
        P(("seq", "dp")),
    )
    out_specs = (
        P("dp", "seq", None),
        P("dp", "seq", None),
        P(("seq", "dp"), None),
        P(("seq", "dp")),
        P(("seq", "dp")),
        P(("seq", "dp"), None),
        P(("seq", "dp")),
        P(("seq", "dp")),
        P(("seq", "dp")),
        P(("seq", "dp"), None),
        P(("seq", "dp")),
        P(("seq", "dp"), None),
        P(("seq", "dp")),
        P(("seq", "dp")),
        P(("seq", "dp")),
    )
    return jax.shard_map(body, mesh=mesh, in_specs=in_specs, out_specs=out_specs, check_vma=False)
```

profile of v0, /device:TPU:0, one launch (start us, length us, event | category | flops | bytes accessed | tf_op | source)
XLA Modules:
  0.0 1362.8 jit_solution(5772942415269895619)
XLA Ops:
  16.7 42.4 %all-reduce.18 = (bf16[1024]{0:T(1024)(128)(2,1)S(1)}, bf16[1024]{0:T(1024)(128)(2,1)S(1)}, bf16[1024]{0:T(1024)(128)(2,1)S(1)}, bf16[1024]{0:T(1024)(128)(2,1)S...) all-reduce(bf16[1024]{0:T(1024)(128)(2,1)S(1)} %dynamic-update-slic, ...), channel_id=1, replica_groups=mesh['seq'=4,'dp'=8] {'seq','dp'}, use_global_device_ids=true, to_apply=%add.1 | all-reduce | flops 8192 | bytes 32768
  62.9 20.4 %all-gather.6.cloned.1.call-done = bf16[1024,3072]{1,0:T(8,128)(2,1)} async-done(((bf16[32,3072]{1,0:T(8,128)(2,1)}), bf16[1024,3072]{1,0:T(8,128)(2,1)}) %all-gather.6.cloned.1.call-update) | async-done | bytes 6291472 | tf_op jit(solution)/shard_map/all_gather | solution.py:160
  99.2 52.8 %collective-permute-done = bf16[2,1,512,16,64]{2,4,3,1,0:T(8,128)(2,1)S(1)} collective-permute-done((bf16[2,1,512,16,64]{2,4,3,1,0:T(8,128)(2,1)S(1)}, bf16[2,1,512,16,64]{2,4,3,1,0:T(8,128)(2,1)S(1)}, u32[]{:S(2)}, u32[]{:S(2)}) %collective-permute-start) | collective-permute-done | bytes 2097184 | tf_op jit(solution)/shard_map/ppermute | solution.py:18
  153.9 62.3 %collective-permute-done.1 = bf16[2,1,512,16,64]{2,4,3,1,0:T(8,128)(2,1)} collective-permute-done((bf16[2,1,512,16,64]{2,4,3,1,0:T(8,128)(2,1)S(1)}, bf16[2,1,512,16,64]{2,4,3,1,0:T(8,128)(2,1)}, u32[]{:S(2)}, u32[]{:S(2)}) %collective-permute-start.1) | collective-permute-done | bytes 2097184 | tf_op jit(solution)/shard_map/ppermute | solution.py:18
  225.6 38.6 %all-gather = bf16[32,1,128]{2,1,0:T(2,128)(2,1)S(1)} all-gather(bf16[1,1,128]{2,1,0:T(2,128)(2,1)S(1)} %bitcast.288), channel_id=1, replica_groups=mesh['seq'=4,'dp'=8] {'seq','dp'}, dimensions={0}, use_global_device_ids=true | all-gather | bytes 8448 | tf_op jit(solution)/shard_map/all_gather | solution.py:170
  265.9 26.9 %conditional.8 = (f32[16,512]{1,0:T(8,128)}, f32[16,512]{1,0:T(8,128)S(1)}, f32[16,512,64]{1,2,0:T(8,128)S(1)}) conditional(s32[]{:T(128)} %bitcast.34, () %tuple.126, (s32[512]{0:T(512)S(1)}, s32[1,512]{1,0:T(1,128)S(1)}, bf16[512,16,64]{0,2,1:T(8,128)(2,1)S(1)}, bf16[512,16,64]{0,2,1:T(8,128)(2,1)S(1)}, f32[16]{0:T(128)S(1)}, ...), branch_computations={%region_2.3_spmd, %region_3.6_spmd} | conditional | flops 1121222656 | bytes 63283316 | solution.py:125
  295.8 29.8 %conditional.9 = ((f32[16,512]{1,0:T(8,128)}, f32[16,512]{1,0:T(8,128)S(1)}, f32[16,512,64]{1,2,0:T(8,128)S(1)})) conditional(s32[]{:T(128)} %bitcast.33, (f32[16,512]{1,0:T(8,128)}, f32[16,512]{1,0:T(8,128)S(1)}, f32[16,512,64]{1,2,0:T(8,128)S(1)}) %conditional.8, (s32[512]{0:T(512)S(1)}, s32[1,512]{1,0:T(1,128)S(1)}, ...), branch_computations={%region_6.7_spmd, %region_7.10_spmd} | conditional | flops 1121730560 | bytes 61350268 | solution.py:125
  332.0 31.2 %conditional.11 = (f32[16,512]{1,0:T(8,128)S(1)}, f32[16,512,64]{1,2,0:T(8,128)S(1)}, f32[16,512]{1,0:T(8,128)}) conditional(s32[]{:T(128)} %bitcast.31, (f32[16,512]{1,0:T(8,128)}, f32[16,512]{1,0:T(8,128)S(1)}, f32[16,512,64]{1,2,0:T(8,128)S(1)}) %get-tuple-element.673, (s32[512]{0:T(512)S(1)}, s32[1,512]{1,0:T(1,128)S(1)}, ...), branch_computations={%region_14.15_spmd.clone, %region_15.18_spmd.clone} | conditional | flops 1121730560 | bytes 61349976 | solution.py:125
  370.6 11.9 fusion.136
  382.5 27.4 %convert_reduce_fusion = (f32[4096]{0:T(1024)}, bf16[512,4096]{1,0:T(8,128)(2,1)S(1)}) fusion(f32[512,4096]{1,0:T(8,128)} %fusion.136, f32[4096]{0:T(1024)S(1)} %bitcast.285, bf16[4096,1024]{1,0:T(8,128)(2,1)} %all-gather.12.cloned.1.call-done, bf16[1,512,1024]{2,1,0:T(8,128)(2,1)} %param.33), kind=kOutput, calls=%fused_computation.128 | convolution fusion | flops 4343197696 | bytes 22052864 | tf_op jit(solution)/shard_map/dot_general | solution.py:49
  429.9 32.5 %conditional.12 = (f32[512,16,64]{0,2,1:T(8,128)S(1)}, bf16[1,1,512,16,64]{2,4,3,1,0:T(8,128)(2,1)}, bf16[1,1,512,16,64]{2,4,3,1,0:T(8,128)(2,1)}) conditional(s32[]{:T(128)} %bitcast.34, () %tuple.131, (s32[512]{0:T(512)S(1)}, s32[1,512]{1,0:T(1,128)S(1)}, bf16[512,16,64]{0,2,1:T(8,128)(2,1)S(1)}, bf16[512,16,64]{0,2,1:T(8,128)(2,1)}, ...), branch_computations={%region_22.23_spmd, %region_23.24_spmd} | conditional | flops 2754347008 | bytes 170762528 | solution.py:125
  464.2 44.5 %collective-permute-done.3 = bf16[2,1,512,16,64]{2,4,3,1,0:T(8,128)(2,1)S(1)} collective-permute-done((bf16[2,1,512,16,64]{2,4,3,1,0:T(8,128)(2,1)S(1)}, bf16[2,1,512,16,64]{2,4,3,1,0:T(8,128)(2,1)S(1)}, u32[]{:S(2)}, u32[]{:S(2)}) %collective-permute-start.3) | collective-permute-done | bytes 2097184 | tf_op jit(solution)/shard_map/ppermute | solution.py:18
  511.1 36.0 %conditional.13 = (f32[512,16,64]{0,2,1:T(8,128)S(1)}, bf16[1,1,512,16,64]{2,4,3,1,0:T(8,128)(2,1)}, bf16[1,1,512,16,64]{2,4,3,1,0:T(8,128)(2,1)}) conditional(s32[]{:T(128)} %bitcast.33, (f32[512,16,64]{0,2,1:T(8,128)S(1)}, f32[512,16,64]{0,2,1:T(8,128)}, f32[512,16,64]{0,2,1:T(8,128)S(1)}) %tuple.133, (s32[512]{0:T(512)S(1)}, ...), branch_computations={%region_24.25_spmd, %region_25.26_spmd} | conditional | flops 2755919872 | bytes 164470976 | solution.py:125
  555.3 35.9 %collective-permute-done.4 = bf16[2,1,512,16,64]{2,4,3,1,0:T(8,128)(2,1)} collective-permute-done((bf16[2,1,512,16,64]{2,4,3,1,0:T(8,128)(2,1)}, bf16[2,1,512,16,64]{2,4,3,1,0:T(8,128)(2,1)}, u32[]{:S(2)}, u32[]{:S(2)}) %collective-permute-start.4) | collective-permute-done | bytes 2097184 | tf_op jit(solution)/shard_map/ppermute | solution.py:18
  600.3 64.9 %collective-permute-start.5 = (bf16[2,1,512,16,64]{2,4,3,1,0:T(8,128)(2,1)S(1)}, bf16[2,1,512,16,64]{2,4,3,1,0:T(8,128)(2,1)S(1)}, u32[]{:S(2)}, u32[]{:S(2)}) collective-permute-start(bf16[2,1,512,16,64]{2,4,3,1,0:T(8,128)(2,1)S(1)} %pad_maximum_fusion.4), channel_id=1, source_target_pairs={{0,8},{8,16},{16,24},{24,0},{1,9},{9,17},{17,25},{25,1},{2,10},{10... | collective-permute-start | bytes 6291464 | tf_op jit(solution)/shard_map/ppermute | solution.py:18
  665.2 44.0 %collective-permute-done.5 = bf16[2,1,512,16,64]{2,4,3,1,0:T(8,128)(2,1)S(1)} collective-permute-done((bf16[2,1,512,16,64]{2,4,3,1,0:T(8,128)(2,1)S(1)}, bf16[2,1,512,16,64]{2,4,3,1,0:T(8,128)(2,1)S(1)}, u32[]{:S(2)}, u32[]{:S(2)}) %collective-permute-start.5) | collective-permute-done | bytes 2097184 | tf_op jit(solution)/shard_map/ppermute | solution.py:18
  712.4 37.4 %conditional.15 = (f32[512,16,64]{0,2,1:T(8,128)}, f32[512,16,64]{0,2,1:T(8,128)}, f32[512,16,64]{0,2,1:T(8,128)S(1)}) conditional(s32[]{:T(128)} %bitcast.31, (f32[512,16,64]{0,2,1:T(8,128)S(1)}, f32[512,16,64]{0,2,1:T(8,128)}, f32[512,16,64]{0,2,1:T(8,128)}) %tuple.137, (s32[512]{0:T(512)S(1)}, s32[1,512]{1,0:T(1,128)S(1)}, ...), branch_computations={%region_28.29_spmd, %region_29.30_spmd} | conditional | flops 2754871296 | bytes 170762464 | solution.py:125
  753.4 38.9 %collective-permute-done.6 = bf16[2,1,512,16,64]{2,4,3,1,0:T(8,128)(2,1)S(1)} collective-permute-done((bf16[2,1,512,16,64]{2,4,3,1,0:T(8,128)(2,1)S(1)}, bf16[2,1,512,16,64]{2,4,3,1,0:T(8,128)(2,1)S(1)}, u32[]{:S(2)}, u32[]{:S(2)}) %collective-permute-start.6) | collective-permute-done | bytes 2097184 | tf_op jit(solution)/shard_map/ppermute | solution.py:18
  806.0 15.5 %fusion.120 = f32[4096,1024]{1,0:T(8,128)} fusion(bf16[1,512,1024]{2,1,0:T(8,128)(2,1)S(1)} %copy-done.22, f32[512,4096]{1,0:T(8,128)} %fusion.136, f32[4096]{0:T(1024)S(1)} %bitcast.286), kind=kOutput, calls=%fused_computation.190 | convolution fusion | flops 4315938816 | bytes 26230784 | tf_op jit(solution)/shard_map/dot_general | solution.py:43
  834.7 13.1 fusion.115
  860.5 61.7 %all-reduce.17 = (f32[1024]{0:T(1024)S(1)}, f32[1024]{0:T(1024)S(1)}, f32[1024]{0:T(1024)S(1)}, f32[1024]{0:T(1024)S(1)}, f32[1024]{0:T(1024)S(1)}, /*index=5*/f...) all-reduce(f32[1024]{0:T(1024)S(1)} %reduce_sum.234, ...), channel_id=3, replica_groups=mesh['seq'=4,'dp'=8] {'seq','dp'}, use_global_device_ids=true, to_apply=%region_34.35.clone | all-reduce | flops 12288 | bytes 98304
  927.5 52.2 %reduce-scatter.5.cloned.1.call-done = f32[32,3072]{1,0:T(8,128)} async-done(((f32[1024,3072]{1,0:T(8,128)}), f32[32,3072]{1,0:T(8,128)}) %reduce-scatter.5.cloned.1.call-update) | async-done | bytes 393232 | tf_op jit(solution)/shard_map/reduce_scatter | solution.py:336
  979.7 188.8 %reduce-scatter.11.cloned.1.call-done = f32[128,1024]{1,0:T(8,128)} async-done(((f32[4096,1024]{1,0:T(8,128)}), f32[128,1024]{1,0:T(8,128)}) %reduce-scatter.11.cloned.1.call-update) | async-done | bytes 524304 | tf_op jit(solution)/shard_map/reduce_scatter | solution.py:280
  1168.5 187.3 %reduce-scatter.9.cloned.1.call-done = f32[32,4096]{1,0:T(8,128)} async-done(((f32[1024,4096]{1,0:T(8,128)}), f32[32,4096]{1,0:T(8,128)}) %reduce-scatter.9.cloned.1.call-update) | async-done | bytes 524304 | tf_op jit(solution)/shard_map/reduce_scatter | solution.py:278
  (301 shorter events, 335.8 us)
Async XLA Ops:
  7.2 76.2 %all-gather.6.cloned.1.call-start = ((), (), s32[]{:S(2)}) async-start(), calls=%async_computation.4 | async-start | bytes 6488064 | tf_op jit(solution)/shard_map/all_gather | solution.py:160
  7.9 356.6 %all-gather.8.cloned.1.call-start = ((), (), s32[]{:S(2)}) async-start(), calls=%async_computation.5 | async-start | bytes 2162688 | tf_op jit(solution)/shard_map/all_gather | solution.py:163
  8.7 361.9 %all-gather.10.cloned.1.call-start = ((), (), s32[]{:S(2)}) async-start(), calls=%async_computation.6 | async-start | bytes 8650752 | tf_op jit(solution)/shard_map/all_gather | solution.py:169
  9.4 373.1 %all-gather.12.cloned.1.call-start = ((), (), s32[]{:S(2)}) async-start(), calls=%async_computation.7 | async-start | bytes 8650752 | tf_op jit(solution)/shard_map/all_gather | solution.py:171
  10.0 917.5 %reduce-scatter.7.cloned.1.call-start = ((), (), s32[]{:S(2)}) async-start(), calls=%async_computation.9 | async-start | bytes 4325376 | tf_op jit(solution)/shard_map/reduce_scatter | solution.py:339
  92.1 124.5 %copy-start.53 = (s32[1,4]{1,0:T(1,128)S(1)}, s32[1,4]{1,0:T(1,128)}, u32[]{:S(2)}) copy-start(s32[1,4]{1,0:T(1,128)} %param.34) | copy-start | bytes 52
  92.1 133.5 %copy-start.63 = (bf16[128]{0:T(256)(128)(2,1)S(1)}, bf16[128]{0:T(256)(128)(2,1)}, u32[]{:S(2)}) copy-start(bf16[128]{0:T(256)(128)(2,1)} %param.43) | copy-start | bytes 772
  92.8 173.1 %copy-start.10 = (bf16[512,1024]{0,1:T(8,128)(2,1)}, bf16[512,1024]{0,1:T(8,128)(2,1)S(1)}, u32[]{:S(2)}) copy-start(bf16[512,1024]{0,1:T(8,128)(2,1)S(1)} %copy.68) | copy-start | bytes 3145732
  97.5 168.3 %copy-start.12 = (bf16[512,1024]{0,1:T(8,128)(2,1)}, bf16[512,1024]{0,1:T(8,128)(2,1)S(1)}, u32[]{:S(2)}) copy-start(bf16[512,1024]{0,1:T(8,128)(2,1)S(1)} %copy.69) | copy-start | bytes 3145732
  97.7 54.3 %collective-permute-start = (bf16[2,1,512,16,64]{2,4,3,1,0:T(8,128)(2,1)S(1)}, bf16[2,1,512,16,64]{2,4,3,1,0:T(8,128)(2,1)S(1)}, u32[]{:S(2)}, u32[]{:S(2)}) collective-permute-start(bf16[2,1,512,16,64]{2,4,3,1,0:T(8,128)(2,1)S(1)} %pad_maximum_fusion.1), channel_id=1, source_target_pairs={{0,8},{8,16},{16,24},{24,0},{1,9},{9,17},{17,25},{25,1},{2,10},{10... | collective-permute-start | bytes 6291464 | tf_op jit(solution)/shard_map/ppermute | solution.py:18
  153.4 62.8 %collective-permute-start.1 = (bf16[2,1,512,16,64]{2,4,3,1,0:T(8,128)(2,1)S(1)}, bf16[2,1,512,16,64]{2,4,3,1,0:T(8,128)(2,1)}, u32[]{:S(2)}, u32[]{:S(2)}) collective-permute-start(bf16[2,1,512,16,64]{2,4,3,1,0:T(8,128)(2,1)S(1)} %collective-permute-done), channel_id=1, source_target_pairs={{0,8},{8,16},{16,24},{24,0},{1,9},{9,17},{17,25},{25,1},{2,10},{10... | collective-permute-start | bytes 6291464 | tf_op jit(solution)/shard_map/ppermute | solution.py:18
  216.1 112.8 %collective-permute-start.2 = (bf16[2,1,512,16,64]{2,4,3,1,0:T(8,128)(2,1)}, bf16[2,1,512,16,64]{2,4,3,1,0:T(8,128)(2,1)}, u32[]{:S(2)}, u32[]{:S(2)}) collective-permute-start(bf16[2,1,512,16,64]{2,4,3,1,0:T(8,128)(2,1)} %collective-permute-done.1), channel_id=1, source_target_pairs={{0,8},{8,16},{16,24},{24,0},{1,9},{9,17},{17,25},{25,1},{2,10},{10... | collective-permute-start | bytes 6291464 | tf_op jit(solution)/shard_map/ppermute | solution.py:18
  225.6 193.9 %copy-start.51 = (f32[1024]{0:T(1024)}, f32[1024]{0:T(1024)S(1)}, u32[]{:S(2)}) copy-start(f32[1024]{0:T(1024)S(1)} %convert_element_type.311) | copy-start | bytes 12292
  225.6 145.0 %copy-start.60 = (f32[1024]{0:T(1024)}, f32[1024]{0:T(1024)S(1)}, u32[]{:S(2)}) copy-start(f32[1024]{0:T(1024)S(1)} %convert_element_type.312) | copy-start | bytes 12292
  264.2 118.2 %copy-start.49 = (f32[32,1,128]{2,1,0:T(1,128)}, f32[32,1,128]{2,1,0:T(1,128)S(1)}, u32[]{:S(2)}) copy-start(f32[32,1,128]{2,1,0:T(1,128)S(1)} %convert_element_type.339) | copy-start | bytes 49156
  464.1 44.6 %collective-permute-start.3 = (bf16[2,1,512,16,64]{2,4,3,1,0:T(8,128)(2,1)S(1)}, bf16[2,1,512,16,64]{2,4,3,1,0:T(8,128)(2,1)S(1)}, u32[]{:S(2)}, u32[]{:S(2)}) collective-permute-start(bf16[2,1,512,16,64]{2,4,3,1,0:T(8,128)(2,1)S(1)} %pad_maximum_fusion.2), channel_id=1, source_target_pairs={{0,8},{8,16},{16,24},{24,0},{1,9},{9,17},{17,25},{25,1},{2,10},{10... | collective-permute-start | bytes 6291464 | tf_op jit(solution)/shard_map/ppermute | solution.py:18
  550.3 41.0 %collective-permute-start.4 = (bf16[2,1,512,16,64]{2,4,3,1,0:T(8,128)(2,1)}, bf16[2,1,512,16,64]{2,4,3,1,0:T(8,128)(2,1)}, u32[]{:S(2)}, u32[]{:S(2)}) collective-permute-start(bf16[2,1,512,16,64]{2,4,3,1,0:T(8,128)(2,1)} %pad_maximum_fusion.3), channel_id=1, source_target_pairs={{0,8},{8,16},{16,24},{24,0},{1,9},{9,17},{17,25},{25,1},{2,10},{10... | collective-permute-start | bytes 6291464 | tf_op jit(solution)/shard_map/ppermute | solution.py:18
  555.3 424.4 %reduce-scatter.5.cloned.1.call-start = ((), (), s32[]{:S(2)}) async-start(), calls=%async_computation.8 | async-start | bytes 12976128 | tf_op jit(solution)/shard_map/reduce_scatter | solution.py:336
  600.3 112.1 %copy-start.19 = (bf16[512,1024]{0,1:T(8,128)(2,1)S(1)}, bf16[512,1024]{0,1:T(8,128)(2,1)}, u32[]{:S(2)}) copy-start(bf16[512,1024]{0,1:T(8,128)(2,1)} %copy.72) | copy-start | bytes 3145732
  600.3 112.1 %copy-start.32 = (s32[512]{0:T(512)S(1)}, s32[512]{0:T(512)}, u32[]{:S(2)}) copy-start(s32[512]{0:T(512)} %copy-done.31) | copy-start | bytes 6148
  600.3 108.9 %collective-permute-start.5 = (bf16[2,1,512,16,64]{2,4,3,1,0:T(8,128)(2,1)S(1)}, bf16[2,1,512,16,64]{2,4,3,1,0:T(8,128)(2,1)S(1)}, u32[]{:S(2)}, u32[]{:S(2)}) collective-permute-start(bf16[2,1,512,16,64]{2,4,3,1,0:T(8,128)(2,1)S(1)} %pad_maximum_fusion.4), channel_id=1, source_target_pairs={{0,8},{8,16},{16,24},{24,0},{1,9},{9,17},{17,25},{25,1},{2,10},{10... | collective-permute-start | bytes 6291464 | tf_op jit(solution)/shard_map/ppermute | solution.py:18
  752.7 39.6 %collective-permute-start.6 = (bf16[2,1,512,16,64]{2,4,3,1,0:T(8,128)(2,1)S(1)}, bf16[2,1,512,16,64]{2,4,3,1,0:T(8,128)(2,1)S(1)}, u32[]{:S(2)}, u32[]{:S(2)}) collective-permute-start(bf16[2,1,512,16,64]{2,4,3,1,0:T(8,128)(2,1)S(1)} %pad_maximum_fusion.5), channel_id=1, source_target_pairs={{0,8},{8,16},{16,24},{24,0},{1,9},{9,17},{17,25},{25,1},{2,10},{10... | collective-permute-start | bytes 6291464 | tf_op jit(solution)/shard_map/ppermute | solution.py:18
  804.8 363.7 %reduce-scatter.11.cloned.1.call-start = ((), (), s32[]{:S(2)}) async-start(), calls=%async_computation.11 | async-start | bytes 17301504 | tf_op jit(solution)/shard_map/reduce_scatter | solution.py:280
  821.5 534.3 %reduce-scatter.9.cloned.1.call-start = ((), (), s32[]{:S(2)}) async-start(), calls=%async_computation.10 | async-start | bytes 17301504 | tf_op jit(solution)/shard_map/reduce_scatter | solution.py:278
  (58 other events, 939.2 us)
Sparse Core Ops, SparseCore 0:
  11.0 72.2 all-gather.5
  86.3 59.7 all-gather.7
  149.1 97.9 all-gather.9
  250.0 76.6 all-gather.11
  555.4 171.3 reduce-scatter.6
  804.9 174.7 reduce-scatter.4
  982.7 185.7 reduce-scatter.10
  1171.4 184.3 reduce-scatter.8
where the time goes:
time: 1370 us; the launch traced here: 1360 us
  waiting for transfers between devices  730 us (53%)
  matrix products  260 us (19%)
  blocking collectives  143 us (10%)
  starting transfers between devices  68.5 us (5%)
  other arithmetic  67.5 us (5%)
  local copies, waits for them, and re-layouts  66.4 us (5%)
  between operations  23.6 us (2%)
    ppermute x7, waiting for transfers between devices, passed_along(): lax.ppermute(value, axis, [(i, (i + by) % count) for i in range(count)])  278 us
    reduce_scatter x1, waiting for transfers between devices, body(): lax.psum_scatter(downward_grad, ('seq', 'dp'), scatter_dimension=0, tiled...  189 us
    reduce_scatter x1, waiting for transfers between devices, body(): lax.psum_scatter(upward_grad, ('seq', 'dp'), scatter_dimension=0, tiled=T...  187 us
    unnamed x2, blocking collectives  104 us
    ppermute x7, starting transfers between devices, passed_along(): lax.ppermute(value, axis, [(i, (i + by) % count) for i in range(count)])  68 us
    reduce_scatter x1, waiting for transfers between devices, body(): lax.psum_scatter(joint_grad, ('seq', 'dp'), scatter_dimension=0, tiled=True)  52.2 us
    dot_general x4, matrix products, right_transposed(): lax.dot_general(left, right, (((1,), (1,)), ((), ())), preferred_element_...  47.1 us
    dot_general x4, matrix products, left_transposed(): lax.dot_general(left, right, (((0,), (0,)), ((), ())), preferred_element_...  40.9 us
  transfers between devices with their start and end apart: 15, of which 10 were waited for; matrix products, arithmetic and copies ran while one was open for 19% of the time, Pallas kernels for 0%

commit v1 on v0

v1 whole, which is shorter than its diff:
```python
import math
from functools import partial

import jax
import jax.numpy as jnp
from jax import lax
from jax.experimental import pallas as pl
from jax.experimental.pallas import tpu as pltpu
from jax.sharding import PartitionSpec as P

HEADS = 16
EVERY = ("seq", "dp")
LOG2E = math.log2(math.e)
epsilon = 1e-05
lowest = -1e30
bf16 = jnp.bfloat16
f32 = jnp.float32


def layer_norm(values, scaling, shifting):
    average = jnp.mean(values, -1, keepdims=True)
    centered = values - average
    variance = jnp.mean(centered * centered, -1, keepdims=True)
    return centered * lax.rsqrt(variance + epsilon) * scaling + shifting


def gelu_tanh(values):
    return jax.nn.gelu(values, approximate=True)


def matmul(left, right):
    return jnp.dot(left, right, preferred_element_type=f32)


def left_transposed(left, right):
    return lax.dot_general(left, right, (((0,), (0,)), ((), ())), preferred_element_type=f32)


def right_transposed(left, right):
    return lax.dot_general(left, right, (((1,), (1,)), ((), ())), preferred_element_type=f32)


def sizes():
    return lax.axis_size("seq"), lax.axis_size("dp") // 2


def places():
    dp = lax.axis_index("dp")
    return lax.axis_index("seq"), dp // 2, dp % 2


def to_core(value):
    count = lax.axis_size("dp")
    return lax.ppermute(value, "dp", [(i, i ^ 1) for i in range(count)])


def to_seq(value, by):
    count = lax.axis_size("seq")
    return lax.ppermute(value, "seq", [(i, i ^ by) for i in range(count)])


def to_z(value, by):
    count = lax.axis_size("dp")
    return lax.ppermute(value, "dp", [(i, (i + 2 * by) % count) for i in range(count)])


def put_in_order(pieces):
    count = len(pieces)
    nz, rows, columns = pieces[0].shape
    total = count * nz

    def kernel(place, *refs):
        ins, out, held, in_sem, out_sem = refs[:count], *refs[count:]
        copies = []
        for p in range(count):
            for t in range(nz):
                slot = p * nz + t
                copy = pltpu.make_async_copy(ins[p].at[t], held.at[slot], in_sem.at[slot])
                copy.start()
                copies.append(copy)
        outs = []
        for p in range(count):
            for t in range(nz):
                slot = p * nz + t
                z = lax.rem(place[1] - t + nz, nz)
                owner = ((place[0] ^ (p // 2)) * nz + z) * 2 + (place[2] ^ (p % 2))
                copies[slot].wait()
                copy = pltpu.make_async_copy(held.at[slot], out.at[owner], out_sem.at[slot])
                copy.start()
                outs.append(copy)
        for copy in outs:
            copy.wait()

    size = total * rows * columns * 2
    return pl.pallas_call(
        kernel,
        name="put_in_order",
        out_shape=jax.ShapeDtypeStruct((total, rows, columns), pieces[0].dtype),
        in_specs=[pl.BlockSpec(memory_space=pltpu.SMEM)]
        + [pl.BlockSpec(memory_space=pl.ANY)] * count,
        out_specs=pl.BlockSpec(memory_space=pl.ANY),
        scratch_shapes=[
            pltpu.VMEM((total, rows, columns), pieces[0].dtype),
            pltpu.SemaphoreType.DMA((total,)),
            pltpu.SemaphoreType.DMA((total,)),
        ],
        compiler_params=pltpu.CompilerParams(vmem_limit_bytes=size + (4 << 20)),
        cost_estimate=pl.CostEstimate(flops=0, bytes_accessed=2 * size, transcendentals=0),
    )(jnp.stack(places()).astype(jnp.int32), *pieces).reshape(total * rows, columns)


def gathered(shard):
    ns, nz = sizes()
    column = jnp.stack([shard] + [to_z(shard, by) for by in range(1, nz)])
    planes = [column] + [to_seq(column, by) for by in range(1, ns)]
    pieces = []
    for plane in planes:
        pieces += [plane, to_core(plane)]
    return put_in_order(pieces)


def scattered(grad):
    ns, nz = sizes()
    seq, z, core = places()
    columns = grad.shape[1]
    blocks = grad.reshape(ns, nz, 2, -1, columns)
    mine = lax.dynamic_index_in_dim(blocks, core, 2, keepdims=False)
    other = lax.dynamic_index_in_dim(blocks, 1 - core, 2, keepdims=False)
    chip = (mine.astype(f32) + to_core(other.astype(bf16)).astype(f32)).astype(bf16)
    total = lax.dynamic_index_in_dim(chip, seq, 0, keepdims=False).astype(f32)
    for by in range(1, ns):
        piece = lax.dynamic_index_in_dim(chip, seq ^ by, 0, keepdims=False)
        total = total + to_seq(piece, by).astype(f32)
    plane = total.astype(bf16)
    total = lax.dynamic_index_in_dim(plane, z, 0, keepdims=False).astype(f32)
    for by in range(1, nz):
        piece = lax.dynamic_index_in_dim(plane, (z + by) % nz, 0, keepdims=False)
        total = total + to_z(piece, by).astype(f32)
    return total


def half_lanes(shape, which):
    lane = lax.broadcasted_iota(jnp.int32, shape, len(shape) - 1)
    return (lane < 64) if which == 0 else (lane >= 64)


def with_bias(keys, slope, first_place, which):
    lane = lax.broadcasted_iota(jnp.int32, keys.shape, 1) - (64 if which == 0 else 0)
    row = lax.broadcasted_iota(jnp.int32, keys.shape, 0) + first_place
    bias = row.astype(f32) * (slope * 8.0)
    high = bias.astype(bf16)
    rest = bias - high.astype(f32)
    middle = rest.astype(bf16)
    low = (rest - middle.astype(f32)).astype(bf16)
    zero = jnp.zeros_like(high)
    terms = jnp.where(
        lane == 0, high, jnp.where(lane == 1, middle, jnp.where(lane == 2, low, zero))
    )
    return jnp.where(half_lanes(keys.shape, which), keys, terms)


def attention_forward(qkv, order, slopes):
    ns, _, length, width = qkv.shape
    pairs = width // 128
    scale = LOG2E / 8.0

    def kernel(order_ref, slope_ref, q_ref, kv_ref, low_ref, full_ref, log_ref):
        pair, place = pl.program_id(0), pl.program_id(1)
        shape = (length, 128)
        queries = [
            jnp.where(half_lanes(shape, w), q_ref[0, 0], jnp.ones(shape, bf16)) for w in (0, 1)
        ]

        def step(block, state, diagonal):
            at = order_ref[block]
            result = []
            for w in (0, 1):
                top, acc = state[w]
                keys = with_bias(kv_ref[at, 1], slope_ref[pair * 2 + w], block * length, w)
                scores = right_transposed(keys, queries[w])
                if diagonal:
                    k = lax.broadcasted_iota(jnp.int32, scores.shape, 0)
                    q = lax.broadcasted_iota(jnp.int32, scores.shape, 1)
                    scores = jnp.where(k <= q, scores, lowest)
                new_top = jnp.maximum(top, jnp.max(scores, 0, keepdims=True))
                weights = jnp.exp2(scores * scale - new_top * scale).astype(bf16)
                values = jnp.where(half_lanes(shape, w), kv_ref[at, 2], jnp.ones(shape, bf16))
                acc = acc * jnp.exp2((top - new_top) * scale) + left_transposed(values, weights)
                result.append((new_top, acc))
            return tuple(result)

        start = (jnp.full((1, length), lowest, f32), jnp.zeros((128, length), f32))
        state = lax.fori_loop(
            0, place, lambda block, state: step(block, state, False), (start, start)
        )
        (top0, acc0), (top1, acc1) = step(place, state, True)
        sum0, sum1 = acc0[64:65], acc1[0:1]
        row = lax.broadcasted_iota(jnp.int32, (128, length), 0)
        attended = jnp.where(row < 64, acc0 / sum0, acc1 / sum1).T
        full_ref[0] = attended
        low_ref[0] = attended.astype(bf16)
        row = lax.broadcasted_iota(jnp.int32, (8, length), 0)
        log_ref[0, 0] = jnp.where(
            row == 0, top0 * scale + jnp.log2(sum0), top1 * scale + jnp.log2(sum1)
        )

    per_block = 2 * 2 * length * length * 128 * 2
    grid_spec = pltpu.PrefetchScalarGridSpec(
        num_scalar_prefetch=2,
        grid=(pairs, ns),
        in_specs=[
            pl.BlockSpec((1, 1, length, 128), lambda p, i, order, slope: (order[i], 0, 0, p)),
            pl.BlockSpec((ns, 3, length, 128), lambda p, i, order, slope: (0, 0, 0, p)),
        ],
        out_specs=[
            pl.BlockSpec((1, length, 128), lambda p, i, order, slope: (order[i], 0, p)),
            pl.BlockSpec((1, length, 128), lambda p, i, order, slope: (order[i], 0, p)),
            pl.BlockSpec((1, 1, 8, length), lambda p, i, order, slope: (p, i, 0, 0)),
        ],
    )
    return pl.pallas_call(
        kernel,
        name="attention_forward",
        grid_spec=grid_spec,
        out_shape=[
            jax.ShapeDtypeStruct((ns, length, width), bf16),
            jax.ShapeDtypeStruct((ns, length, width), f32),
            jax.ShapeDtypeStruct((pairs, ns, 8, length), f32),
        ],
        compiler_params=pltpu.CompilerParams(vmem_limit_bytes=40 << 20),
        cost_estimate=pl.CostEstimate(
            flops=pairs * per_block * ns * (ns + 1) // 2 * 4,
            bytes_accessed=qkv.size * 2 + ns * length * width * 6,
            transcendentals=pairs * ns * (ns + 1) * length * length,
        ),
    )(order, slopes, qkv, qkv)


def attention_backward(qkv, grad, full, logs, order, slopes):
    ns, _, length, width = qkv.shape
    pairs = width // 128
    scale = LOG2E / 8.0

    def kernel(
        order_ref, slope_ref, qkv_ref, grad_ref, full_ref, log_ref, out_ref, dq_ref, delta_ref
    ):
        pair, block = pl.program_id(0), pl.program_id(1)
        shape = (length, 128)

        @pl.when(block == 0)
        def _():
            def one(i, _):
                at = order_ref[i]
                product = (grad_ref[at].astype(f32) * full_ref[at]).T
                delta_ref[i] = jnp.concatenate(
                    [
                        jnp.sum(product[:64], 0, keepdims=True),
                        jnp.sum(product[64:], 0, keepdims=True),
                    ],
                    0,
                )
                dq_ref[i] = jnp.zeros((128, length), f32)
                return 0

            lax.fori_loop(0, ns, one, 0)

        here = order_ref[block]
        keys, values = qkv_ref[here, 1], qkv_ref[here, 2]
        zero = jnp.zeros(shape, bf16)
        one = jnp.ones(shape, bf16)
        masks = [half_lanes(shape, w) for w in (0, 1)]
        biased = [
            with_bias(keys, slope_ref[pair * 2 + w], block * length, w) for w in (0, 1)
        ]
        own_keys = [jnp.where(masks[w], keys, zero) for w in (0, 1)]
        own_values = [jnp.where(masks[w], values, zero) for w in (0, 1)]

        def step(i, state, diagonal):
            at = order_ref[i]
            grad_keys, grad_values = state
            queries, grads = qkv_ref[at, 0], grad_ref[at]
            grad_queries = dq_ref[i]
            for w in (0, 1):
                scores = right_transposed(biased[w], jnp.where(masks[w], queries, one))
                weights = jnp.exp2(scores * scale - log_ref[0, i, w : w + 1])
                if diagonal:
                    k = lax.broadcasted_iota(jnp.int32, scores.shape, 0)
                    q = lax.broadcasted_iota(jnp.int32, scores.shape, 1)
                    weights = jnp.where(k <= q, weights, 0.0)
                grad_weights = right_transposed(own_values[w], grads)
                grad_scores = (weights * (grad_weights - delta_ref[i, w : w + 1])).astype(bf16)
                own_grads = jnp.where(masks[w], grads, zero)
                own_queries = jnp.where(masks[w], queries, zero)
                grad_values = grad_values + matmul(weights.astype(bf16), own_grads)
                grad_keys = grad_keys + matmul(grad_scores, own_queries)
                grad_queries = grad_queries + left_transposed(own_keys[w], grad_scores)
            dq_ref[i] = grad_queries
            return grad_keys, grad_values

        start = (jnp.zeros(shape, f32), jnp.zeros(shape, f32))
        state = step(block, start, True)
        grad_keys, grad_values = lax.fori_loop(
            block + 1, ns, lambda i, state: step(i, state, False), state
        )
        out_ref[here, 1] = (grad_keys * 0.125).astype(bf16)
        out_ref[here, 2] = grad_values.astype(bf16)
        out_ref[here, 0] = (dq_ref[block].T * 0.125).astype(bf16)

    per_block = 2 * 5 * length * length * 128 * 2
    grid_spec = pltpu.PrefetchScalarGridSpec(
        num_scalar_prefetch=2,
        grid=(pairs, ns),
        in_specs=[
            pl.BlockSpec((ns, 3, length, 128), lambda p, i, order, slope: (0, 0, 0, p)),
            pl.BlockSpec((ns, length, 128), lambda p, i, order, slope: (0, 0, p)),
            pl.BlockSpec((ns, length, 128), lambda p, i, order, slope: (0, 0, p)),
            pl.BlockSpec((1, ns, 8, length), lambda p, i, order, slope: (p, 0, 0, 0)),
        ],
        out_specs=pl.BlockSpec((ns, 3, length, 128), lambda p, i, order, slope: (0, 0, 0, p)),
        scratch_shapes=[
            pltpu.VMEM((ns, 128, length), f32),
            pltpu.VMEM((ns, 2, length), f32),
        ],
    )
    return pl.pallas_call(
        kernel,
        name="attention_backward",
        grid_spec=grid_spec,
        out_shape=jax.ShapeDtypeStruct((ns, 3, length, width), bf16),
        compiler_params=pltpu.CompilerParams(vmem_limit_bytes=48 << 20),
        cost_estimate=pl.CostEstimate(
            flops=pairs * per_block * ns * (ns + 1) // 2 * 4,
            bytes_accessed=qkv.size * 4 + ns * length * width * 6,
            transcendentals=pairs * ns * (ns + 1) * length * length,
        ),
    )(order, slopes, qkv, grad, full, logs)


def body(
    tokens,
    cotangent,
    block_order,
    joint_weight,
    query_bias,
    value_bias,
    projection,
    offset,
    first_gain,
    first_shift,
    upward_weight,
    upward_bias,
    downward_weight,
    downward_bias,
    second_gain,
    second_shift,
):
    members, length, features = tokens.shape
    ns, nz = sizes()
    seq = lax.axis_index("seq")
    width = features // ns
    group = HEADS // ns
    devices = ns * nz * 2

    small = (
        query_bias,
        value_bias,
        offset,
        first_gain,
        first_shift,
        upward_bias,
        downward_bias,
        second_gain,
        second_shift,
    )
    packed = lax.all_gather(jnp.concatenate(small)[None], EVERY, axis=0, tiled=True)
    smalls, first = [], 0
    for one in small:
        smalls.append(packed[:, first : first + one.shape[0]].reshape(-1).astype(f32))
        first += one.shape[0]
    (
        query_add,
        value_add,
        offset_add,
        gain_one,
        shift_one,
        upward_add,
        downward_add,
        gain_two,
        shift_two,
    ) = smalls

    joint_full = gathered(joint_weight)
    projection_full = gathered(projection)
    upward_full = gathered(upward_weight)
    downward_full = gathered(downward_weight)

    slopes = 2.0 ** (-8.0 * (jnp.arange(HEADS, dtype=f32) + 1.0) / HEADS) * (4.0 / (length * ns))
    slopes = lax.dynamic_slice_in_dim(slopes, seq * group, group)
    order = jnp.argsort(block_order[0]).astype(jnp.int32)

    inputs = tokens.reshape(length, features).astype(f32)
    normed, first_pull = jax.vjp(layer_norm, inputs, gain_one, shift_one)
    normed_low = normed.astype(bf16)
    zeros = jnp.zeros_like(query_add)
    mixture = matmul(normed_low, joint_full) + jnp.concatenate([query_add, zeros, value_add])
    mixture = mixture.astype(bf16).reshape(length, 3, ns, width).transpose(2, 1, 0, 3)
    qkv = lax.all_to_all(mixture, "seq", 0, 0, tiled=True)
    attended, attended_full, logs = attention_forward(qkv, order, slopes)
    attended = lax.all_to_all(attended, "seq", 0, 0, tiled=True)
    attended_low = attended.transpose(1, 0, 2).reshape(length, features)

    middle = inputs + matmul(attended_low, projection_full) + offset_add
    second, second_pull = jax.vjp(layer_norm, middle, gain_two, shift_two)
    second_low = second.astype(bf16)
    hidden = matmul(second_low, upward_full) + upward_add
    active, gelu_pull = jax.vjp(gelu_tanh, hidden)
    active_low = active.astype(bf16)
    result = matmul(active_low, downward_full) + downward_add
    output = (middle + result).astype(bf16).reshape(members, length, features)

    grad_result = cotangent.reshape(length, features)
    grad_result_full = grad_result.astype(f32)
    downward_grad = left_transposed(active_low, grad_result)
    downwardbias_grad = jnp.sum(grad_result_full, 0)
    (grad_hidden,) = gelu_pull(right_transposed(grad_result, downward_full))
    grad_hidden_low = grad_hidden.astype(bf16)
    upward_grad = left_transposed(second_low, grad_hidden_low)
    upwardbias_grad = jnp.sum(grad_hidden_low.astype(f32), 0)
    grad_second = right_transposed(grad_hidden_low, upward_full)
    middle_part, secondgain_grad, secondshift_grad = second_pull(grad_second)
    downward_sum = scattered(downward_grad)
    upward_sum = scattered(upward_grad)

    grad_middle = grad_result_full + middle_part
    grad_branch = grad_middle.astype(bf16)
    projection_sum = scattered(left_transposed(attended_low, grad_branch))
    offset_grad = jnp.sum(grad_branch.astype(f32), 0)
    grad_attended = right_transposed(grad_branch, projection_full).astype(bf16)
    grad_attended = grad_attended.reshape(length, ns, width).transpose(1, 0, 2)
    grad_attended = lax.all_to_all(grad_attended, "seq", 0, 0, tiled=True)
    grad_qkv = attention_backward(qkv, grad_attended, attended_full, logs, order, slopes)
    grad_qkv = lax.all_to_all(grad_qkv, "seq", 0, 0, tiled=True)
    grad_mixture = grad_qkv.transpose(2, 1, 0, 3).reshape(length, 3 * features)
    joint_sum = scattered(left_transposed(normed_low, grad_mixture))
    mixture_sums = jnp.sum(grad_mixture.astype(f32), 0)
    grad_normed = right_transposed(grad_mixture, joint_full)
    input_part, firstgain_grad, firstshift_grad = first_pull(grad_normed)
    input_grad = (grad_middle + input_part).astype(bf16).reshape(members, length, features)

    grads = (
        mixture_sums[:features],
        mixture_sums[2 * features :],
        offset_grad,
        firstgain_grad,
        firstshift_grad,
        upwardbias_grad,
        downwardbias_grad,
        secondgain_grad,
        secondshift_grad,
    )
    packed = jnp.concatenate([g.reshape(devices, -1) for g in grads], 1)
    packed = lax.psum_scatter(packed, EVERY, scatter_dimension=0, tiled=True)[0]
    sums, first = [], 0
    for one in small:
        sums.append(packed[first : first + one.shape[0]])
        first += one.shape[0]
    return (
        output,
        input_grad,
        joint_sum,
        sums[0],
        sums[1],
        projection_sum,
        sums[2],
        sums[3],
        sums[4],
        upward_sum,
        sums[5],
        downward_sum,
        sums[6],
        sums[7],
        sums[8],
    )


def solution(mesh):
    tokens = P("dp", "seq", None)
    matrix = P(EVERY, None)
    vector = P(EVERY)
    kinds = (tokens, tokens, P("dp", None), matrix, vector, vector, matrix, vector, vector, vector)
    kinds += (matrix, vector, matrix, vector, vector, vector)
    in_specs = kinds
    out_specs = kinds[:2] + kinds[3:]
    return jax.shard_map(body, mesh=mesh, in_specs=in_specs, out_specs=out_specs, check_vma=False)
```

time: 1370 us -> 786 us (0.57)
  waiting for transfers between devices: 730 us -> 252 us
  matrix products: 260 us -> 93.5 us
  Pallas kernels: 0 us -> 91.7 us
  local copies, waits for them, and re-layouts: 66.4 us -> 92.3 us
  other arithmetic: 67.5 us -> 45 us
  between operations: 23.6 us -> 2.2 us
  blocking collectives: 143 us -> 122 us
    reduce_scatter x4 -> x0, waiting for transfers between devices: 428 us -> none  [the longest x1 189 us: body(): lax.psum_scatter(downward_grad, ('seq', 'dp'), scatter_dimension=0, tiled...]
    dot_general x25 -> x4, matrix products: 172 us -> 27 us  [matmul(): return jnp.dot(left, right, preferred_element_type=f32)]
    pallas_call x0 -> x6, Pallas kernels: none -> 91.7 us  [the longest x1 36.5 us: attention_backward(): pl.pallas_call(kernel, name='attention_backward', grid_spec=grid_spec, ou...]
    reduce_sum x6 -> x2, other arithmetic: 28.6 us -> 1.41 us  [the longest x1 0.98 us: body(): offset_grad = jnp.sum(grad_branch.astype(f32), 0)]
    ppermute x7 -> x68, waiting for transfers between devices: 278 us -> 252 us  [the longest x24 202 us: to_seq(): return lax.ppermute(value, 'seq', [(i, i ^ by) for i in range(count)])]
    unnamed x2 -> x1, blocking collectives: 104 us -> 79.4 us
    convert_element_type x3 -> x14, local copies, waits for them, and re-layouts: 4.33 us -> 25.6 us  [the longest x4 15.3 us: scattered(): other.astype(bf16)]
    all_gather x4 -> x0, waiting for transfers between devices: 20.5 us -> none  [the longest x1 20.4 us: body(): lax.all_gather(joint_weight, ('seq', 'dp'), axis=0, tiled=True)]
  transfers between devices with their start and end apart: 15 -> 72, of which waited for: 10 -> 21; matrix products, arithmetic and copies ran while one was open for 19% -> 18% of each run, Pallas kernels for 0% -> 12%
where the time goes in v1:
time: 786 us; the launch traced here: 777 us
  waiting for transfers between devices  252 us (32%)
  blocking collectives  122 us (16%)
  matrix products  93.5 us (12%)
  local copies, waits for them, and re-layouts  92.3 us (12%)
  Pallas kernels  91.7 us (12%)
  starting transfers between devices  77.5 us (10%)
  other arithmetic  45 us (6%)
    ppermute x24, waiting for transfers between devices, to_seq(): return lax.ppermute(value, 'seq', [(i, i ^ by) for i in range(count)])  202 us
    unnamed x1, blocking collectives  79.4 us
    ppermute x24, waiting for transfers between devices, to_z(): lax.ppermute(value, 'dp', [(i, (i + 2 * by) % count) for i in range(count)])  46.7 us
    all_gather x1, blocking collectives, body(): lax.all_gather(jnp.concatenate(small)[None], EVERY, axis=0, tiled=True)  42.9 us
    pallas_call x1, Pallas kernels, attention_backward(): pl.pallas_call(kernel, name='attention_backward', grid_spec=grid_spec, ou...  36.5 us
    unnamed x140, local copies, waits for them, and re-layouts  36.1 us
    dot_general x4, matrix products, left_transposed(): lax.dot_general(left, right, (((0,), (0,)), ((), ())), preferred_element_...  33.4 us
    dot_general x4, matrix products, right_transposed(): lax.dot_general(left, right, (((1,), (1,)), ((), ())), preferred_element_...  33.1 us
  transfers between devices with their start and end apart: 72, of which 21 were waited for; matrix products, arithmetic and copies ran while one was open for 18% of the time, Pallas kernels for 12%

profile of v1, /device:TPU:0, one launch (start us, length us, event | category | flops | bytes accessed | tf_op | source)
XLA Modules:
  0.0 776.9 jit_solution(16546242025904947712)
XLA Ops:
  11.4 11.2 %collective-permute-done.1 = bf16[32,3072]{1,0:T(8,128)(2,1)S(1)} collective-permute-done((bf16[32,3072]{1,0:T(8,128)(2,1)}, bf16[32,3072]{1,0:T(8,128)(2,1)S(1)}, u32[]{:S(2)}, u32[]{:S(2)}) %collective-permute-start.1) | collective-permute-done | bytes 196640 | tf_op jit(solution)/shard_map/ppermute | solution.py:64
  33.7 42.9 %all-gather.1 = bf16[32,1,384]{2,1,0:T(2,128)(2,1)S(1)} all-gather(bf16[1,1,384]{2,1,0:T(2,128)(2,1)S(1)} %reshape.326), channel_id=2, replica_groups=mesh['seq'=4,'dp'=8] {'seq','dp'}, dimensions={0}, use_global_device_ids=true | all-gather | bytes 25344 | tf_op jit(solution)/shard_map/all_gather | solution.py:375
  99.5 13.6 %put_in_order.4 = bf16[32,32,3072]{2,1,0:T(8,128)(2,1)S(1)} custom-call(s32[3]{0:T(128)S(1)} %pad_add_fusion.place, bf16[4,32,3072]{2,1,0:T(8,128)(2,1)S(1)} %pad_maximum_fusion.2.refs_0_, bf16[4,32,3072]{2,1,0:T(8,128)(2,1)} %collective-permute-done.3.refs_1_, bf16[4,32,3072]{2,1,0:T(8,128)(2,1)S(1)} %collective-permute-done.4.refs_2_, ...), custom_call_target="tpu_custom_call" | custom-call | bytes 12582912 | tf_op jit(solution)/shard_map/put_in_order/pallas_call | solution.py:95
  144.9 33.6 %collective-permute-done.18.refs_6_ = bf16[4,32,1024]{2,1,0:T(8,128)(2,1)S(1)} collective-permute-done((bf16[4,32,1024]{2,1,0:T(8,128)(2,1)S(1)}, bf16[4,32,1024]{2,1,0:T(8,128)(2,1)S(1)}, u32[]{:S(2)}, u32[]{:S(2)}) %collective-permute-start.18) | collective-permute-done | bytes 262176 | tf_op jit(solution)/shard_map/ppermute | solution.py:59
  188.0 12.0 %collective-permute-done.34.refs_2_ = bf16[4,128,1024]{2,1,0:T(8,128)(2,1)S(1)} collective-permute-done((bf16[4,128,1024]{2,1,0:T(8,128)(2,1)S(1)}, bf16[4,128,1024]{2,1,0:T(8,128)(2,1)S(1)}, u32[]{:S(2)}, u32[]{:S(2)}) %collective-permute-start.34) | collective-permute-done | bytes 1048608 | tf_op jit(solution)/shard_map/ppermute | solution.py:59
  201.4 22.1 %collective-permute-done.38.refs_6_ = bf16[4,128,1024]{2,1,0:T(8,128)(2,1)S(1)} collective-permute-done((bf16[4,128,1024]{2,1,0:T(8,128)(2,1)S(1)}, bf16[4,128,1024]{2,1,0:T(8,128)(2,1)S(1)}, u32[]{:S(2)}, u32[]{:S(2)}) %collective-permute-start.38) | collective-permute-done | bytes 1048608 | tf_op jit(solution)/shard_map/ppermute | solution.py:59
  225.3 19.7 %collective-permute-done.24.refs_2_ = bf16[4,32,4096]{2,1,0:T(8,128)(2,1)} collective-permute-done((bf16[4,32,4096]{2,1,0:T(8,128)(2,1)}, bf16[4,32,4096]{2,1,0:T(8,128)(2,1)}, u32[]{:S(2)}, u32[]{:S(2)}) %collective-permute-start.24) | collective-permute-done | bytes 1048608 | tf_op jit(solution)/shard_map/ppermute | solution.py:59
  245.6 22.2 %collective-permute-done.28.refs_6_ = bf16[4,32,4096]{2,1,0:T(8,128)(2,1)} collective-permute-done((bf16[4,32,4096]{2,1,0:T(8,128)(2,1)}, bf16[4,32,4096]{2,1,0:T(8,128)(2,1)}, u32[]{:S(2)}, u32[]{:S(2)}) %collective-permute-start.28) | collective-permute-done | bytes 1048608 | tf_op jit(solution)/shard_map/ppermute | solution.py:59
  268.3 27.6 %attention_forward.1 = (bf16[4,512,256]{2,1,0:T(8,128)(2,1)S(1)}, f32[4,512,256]{2,1,0:T(8,128)S(1)}, f32[2,4,8,512]{3,2,1,0:T(8,128)S(1)}) custom-call(s32[4]{0:T(128)S(1)} %get-tuple-element.19.order_ref, f32[4]{0:T(128)S(1)} %dynamic_slice.135.slope_ref, bf16[4,3,512,256]{3,2,1,0:T(8,128)(2,1)} %all-to-all-done.q_ref.kv_ref.qkv_ref, ...), custom_call_target="tpu_custom_call" | custom-call | flops 21474836480 | bytes 6291456 | tf_op jit(solution)/shard_map/attention_forward/pallas_call | solution.py:221
  342.8 9.9 %fusion.14 = (bf16[4096,512]{0,1:T(8,128)(2,1)}, f32[512,4096]{1,0:T(8,128)}) fusion(f32[4096]{0:T(1024)S(1)} %copy-done.60, bf16[1024,4096]{1,0:T(8,128)(2,1)S(1)} %bitcast.274, f32[512,1024]{1,0:T(8,128)S(1)} %get-tuple-element.80, f32[1024]{0:T(1024)S(1)} %copy-done.62, f32[1024]{0:T(1024)S(1)} %copy-done.61, f32[512]{0:T(512)S(1)} %fusion.85, ...), kind=kOutput, calls=%fused_computation.17 | convolution fusion | flops 4318560256 | bytes 23097344 | tf_op jit(solution)/shard_map/dot_general | solution.py:32
  352.8 10.1 %fusion.53 = bf16[1,512,1024]{2,1,0:T(8,128)(2,1)} fusion(f32[512,1024]{1,0:T(8,128)S(1)} %get-tuple-element.80, bf16[4096,1024]{1,0:T(8,128)(2,1)S(1)} %bitcast.272, f32[512,4096]{1,0:T(8,128)} %get-tuple-element.86, f32[4096]{0:T(1024)S(1)} %copy-done.60, f32[1024]{0:T(1024)S(1)} %copy-done.63), kind=kOutput, calls=%fused_computation.88 | convolution fusion | flops 4317511680 | bytes 19943424 | tf_op jit(solution)/shard_map/dot_general | solution.py:32
  362.9 14.2 %convert_reduce_fusion = (f32[4096]{0:T(1024)}, bf16[512,4096]{1,0:T(8,128)(2,1)}) fusion(f32[512,4096]{1,0:T(8,128)} %get-tuple-element.86, f32[4096]{0:T(1024)S(1)} %copy-done.60, bf16[4096,1024]{1,0:T(8,128)(2,1)S(1)} %bitcast.273, bf16[1,512,1024]{2,1,0:T(8,128)(2,1)S(1)} %copy-done.41), kind=kOutput, calls=%fused_computation.29 | convolution fusion | flops 4343197696 | bytes 22052864 | tf_op jit(solution)/shard_map/dot_general | solution.py:40
  377.2 8.8 %multiply_reduce_fusion = (f32[1024]{0:T(1024)}, f32[512]{0:T(512)S(1)}, f32[1024]{0:T(1024)}, f32[512,1024]{1,0:T(8,128)S(1)}) fusion(f32[512,1024]{1,0:T(8,128)} %copy-done.28, f32[512]{0:T(512)S(1)} %fusion.85, f32[512]{0:T(512)S(1)} %broadcast_multiply_fusion, f32[1024]{0:T(1024)S(1)} %copy-done.61, bf16[512,4096]{1,0:T(8,128)(2,1)} %get-tuple-element.84, ...), kind=kOutput, calls=%fused_computation.76 | convolution fusion | flops 4299159040 | bytes 16795648 | tf_op jit(solution)/shard_map/dot_general | solution.py:40
  410.3 13.5 %fusion.91 = f32[1024,4096]{1,0:T(8,128)} fusion(bf16[512,4096]{1,0:T(8,128)(2,1)} %get-tuple-element.84, f32[512,1024]{1,0:T(8,128)} %copy-done.28, f32[1024]{0:T(1024)S(1)} %copy-done.62, f32[1024]{0:T(1024)S(1)} %copy-done.61, f32[512]{0:T(512)S(1)} %fusion.85, f32[512]{0:T(512)S(1)} %broadcast_multiply_fusion), kind=kOutput, calls=%fused_computation.188 | convolution fusion | flops 4297588736 | bytes 23080960 | tf_op jit(solution)/shard_map/dot_general | solution.py:36
  423.8 36.5 %attention_backward.1 = bf16[4,3,512,256]{3,2,1,0:T(8,128)(2,1)} custom-call(s32[4]{0:T(128)S(1)} %get-tuple-element.19.order_ref, f32[4]{0:T(128)S(1)} %dynamic_slice.135.slope_ref, bf16[4,3,512,256]{3,2,1,0:T(8,128)(2,1)} %all-to-all-done.q_ref.kv_ref.qkv_ref, bf16[4,512,256]{2,1,0:T(8,128)(2,1)S(1)} %all-to-all-done.2.grad_ref, ...), custom_call_target="tpu_custom_call" | custom-call | flops 53687091200 | bytes 9437184 | tf_op jit(solution)/shard_map/attention_backward/pallas_call | solution.py:325
  464.7 13.0 %fusion.60 = f32[4,4,2,128,1024]{4,3,2,1,0:T(8,128)} fusion(bf16[4,4,2,128,512]{4,3,2,1,0:T(8,128)(2,1)} %bitcast.287, bf16[1,512,1024]{2,1,0:T(8,128)(2,1)} %param.17), kind=kOutput, calls=%fused_computation.96 | convolution fusion | flops 4294967296 | bytes 22020096 | tf_op jit(solution)/shard_map/dot_general | solution.py:36
  491.0 17.8 %collective-permute-done.50 = bf16[4,32,1024]{2,1,0:T(8,128)(2,1)S(1)} collective-permute-done((bf16[4,32,1024]{2,1,0:T(8,128)(2,1)}, bf16[4,32,1024]{2,1,0:T(8,128)(2,1)S(1)}, u32[]{:S(2)}, u32[]{:S(2)}) %collective-permute-start.50) | collective-permute-done | bytes 262176 | tf_op jit(solution)/shard_map/ppermute | solution.py:59
  532.4 7.8 %fusion.93 = (f32[1024]{0:T(1024)S(1)}, f32[512]{0:T(512)S(1)}, f32[512,1024]{1,0:T(8,128)S(1)}) fusion(f32[1024]{0:T(1024)S(1)} %copy-done.49, f32[512]{0:T(512)S(1)} %copy-done.51, bf16[1,512,1024]{2,1,0:T(8,128)(2,1)} %param.16, bf16[512,3072]{0,1:T(8,128)(2,1)} %bitcast.289, bf16[1024,3072]{1,0:T(8,128)(2,1)} %bitcast.279), kind=kOutput, calls=%fused_computation.190 | convolution fusion | flops 3224369664 | bytes 12595200 | tf_op jit(solution)/shard_map/dot_general | solution.py:40
  573.1 79.4 %all-reduce = f32[32,384]{1,0:T(8,128)S(1)} all-reduce(f32[32,384]{1,0:T(8,128)S(1)} %concatenate.11), channel_id=3, replica_groups=mesh['seq'=4,'dp'=8] {'seq','dp'}, use_global_device_ids=true, to_apply=%region_17.18.clone | all-reduce | flops 12288 | bytes 98304
  668.8 18.7 %collective-permute-done.64 = bf16[4,128,1024]{2,1,0:T(8,128)(2,1)S(1)} collective-permute-done((bf16[4,128,1024]{2,1,0:T(8,128)(2,1)S(1)}, bf16[4,128,1024]{2,1,0:T(8,128)(2,1)S(1)}, u32[]{:S(2)}, u32[]{:S(2)}) %collective-permute-start.64) | collective-permute-done | bytes 1048608 | tf_op jit(solution)/shard_map/ppermute | solution.py:59
  687.5 20.4 %collective-permute-done.63 = bf16[4,128,1024]{2,1,0:T(8,128)(2,1)S(1)} collective-permute-done((bf16[4,128,1024]{2,1,0:T(8,128)(2,1)S(1)}, bf16[4,128,1024]{2,1,0:T(8,128)(2,1)S(1)}, u32[]{:S(2)}, u32[]{:S(2)}) %collective-permute-start.63) | collective-permute-done | bytes 1048608 | tf_op jit(solution)/shard_map/ppermute | solution.py:59
  722.3 17.0 %collective-permute-done.43 = bf16[4,32,3072]{2,1,0:T(8,128)(2,1)S(1)} collective-permute-done((bf16[4,32,3072]{2,1,0:T(8,128)(2,1)S(1)}, bf16[4,32,3072]{2,1,0:T(8,128)(2,1)S(1)}, u32[]{:S(2)}, u32[]{:S(2)}) %collective-permute-start.43) | collective-permute-done | bytes 786464 | tf_op jit(solution)/shard_map/ppermute | solution.py:59
  740.0 14.6 %collective-permute-done.42 = bf16[4,32,3072]{2,1,0:T(8,128)(2,1)S(1)} collective-permute-done((bf16[4,32,3072]{2,1,0:T(8,128)(2,1)S(1)}, bf16[4,32,3072]{2,1,0:T(8,128)(2,1)S(1)}, u32[]{:S(2)}, u32[]{:S(2)}) %collective-permute-start.42) | collective-permute-done | bytes 786464 | tf_op jit(solution)/shard_map/ppermute | solution.py:59
  762.0 13.5 %collective-permute-done.45 = bf16[32,3072]{1,0:T(8,128)(2,1)S(1)} collective-permute-done((bf16[32,3072]{1,0:T(8,128)(2,1)S(1)}, bf16[32,3072]{1,0:T(8,128)(2,1)S(1)}, u32[]{:S(2)}, u32[]{:S(2)}) %collective-permute-start.45) | collective-permute-done | bytes 196640 | tf_op jit(solution)/shard_map/ppermute | solution.py:64
  (363 shorter events, 274.6 us)
Async XLA Ops:
  23.7 56.4 %collective-permute-start.4 = (bf16[4,32,3072]{2,1,0:T(8,128)(2,1)S(1)}, bf16[4,32,3072]{2,1,0:T(8,128)(2,1)S(1)}, u32[]{:S(2)}, u32[]{:S(2)}) collective-permute-start(bf16[4,32,3072]{2,1,0:T(8,128)(2,1)S(1)} %pad_maximum_fusion.2.refs_0_), channel_id=1, source_target_pairs={{0,8},{8,0},{16,24},{24,16},{1,9},{9,1},{17,25},{25,17},{2,10},{10... | collective-permute-start | bytes 2359304 | tf_op jit(solution)/shard_map/ppermute | solution.py:59
  25.3 55.0 %collective-permute-start.6 = (bf16[4,32,3072]{2,1,0:T(8,128)(2,1)S(1)}, bf16[4,32,3072]{2,1,0:T(8,128)(2,1)S(1)}, u32[]{:S(2)}, u32[]{:S(2)}) collective-permute-start(bf16[4,32,3072]{2,1,0:T(8,128)(2,1)S(1)} %pad_maximum_fusion.2.refs_0_), channel_id=1, source_target_pairs={{0,16},{8,24},{16,0},{24,8},{1,17},{9,25},{17,1},{25,9},{2,18},{10... | collective-permute-start | bytes 2359304 | tf_op jit(solution)/shard_map/ppermute | solution.py:59
  27.2 55.2 %collective-permute-start.12 = (bf16[32,1024]{1,0:T(8,128)(2,1)}, bf16[32,1024]{1,0:T(8,128)(2,1)S(1)}, u32[]{:S(2)}, u32[]{:S(2)}) collective-permute-start(bf16[32,1024]{1,0:T(8,128)(2,1)} %param.22), channel_id=1, source_target_pairs={{0,6},{1,7},{2,0},{3,1},{4,2},{5,3},{6,4},{7,5},{8,14},{9,15},{10,... | collective-permute-start | bytes 196616 | tf_op jit(solution)/shard_map/ppermute | solution.py:64
  129.7 138.6 %all-to-all-start = ((bf16[4,3,512,256]{3,2,1,0:T(8,128)(2,1)}), bf16[4,3,512,256]{3,2,1,0:T(8,128)(2,1)}, u32[]{:S(2)}, u32[]{:S(2)}) async-start(bf16[4,3,512,256]{3,2,1,0:T(8,128)(2,1)} %bitcast.281), calls=%async_computation | async-start | bytes 6291456 | tf_op jit(solution)/shard_map/all_to_all | solution.py:407
  141.4 58.6 %collective-permute-start.34 = (bf16[4,128,1024]{2,1,0:T(8,128)(2,1)S(1)}, bf16[4,128,1024]{2,1,0:T(8,128)(2,1)S(1)}, u32[]{:S(2)}, u32[]{:S(2)}) collective-permute-start(bf16[4,128,1024]{2,1,0:T(8,128)(2,1)S(1)} %pad_maximum_fusion.1.refs_0_), channel_id=1, source_target_pairs={{0,8},{8,0},{16,24},{24,16},{1,9},{9,1},{17,25},{25,17},{2,10},{10... | collective-permute-start | bytes 3145736 | tf_op jit(solution)/shard_map/ppermute | solution.py:59
  143.3 58.1 %collective-permute-start.36 = (bf16[4,128,1024]{2,1,0:T(8,128)(2,1)S(1)}, bf16[4,128,1024]{2,1,0:T(8,128)(2,1)S(1)}, u32[]{:S(2)}, u32[]{:S(2)}) collective-permute-start(bf16[4,128,1024]{2,1,0:T(8,128)(2,1)S(1)} %pad_maximum_fusion.1.refs_0_), channel_id=1, source_target_pairs={{0,16},{8,24},{16,0},{24,8},{1,17},{9,25},{17,1},{25,9},{2,18},{10... | collective-permute-start | bytes 3145736 | tf_op jit(solution)/shard_map/ppermute | solution.py:59
  144.9 78.6 %collective-permute-start.38 = (bf16[4,128,1024]{2,1,0:T(8,128)(2,1)S(1)}, bf16[4,128,1024]{2,1,0:T(8,128)(2,1)S(1)}, u32[]{:S(2)}, u32[]{:S(2)}) collective-permute-start(bf16[4,128,1024]{2,1,0:T(8,128)(2,1)S(1)} %pad_maximum_fusion.1.refs_0_), channel_id=1, source_target_pairs={{0,24},{8,16},{16,8},{24,0},{1,25},{9,17},{17,9},{25,1},{2,26},{10... | collective-permute-start | bytes 3145736 | tf_op jit(solution)/shard_map/ppermute | solution.py:59
  186.5 58.6 %collective-permute-start.24 = (bf16[4,32,4096]{2,1,0:T(8,128)(2,1)}, bf16[4,32,4096]{2,1,0:T(8,128)(2,1)}, u32[]{:S(2)}, u32[]{:S(2)}) collective-permute-start(bf16[4,32,4096]{2,1,0:T(8,128)(2,1)} %pad_maximum_fusion.refs_0_), channel_id=1, source_target_pairs={{0,8},{8,0},{16,24},{24,16},{1,9},{9,1},{17,25},{25,17},{2,10},{10... | collective-permute-start | bytes 3145736 | tf_op jit(solution)/shard_map/ppermute | solution.py:59
  188.0 57.1 %collective-permute-start.26 = (bf16[4,32,4096]{2,1,0:T(8,128)(2,1)}, bf16[4,32,4096]{2,1,0:T(8,128)(2,1)}, u32[]{:S(2)}, u32[]{:S(2)}) collective-permute-start(bf16[4,32,4096]{2,1,0:T(8,128)(2,1)} %pad_maximum_fusion.refs_0_), channel_id=1, source_target_pairs={{0,16},{8,24},{16,0},{24,8},{1,17},{9,25},{17,1},{25,9},{2,18},{10... | collective-permute-start | bytes 3145736 | tf_op jit(solution)/shard_map/ppermute | solution.py:59
  200.0 67.8 %collective-permute-start.28 = (bf16[4,32,4096]{2,1,0:T(8,128)(2,1)}, bf16[4,32,4096]{2,1,0:T(8,128)(2,1)}, u32[]{:S(2)}, u32[]{:S(2)}) collective-permute-start(bf16[4,32,4096]{2,1,0:T(8,128)(2,1)} %pad_maximum_fusion.refs_0_), channel_id=1, source_target_pairs={{0,24},{8,16},{16,8},{24,0},{1,25},{9,17},{17,9},{25,1},{2,26},{10... | collective-permute-start | bytes 3145736 | tf_op jit(solution)/shard_map/ppermute | solution.py:59
  201.4 66.3 %collective-permute-start.35 = (bf16[4,128,1024]{2,1,0:T(8,128)(2,1)S(1)}, bf16[4,128,1024]{2,1,0:T(8,128)(2,1)}, u32[]{:S(2)}, u32[]{:S(2)}) collective-permute-start(bf16[4,128,1024]{2,1,0:T(8,128)(2,1)S(1)} %collective-permute-done.34.refs_2_), channel_id=1, source_target_pairs={{0,1},{1,0},{2,3},{3,2},{4,5},{5,4},{6,7},{7,6},{8,9},{9,8},{10,11... | collective-permute-start | bytes 3145736 | tf_op jit(solution)/shard_map/ppermute | solution.py:54
  245.1 84.2 %collective-permute-start.23 = (bf16[4,32,4096]{2,1,0:T(8,128)(2,1)}, bf16[4,32,4096]{2,1,0:T(8,128)(2,1)}, u32[]{:S(2)}, u32[]{:S(2)}) collective-permute-start(bf16[4,32,4096]{2,1,0:T(8,128)(2,1)} %pad_maximum_fusion.refs_0_), channel_id=1, source_target_pairs={{0,1},{1,0},{2,3},{3,2},{4,5},{5,4},{6,7},{7,6},{8,9},{9,8},{10,11... | collective-permute-start | bytes 3145736 | tf_op jit(solution)/shard_map/ppermute | solution.py:54
  245.1 75.1 %collective-permute-start.39 = (bf16[4,128,1024]{2,1,0:T(8,128)(2,1)}, bf16[4,128,1024]{2,1,0:T(8,128)(2,1)}, u32[]{:S(2)}, u32[]{:S(2)}) collective-permute-start(bf16[4,128,1024]{2,1,0:T(8,128)(2,1)} %copy-done.10), channel_id=1, source_target_pairs={{0,1},{1,0},{2,3},{3,2},{4,5},{5,4},{6,7},{7,6},{8,9},{9,8},{10,11... | collective-permute-start | bytes 3145736 | tf_op jit(solution)/shard_map/ppermute | solution.py:54
  267.8 61.5 %collective-permute-start.25 = (bf16[4,32,4096]{2,1,0:T(8,128)(2,1)}, bf16[4,32,4096]{2,1,0:T(8,128)(2,1)}, u32[]{:S(2)}, u32[]{:S(2)}) collective-permute-start(bf16[4,32,4096]{2,1,0:T(8,128)(2,1)} %collective-permute-done.24.refs_2_), channel_id=1, source_target_pairs={{0,1},{1,0},{2,3},{3,2},{4,5},{5,4},{6,7},{7,6},{8,9},{9,8},{10,11... | collective-permute-start | bytes 3145736 | tf_op jit(solution)/shard_map/ppermute | solution.py:54
  267.8 61.5 %collective-permute-start.27 = (bf16[4,32,4096]{2,1,0:T(8,128)(2,1)}, bf16[4,32,4096]{2,1,0:T(8,128)(2,1)}, u32[]{:S(2)}, u32[]{:S(2)}) collective-permute-start(bf16[4,32,4096]{2,1,0:T(8,128)(2,1)} %collective-permute-done.26.refs_4_), channel_id=1, source_target_pairs={{0,1},{1,0},{2,3},{3,2},{4,5},{5,4},{6,7},{7,6},{8,9},{9,8},{10,11... | collective-permute-start | bytes 3145736 | tf_op jit(solution)/shard_map/ppermute | solution.py:54
  268.3 61.0 %collective-permute-start.29 = (bf16[4,32,4096]{2,1,0:T(8,128)(2,1)}, bf16[4,32,4096]{2,1,0:T(8,128)(2,1)}, u32[]{:S(2)}, u32[]{:S(2)}) collective-permute-start(bf16[4,32,4096]{2,1,0:T(8,128)(2,1)} %collective-permute-done.28.refs_6_), channel_id=1, source_target_pairs={{0,1},{1,0},{2,3},{3,2},{4,5},{5,4},{6,7},{7,6},{8,9},{9,8},{10,11... | collective-permute-start | bytes 3145736 | tf_op jit(solution)/shard_map/ppermute | solution.py:54
  403.9 73.8 %collective-permute-start.47 = (bf16[4,4,32,1024]{3,2,1,0:T(8,128)(2,1)}, bf16[4,4,32,1024]{3,2,1,0:T(8,128)(2,1)}, u32[]{:S(2)}, u32[]{:S(2)}) collective-permute-start(bf16[4,4,32,1024]{3,2,1,0:T(8,128)(2,1)} %fusion.56), channel_id=1, source_target_pairs={{0,1},{1,0},{2,3},{3,2},{4,5},{5,4},{6,7},{7,6},{8,9},{9,8},{10,11... | collective-permute-start | bytes 3145736 | tf_op jit(solution)/shard_map/ppermute | solution.py:54
  460.3 69.0 %all-to-all-start.3 = ((bf16[4,3,512,256]{3,2,1,0:T(8,128)(2,1)}), bf16[4,3,512,256]{3,2,1,0:T(8,128)(2,1)S(1)}, u32[]{:S(2)}, u32[]{:S(2)}) async-start(bf16[4,3,512,256]{3,2,1,0:T(8,128)(2,1)} %attention_backward.1), calls=%async_computation.3 | async-start | bytes 6291456 | tf_op jit(solution)/shard_map/all_to_all | solution.py:442
  490.9 68.8 %collective-permute-start.54 = (bf16[4,4,32,4096]{3,2,1,0:T(8,128)(2,1)}, bf16[4,4,32,4096]{3,2,1,0:T(8,128)(2,1)}, u32[]{:S(2)}, u32[]{:S(2)}) collective-permute-start(bf16[4,4,32,4096]{3,2,1,0:T(8,128)(2,1)} %fusion.22), channel_id=1, source_target_pairs={{0,1},{1,0},{2,3},{3,2},{4,5},{5,4},{6,7},{7,6},{8,9},{9,8},{10,11... | collective-permute-start | bytes 12582920 | tf_op jit(solution)/shard_map/ppermute | solution.py:54
  528.6 125.2 %collective-permute-start.61 = (bf16[4,4,128,1024]{3,2,1,0:T(8,128)(2,1)}, bf16[4,4,128,1024]{3,2,1,0:T(8,128)(2,1)}, u32[]{:S(2)}, u32[]{:S(2)}) collective-permute-start(bf16[4,4,128,1024]{3,2,1,0:T(8,128)(2,1)} %fusion.21), channel_id=1, source_target_pairs={{0,1},{1,0},{2,3},{3,2},{4,5},{5,4},{6,7},{7,6},{8,9},{9,8},{10,11... | collective-permute-start | bytes 12582920 | tf_op jit(solution)/shard_map/ppermute | solution.py:54
  552.6 160.3 %collective-permute-start.40 = (bf16[4,4,32,3072]{3,2,1,0:T(8,128)(2,1)}, bf16[4,4,32,3072]{3,2,1,0:T(8,128)(2,1)}, u32[]{:S(2)}, u32[]{:S(2)}) collective-permute-start(bf16[4,4,32,3072]{3,2,1,0:T(8,128)(2,1)} %fusion.24), channel_id=1, source_target_pairs={{0,1},{1,0},{2,3},{3,2},{4,5},{5,4},{6,7},{7,6},{8,9},{9,8},{10,11... | collective-permute-start | bytes 9437192 | tf_op jit(solution)/shard_map/ppermute | solution.py:54
  568.7 94.2 %collective-permute-start.57 = (bf16[4,32,4096]{2,1,0:T(8,128)(2,1)}, bf16[4,32,4096]{2,1,0:T(8,128)(2,1)}, u32[]{:S(2)}, u32[]{:S(2)}) collective-permute-start(bf16[4,32,4096]{2,1,0:T(8,128)(2,1)} %get-tuple-element.40), channel_id=1, source_target_pairs={{0,24},{8,16},{16,8},{24,0},{1,25},{9,17},{17,9},{25,1},{2,26},{10... | collective-permute-start | bytes 3145736 | tf_op jit(solution)/shard_map/ppermute | solution.py:59
  570.1 94.1 %collective-permute-start.56 = (bf16[4,32,4096]{2,1,0:T(8,128)(2,1)}, bf16[4,32,4096]{2,1,0:T(8,128)(2,1)}, u32[]{:S(2)}, u32[]{:S(2)}) collective-permute-start(bf16[4,32,4096]{2,1,0:T(8,128)(2,1)} %get-tuple-element.41), channel_id=1, source_target_pairs={{0,16},{8,24},{16,0},{24,8},{1,17},{9,25},{17,1},{25,9},{2,18},{10... | collective-permute-start | bytes 3145736 | tf_op jit(solution)/shard_map/ppermute | solution.py:59
  571.7 92.6 %collective-permute-start.55 = (bf16[4,32,4096]{2,1,0:T(8,128)(2,1)}, bf16[4,32,4096]{2,1,0:T(8,128)(2,1)}, u32[]{:S(2)}, u32[]{:S(2)}) collective-permute-start(bf16[4,32,4096]{2,1,0:T(8,128)(2,1)} %get-tuple-element.39), channel_id=1, source_target_pairs={{0,8},{8,0},{16,24},{24,16},{1,9},{9,1},{17,25},{25,17},{2,10},{10... | collective-permute-start | bytes 3145736 | tf_op jit(solution)/shard_map/ppermute | solution.py:59
  (117 other events, 2012.3 us)

commit v2 on v1

--- a/solution.py
+++ b/solution.py
@@ -6,10 +6,10 @@
 from jax import lax
 from jax.experimental import pallas as pl
 from jax.experimental.pallas import tpu as pltpu
-from jax.sharding import PartitionSpec as P
+from jax.sharding import Mesh, PartitionSpec as P
 
 HEADS = 16
-EVERY = ("seq", "dp")
+EVERY = ("seq", "z", "core")
 LOG2E = math.log2(math.e)
 epsilon = 1e-05
 lowest = -1e30
@@ -41,17 +41,15 @@
 
 
 def sizes():
-    return lax.axis_size("seq"), lax.axis_size("dp") // 2
+    return lax.axis_size("seq"), lax.axis_size("z")
 
 
 def places():
-    dp = lax.axis_index("dp")
-    return lax.axis_index("seq"), dp // 2, dp % 2
+    return lax.axis_index("seq"), lax.axis_index("z"), lax.axis_index("core")
 
 
 def to_core(value):
-    count = lax.axis_size("dp")
-    return lax.ppermute(value, "dp", [(i, i ^ 1) for i in range(count)])
+    return lax.ppermute(value, "core", [(0, 1), (1, 0)])
 
 
 def to_seq(value, by):
@@ -60,83 +58,357 @@
 
 
 def to_z(value, by):
-    count = lax.axis_size("dp")
-    return lax.ppermute(value, "dp", [(i, (i + 2 * by) % count) for i in range(count)])
-
-
-def put_in_order(pieces):
+    count = lax.axis_size("z")
+    return lax.ppermute(value, "z", [(i, (i + by) % count) for i in range(count)])
+
+
+def after(value, *others):
+    return lax.optimization_barrier((value, *others))[0]
+
+
+def along_z(value):
+    return [value] + [to_z(value, by) for by in range(1, sizes()[1])]
+
+
+def along_seq(value):
+    return [value] + [to_seq(value, by) for by in range(1, sizes()[0])]
+
+
+def with_core(pieces):
+    return [p for piece in pieces for p in (piece, to_core(piece))]
+
+
+def owner_seq_outer(nz):
+    def owner(p, t, seq, z, core):
+        return ((seq ^ (p // 2)) * nz + lax.rem(z - t + nz, nz)) * 2 + (core ^ (p % 2))
+
+    return owner
+
+
+def owner_z_outer(nz):
+    def owner(p, t, seq, z, core):
+        return ((seq ^ t) * nz + lax.rem(z - p // 2 + nz, nz)) * 2 + (core ^ (p % 2))
+
+    return owner
+
+
+def gathered_small(shard):
+    ns, nz = sizes()
+    seq, z, core = places()
+    count = shard.shape[0]
+    column = jnp.stack(along_z(shard))
+    plane = jnp.stack(along_seq(column))
+    both = jnp.stack([plane, to_core(plane)]).reshape(-1, count)
+    device = jnp.arange(ns * nz * 2)
+    s, t, c = device // (2 * nz), (device // 2) % nz, device % 2
+    held_at = ((c ^ core) * ns + (s ^ seq)) * nz + (z - t + nz) % nz
+    chosen = held_at[:, None] == jnp.arange(ns * nz * 2)[None]
+    return matmul(chosen.astype(bf16), both)
+
+
+def halves(left, right):
+    ns, nz = sizes()
+    tokens, depth = left.shape
+    columns = right.shape[1]
+    rows = depth // (ns * nz * 2)
+    core = places()[2].astype(jnp.int32)
+    if rows % 16:
+        blocks = left_transposed(left, right).astype(bf16).reshape(ns, nz, 2, rows, columns)
+        return (
+            lax.dynamic_index_in_dim(blocks, core, 2, keepdims=False),
+            lax.dynamic_index_in_dim(blocks, 1 - core, 2, keepdims=False),
+        )
+    tile = depth // ns
+
+    def kernel(core_ref, left_ref, right_ref, mine_ref, other_ref):
+        product = left_transposed(left_ref[...], right_ref[...]).astype(bf16)
+        product = product.reshape(nz, 2, rows, columns)
+        first = core_ref[0] == 0
+        mine_ref[0] = jnp.where(first, product[:, 0], product[:, 1])
+        other_ref[0] = jnp.where(first, product[:, 1], product[:, 0])
+
+    out = pl.BlockSpec((1, nz, rows, columns), lambda i, core: (i, 0, 0, 0))
+    return pl.pallas_call(
+        kernel,
+        name="halves",
+        grid_spec=pltpu.PrefetchScalarGridSpec(
+            num_scalar_prefetch=1,
+            grid=(ns,),
+            in_specs=[
+                pl.BlockSpec((tokens, tile), lambda i, core: (0, i)),
+                pl.BlockSpec((tokens, columns), lambda i, core: (0, 0)),
+            ],
+            out_specs=[out, out],
+        ),
+        out_shape=[jax.ShapeDtypeStruct((ns, nz, rows, columns), bf16)] * 2,
+        compiler_params=pltpu.CompilerParams(vmem_limit_bytes=40 << 20),
+        cost_estimate=pl.CostEstimate(
+            flops=2 * tokens * depth * columns,
+            bytes_accessed=2 * (tokens * (depth + columns) + depth * columns),
+            transcendentals=0,
+        ),
+    )(core[None], left, right)
+
+
+def joint_halves(left, rights):
+    ns, nz = sizes()
+    tokens, depth = left.shape
+    pairs = len(rights)
+    width = pairs * 128
+    columns = 3 * ns * width
+    rows = depth // (ns * nz * 2)
+    if rows % 16:
+        right = jnp.concatenate(rights, 3)
+        return halves(left, right.transpose(2, 1, 0, 3).reshape(tokens, columns))
+    tile = depth // ns
+
+    def kernel(core_ref, left_ref, *refs):
+        rights_ref, mine_ref, other_ref = refs[:pairs], *refs[pairs:]
+        first = core_ref[0] == 0
+        rows_left = left_ref[...].T
+        for group in range(ns):
+            for kind in range(3):
+                at = (kind * ns + group) * width
+                right = jnp.concatenate([ref[group, kind] for ref in rights_ref], 1)
+                product = matmul(rows_left, right).astype(bf16)
+                product = product.reshape(nz, 2, rows, width)
+                mine_ref[0, :, :, at : at + width] = jnp.where(first, product[:, 0], product[:, 1])
+                other_ref[0, :, :, at : at + width] = jnp.where(first, product[:, 1], product[:, 0])
+
+    out = pl.BlockSpec((1, nz, rows, columns), lambda i, core: (i, 0, 0, 0))
+    right = pl.BlockSpec((ns, 3, tokens, 128), lambda i, core: (0, 0, 0, 0))
+    return pl.pallas_call(
+        kernel,
+        name="joint_halves",
+        grid_spec=pltpu.PrefetchScalarGridSpec(
+            num_scalar_prefetch=1,
+            grid=(ns,),
+            in_specs=[pl.BlockSpec((tokens, tile), lambda i, core: (0, i))] + [right] * pairs,
+            out_specs=[out, out],
+        ),
+        out_shape=[jax.ShapeDtypeStruct((ns, nz, rows, columns), bf16)] * 2,
+        compiler_params=pltpu.CompilerParams(vmem_limit_bytes=40 << 20),
+        cost_estimate=pl.CostEstimate(
+            flops=2 * tokens * depth * columns,
+            bytes_accessed=2 * (tokens * (depth + columns) + depth * columns),
+            transcendentals=0,
+        ),
+    )(places()[2].astype(jnp.int32)[None], left, *rights)
+
+
+def joint_back(grads, weight):
+    ns, _, tokens, _ = grads[0].shape
+    pairs = len(grads)
+    width = pairs * 128
+    depth = weight.shape[0]
+
+    def kernel(*refs):
+        grads_ref, weight_ref, out_ref = refs[:pairs], *refs[pairs:]
+        result = jnp.zeros((tokens, depth), f32)
+        for group in range(ns):
+            for kind in range(3):
+                at = (kind * ns + group) * width
+                grad = jnp.concatenate([ref[group, kind] for ref in grads_ref], 1)
+                result += right_transposed(grad, weight_ref[:, at : at + width])
+        out_ref[...] = result
+
+    return pl.pallas_call(
+        kernel,
+        name="joint_back",
+        out_shape=jax.ShapeDtypeStruct((tokens, depth), f32),
+        compiler_params=pltpu.CompilerParams(vmem_limit_bytes=24 << 20),
+        cost_estimate=pl.CostEstimate(
+            flops=2 * tokens * weight.size,
+            bytes_accessed=4 * weight.size + 4 * tokens * depth,
+            transcendentals=0,
+        ),
+    )(*grads, weight)
+
+
+def summed(terms, order, axis=0, cut=None):
+    _, _, rows, columns = terms[0].shape
+    n, m = terms[0].shape[axis], terms[0].shape[1 - axis]
+    first, last = cut or (0, columns // 1024)
+    count = len(terms)
+
+    def kernel(order_ref, *refs):
+        for k in range(n):
+            result = refs[k * count][0, 0].astype(f32)
+            for j in range(1, count):
+                result = result + refs[k * count + j][0, 0].astype(f32)
+            refs[n * count + k][0] = result.astype(bf16)
+
+    def block(k):
+        def index(i, c, order):
+            return (order[k], i, 0, first + c) if axis == 0 else (i, order[k], 0, first + c)
+
+        return pl.BlockSpec((1, 1, rows, 1024), index)
+
+    size = 2 * n * m * rows * (last - first) * 1024
+    return pl.pallas_call(
+        kernel,
+        name="summed",
+        grid_spec=pltpu.PrefetchScalarGridSpec(
+            num_scalar_prefetch=1,
+            grid=(m, last - first),
+            in_specs=[block(k) for k in range(n) for _ in range(count)],
+            out_specs=[pl.BlockSpec((1, rows, 1024), lambda i, c, order: (i, 0, c))] * n,
+        ),
+        out_shape=[jax.ShapeDtypeStruct((m, rows, (last - first) * 1024), bf16)] * n,
+        compiler_params=pltpu.CompilerParams(vmem_limit_bytes=32 << 20),
+        cost_estimate=pl.CostEstimate(
+            flops=0, bytes_accessed=(count + 1) * size, transcendentals=0
+        ),
+    )(order.astype(jnp.int32), *([*terms] * n))
+
+
+def first_step(mine, other, along, cut=None):
+    ns, nz = sizes()
+    if mine.shape[2] % 16:
+        if cut:
+            mine, other = (v[..., cut[0] * 1024 : cut[1] * 1024] for v in (mine, other))
+        return [(mine.astype(f32) + other.astype(f32)).astype(bf16)]
+    seq, z, _ = places()
+    if along == "seq":
+        parts = summed([mine, other], seq ^ jnp.arange(ns), 0, cut)
+        return [parts[0]] + [to_seq(parts[by], by) for by in range(1, ns)]
+    parts = summed([mine, other], (z + jnp.arange(nz)) % nz, 1, cut)
+    return [parts[0]] + [to_z(parts[by], by) for by in range(1, nz)]
+
+
+def second_sums(terms, along):
+    ns, nz = sizes()
+    if len(terms) == 1:
+        return terms
+    seq, z, _ = places()
+    order = (z + jnp.arange(nz)) % nz if along == "seq" else seq ^ jnp.arange(ns)
+    return summed([term[:, None] for term in terms], order)
+
+
+def second_step(parts, along):
+    ns, nz = sizes()
+    if len(parts) == 1:
+        return parts
+    if along == "seq":
+        return [parts[0][0]] + [to_z(parts[by][0], by) for by in range(1, nz)]
+    return [parts[0][0]] + [to_seq(parts[by][0], by) for by in range(1, ns)]
+
+
+def last_step(terms):
+    if len(terms) == 1:
+        chip = terms[0].reshape(-1, *terms[0].shape[2:])
+        return lax.psum_scatter(chip, ("seq", "z"), scatter_dimension=0, tiled=True)[0].astype(f32)
+    result = terms[0].astype(f32)
+    for term in terms[1:]:
+        result = result + term.astype(f32)
+    return result
+
+
+def over_seq(value):
+    return lax.all_to_all(value, "seq", 0, 0, tiled=True)
+
+
+def scattered_small(values):
+    ns, nz = sizes()
+    seq, z, core = places()
+    blocks = values.reshape(ns, nz, 2, -1)
+
+    def pick(array, index, axis):
+        return lax.dynamic_index_in_dim(array, index, axis, keepdims=False)
+
+    chip = pick(blocks, core, 2) + to_core(pick(blocks, 1 - core, 2))
+    plane = pick(chip, seq, 0)
+    for by in range(1, ns):
+        plane = plane + to_seq(pick(chip, seq ^ by, 0), by)
+    result = pick(plane, z, 0)
+    for by in range(1, nz):
+        result = result + to_z(pick(plane, (z + by) % nz, 0), by)
+    return result
+
+
+def joint_product(normed, shard, bias, later):
+    ns, nz = sizes()
+    tokens, features = normed.shape
+    rows, columns = shard.shape
+    width = features // ns
+    pairs = width // 128
+    if rows % 16:
+        full = lax.all_gather(shard, EVERY, axis=0, tiled=True)
+        last = lax.all_gather(later, EVERY, axis=0, tiled=True)
+        mixture = (matmul(normed, full) + bias).astype(bf16)
+        mixture = mixture.reshape(tokens, 3, ns, pairs, 128).transpose(3, 2, 1, 0, 4)
+        return full, last, [mixture[pair] for pair in range(pairs)]
+    one = jnp.stack(along_z(shard))
+    two = jnp.stack(along_seq(later))
+    ones = with_core(along_seq(one))
+    twos = with_core(along_z(two))
+    owners = [owner_seq_outer(nz)] * len(ones) + [owner_z_outer(nz)] * len(twos)
+    numbers = list(range(len(ones))) + list(range(len(twos)))
+    pieces = ones + twos
     count = len(pieces)
-    nz, rows, columns = pieces[0].shape
-    total = count * nz
+    slots = sum(piece.shape[0] for piece in pieces)
+    devices = slots // 2
 
     def kernel(place, *refs):
-        ins, out, held, in_sem, out_sem = refs[:count], *refs[count:]
+        ins = refs[:count]
+        normed_ref, bias_ref, full_ref, last_ref = refs[count : count + 4]
+        outs_ref = refs[count + 4 : count + 4 + pairs]
+        held, held_last, in_sem, out_sem = refs[count + 4 + pairs :]
         copies = []
         for p in range(count):
-            for t in range(nz):
-                slot = p * nz + t
-                copy = pltpu.make_async_copy(ins[p].at[t], held.at[slot], in_sem.at[slot])
+            to = held if p < len(ones) else held_last
+            for t in range(ins[p].shape[0]):
+                device = owners[p](numbers[p], t, place[0], place[1], place[2])
+                sem = in_sem.at[len(copies)]
+                copy = pltpu.make_async_copy(ins[p].at[t], to.at[device], sem)
                 copy.start()
                 copies.append(copy)
-        outs = []
-        for p in range(count):
-            for t in range(nz):
-                slot = p * nz + t
-                z = lax.rem(place[1] - t + nz, nz)
-                owner = ((place[0] ^ (p // 2)) * nz + z) * 2 + (place[2] ^ (p % 2))
-                copies[slot].wait()
-                copy = pltpu.make_async_copy(held.at[slot], out.at[owner], out_sem.at[slot])
-                copy.start()
-                outs.append(copy)
-        for copy in outs:
+        for copy in copies[:devices]:
             copy.wait()
-
-    size = total * rows * columns * 2
-    return pl.pallas_call(
+        full_copy = pltpu.make_async_copy(held, full_ref, out_sem.at[0])
+        full_copy.start()
+        for kind in range(3):
+            for group in range(ns):
+                at = kind * features + group * width
+                weight = held[:, :, at : at + width].reshape(features, width)
+                product = matmul(normed_ref[...], weight) + bias_ref[:, at : at + width]
+                product = product.astype(bf16)
+                for pair in range(pairs):
+                    outs_ref[pair][group, kind] = product[:, pair * 128 : pair * 128 + 128]
+        for copy in copies[devices:]:
+            copy.wait()
+        last_copy = pltpu.make_async_copy(held_last, last_ref, out_sem.at[1])
+        last_copy.start()
+        full_copy.wait()
+        last_copy.wait()
+
+    place = jnp.stack(places()).astype(jnp.int32)
+    anywhere = pl.BlockSpec(memory_space=pl.ANY)
+    inside = pl.BlockSpec(memory_space=pltpu.VMEM)
+    full, last, *mixture = pl.pallas_call(
         kernel,
-        name="put_in_order",
-        out_shape=jax.ShapeDtypeStruct((total, rows, columns), pieces[0].dtype),
-        in_specs=[pl.BlockSpec(memory_space=pltpu.SMEM)]
-        + [pl.BlockSpec(memory_space=pl.ANY)] * count,
-        out_specs=pl.BlockSpec(memory_space=pl.ANY),
+        name="joint_product",
+        out_shape=[
+            jax.ShapeDtypeStruct((devices, rows, columns), bf16),
+            jax.ShapeDtypeStruct((devices, *later.shape), bf16),
+        ]
+        + [jax.ShapeDtypeStruct((ns, 3, tokens, 128), bf16)] * pairs,
+        in_specs=[pl.BlockSpec(memory_space=pltpu.SMEM)] + [anywhere] * count + [inside] * 2,
+        out_specs=[anywhere, anywhere] + [inside] * pairs,
         scratch_shapes=[
-            pltpu.VMEM((total, rows, columns), pieces[0].dtype),
-            pltpu.SemaphoreType.DMA((total,)),
-            pltpu.SemaphoreType.DMA((total,)),
+            pltpu.VMEM((devices, rows, columns), bf16),
+            pltpu.VMEM((devices, *later.shape), bf16),
+            pltpu.SemaphoreType.DMA((slots,)),
+            pltpu.SemaphoreType.DMA((2,)),
         ],
-        compiler_params=pltpu.CompilerParams(vmem_limit_bytes=size + (4 << 20)),
-        cost_estimate=pl.CostEstimate(flops=0, bytes_accessed=2 * size, transcendentals=0),
-    )(jnp.stack(places()).astype(jnp.int32), *pieces).reshape(total * rows, columns)
-
-
-def gathered(shard):
-    ns, nz = sizes()
-    column = jnp.stack([shard] + [to_z(shard, by) for by in range(1, nz)])
-    planes = [column] + [to_seq(column, by) for by in range(1, ns)]
-    pieces = []
-    for plane in planes:
-        pieces += [plane, to_core(plane)]
-    return put_in_order(pieces)
-
-
-def scattered(grad):
-    ns, nz = sizes()
-    seq, z, core = places()
-    columns = grad.shape[1]
-    blocks = grad.reshape(ns, nz, 2, -1, columns)
-    mine = lax.dynamic_index_in_dim(blocks, core, 2, keepdims=False)
-    other = lax.dynamic_index_in_dim(blocks, 1 - core, 2, keepdims=False)
-    chip = (mine.astype(f32) + to_core(other.astype(bf16)).astype(f32)).astype(bf16)
-    total = lax.dynamic_index_in_dim(chip, seq, 0, keepdims=False).astype(f32)
-    for by in range(1, ns):
-        piece = lax.dynamic_index_in_dim(chip, seq ^ by, 0, keepdims=False)
-        total = total + to_seq(piece, by).astype(f32)
-    plane = total.astype(bf16)
-    total = lax.dynamic_index_in_dim(plane, z, 0, keepdims=False).astype(f32)
-    for by in range(1, nz):
-        piece = lax.dynamic_index_in_dim(plane, (z + by) % nz, 0, keepdims=False)
-        total = total + to_z(piece, by).astype(f32)
-    return total
+        compiler_params=pltpu.CompilerParams(vmem_limit_bytes=24 << 20),
+        cost_estimate=pl.CostEstimate(
+            flops=2 * tokens * features * columns,
+            bytes_accessed=6 * features * columns,
+            transcendentals=0,
+        ),
+    )(place, *pieces, normed, bias[None])
+    return full.reshape(features, columns), last.reshape(features, -1), mixture
 
 
 def half_lanes(shape, which):
@@ -229,7 +501,7 @@
         ],
         compiler_params=pltpu.CompilerParams(vmem_limit_bytes=40 << 20),
         cost_estimate=pl.CostEstimate(
-            flops=pairs * per_block * ns * (ns + 1) // 2 * 4,
+            flops=pairs * per_block * ns * (ns + 1) // 2 * 12,
             bytes_accessed=qkv.size * 2 + ns * length * width * 6,
             transcendentals=pairs * ns * (ns + 1) * length * length,
         ),
@@ -329,7 +601,7 @@
         out_shape=jax.ShapeDtypeStruct((ns, 3, length, width), bf16),
         compiler_params=pltpu.CompilerParams(vmem_limit_bytes=48 << 20),
         cost_estimate=pl.CostEstimate(
-            flops=pairs * per_block * ns * (ns + 1) // 2 * 4,
+            flops=pairs * per_block * ns * (ns + 1) // 2 * 12,
             bytes_accessed=qkv.size * 4 + ns * length * width * 6,
             transcendentals=pairs * ns * (ns + 1) * length * length,
         ),
@@ -372,10 +644,16 @@
         second_gain,
         second_shift,
     )
-    packed = lax.all_gather(jnp.concatenate(small)[None], EVERY, axis=0, tiled=True)
+    sizes_small = [one.shape[0] for one in small]
+    count = sum(sizes_small)
+    packed, first = jnp.zeros((count,), f32), 0
+    for one in small:
+        packed += jnp.pad(one.astype(f32), (first, count - first - one.shape[0]))
+        first += one.shape[0]
+    packed = gathered_small(packed.astype(bf16))
     smalls, first = [], 0
     for one in small:
-        smalls.append(packed[:, first : first + one.shape[0]].reshape(-1).astype(f32))
+        smalls.append(packed[:, first : first + one.shape[0]].reshape(-1))
         first += one.shape[0]
     (
         query_add,
@@ -389,10 +667,8 @@
         shift_two,
     ) = smalls
 
-    joint_full = gathered(joint_weight)
-    projection_full = gathered(projection)
-    upward_full = gathered(upward_weight)
-    downward_full = gathered(downward_weight)
+    upward_full = lax.all_gather(upward_weight, EVERY, axis=0, tiled=True)
+    downward_full = lax.all_gather(downward_weight, EVERY, axis=0, tiled=True)
 
     slopes = 2.0 ** (-8.0 * (jnp.arange(HEADS, dtype=f32) + 1.0) / HEADS) * (4.0 / (length * ns))
     slopes = lax.dynamic_slice_in_dim(slopes, seq * group, group)
@@ -402,12 +678,16 @@
     normed, first_pull = jax.vjp(layer_norm, inputs, gain_one, shift_one)
     normed_low = normed.astype(bf16)
     zeros = jnp.zeros_like(query_add)
-    mixture = matmul(normed_low, joint_full) + jnp.concatenate([query_add, zeros, value_add])
-    mixture = mixture.astype(bf16).reshape(length, 3, ns, width).transpose(2, 1, 0, 3)
-    qkv = lax.all_to_all(mixture, "seq", 0, 0, tiled=True)
-    attended, attended_full, logs = attention_forward(qkv, order, slopes)
-    attended = lax.all_to_all(attended, "seq", 0, 0, tiled=True)
-    attended_low = attended.transpose(1, 0, 2).reshape(length, features)
+    bias = jnp.concatenate([query_add, zeros, value_add])
+    joint_full, projection_full, mixture = joint_product(
+        normed_low, joint_weight, bias, projection
+    )
+    pairs = len(mixture)
+    slopes = slopes.reshape(pairs, 2)
+    qkv = [over_seq(one) for one in mixture]
+    forward = [attention_forward(qkv[pair], order, slopes[pair]) for pair in range(pairs)]
+    attended = jnp.stack([over_seq(one[0]) for one in forward])
+    attended_low = attended.transpose(2, 1, 0, 3).reshape(length, features)
 
     middle = inputs + matmul(attended_low, projection_full) + offset_add
     second, second_pull = jax.vjp(layer_norm, middle, gain_two, shift_two)
@@ -420,30 +700,57 @@
 
     grad_result = cotangent.reshape(length, features)
     grad_result_full = grad_result.astype(f32)
-    downward_grad = left_transposed(active_low, grad_result)
+    downward_mine, downward_other = halves(active_low, grad_result)
     downwardbias_grad = jnp.sum(grad_result_full, 0)
-    (grad_hidden,) = gelu_pull(right_transposed(grad_result, downward_full))
+    downward_other = to_core(downward_other)
+    (grad_hidden,) = gelu_pull(right_transposed(after(grad_result, downward_mine), downward_full))
     grad_hidden_low = grad_hidden.astype(bf16)
-    upward_grad = left_transposed(second_low, grad_hidden_low)
+    downward_chip = (downward_mine.astype(f32) + downward_other.astype(f32)).astype(bf16)
+    downward_sum = lax.psum_scatter(
+        downward_chip.reshape(ns * nz, -1, features), ("seq", "z"), scatter_dimension=0, tiled=True
+    )[0].astype(f32)
+    upward_mine, upward_other = halves(after(second_low, downward_chip), grad_hidden_low)
+    upward_other = to_core(upward_other)
     upwardbias_grad = jnp.sum(grad_hidden_low.astype(f32), 0)
-    grad_second = right_transposed(grad_hidden_low, upward_full)
+    grad_second = right_transposed(after(grad_hidden_low, upward_mine), upward_full)
     middle_part, secondgain_grad, secondshift_grad = second_pull(grad_second)
-    downward_sum = scattered(downward_grad)
-    upward_sum = scattered(upward_grad)
 
     grad_middle = grad_result_full + middle_part
     grad_branch = grad_middle.astype(bf16)
-    projection_sum = scattered(left_transposed(attended_low, grad_branch))
     offset_grad = jnp.sum(grad_branch.astype(f32), 0)
     grad_attended = right_transposed(grad_branch, projection_full).astype(bf16)
-    grad_attended = grad_attended.reshape(length, ns, width).transpose(1, 0, 2)
-    grad_attended = lax.all_to_all(grad_attended, "seq", 0, 0, tiled=True)
-    grad_qkv = attention_backward(qkv, grad_attended, attended_full, logs, order, slopes)
-    grad_qkv = lax.all_to_all(grad_qkv, "seq", 0, 0, tiled=True)
-    grad_mixture = grad_qkv.transpose(2, 1, 0, 3).reshape(length, 3 * features)
-    joint_sum = scattered(left_transposed(normed_low, grad_mixture))
-    mixture_sums = jnp.sum(grad_mixture.astype(f32), 0)
-    grad_normed = right_transposed(grad_mixture, joint_full)
+    grad_attended = grad_attended.reshape(length, ns, pairs, 128).transpose(2, 1, 0, 3)
+    grad_attended = [over_seq(grad_attended[pair]) for pair in range(pairs)]
+    projection_mine, projection_other = halves(attended_low, grad_branch)
+    projection_other = to_core(projection_other)
+    upward_terms = first_step(upward_mine, upward_other, "seq")
+    projection_terms = first_step(projection_mine, projection_other, "seq")
+    grad_attended[0] = after(grad_attended[0], upward_terms[0], projection_terms[0])
+    grad_qkv = []
+    for pair in range(pairs):
+        if pair == pairs - 1:
+            upward_parts = second_sums(upward_terms, "seq")
+            projection_parts = second_sums(projection_terms, "seq")
+            grad_attended[pair] = after(grad_attended[pair], upward_parts[0], projection_parts[0])
+        low, full, logs = forward[pair]
+        grad = attention_backward(qkv[pair], grad_attended[pair], full, logs, order, slopes[pair])
+        grad_qkv.append(over_seq(grad))
+    upward_sum = last_step(second_step(upward_parts, "seq"))
+    projection_sum = last_step(second_step(projection_parts, "seq"))
+    grad_qkv[0] = after(grad_qkv[0], upward_sum, projection_sum, downward_sum, output)
+    joint_mine, joint_other = joint_halves(normed_low, grad_qkv)
+    joint_other = to_core(joint_other)
+    joint_terms = first_step(joint_mine, joint_other, "seq", (0, 2))
+    joint_more = first_step(joint_mine, joint_other, "z", (2, 3))
+    joint_parts = second_sums(joint_terms, "seq")
+    more_parts = second_sums(joint_more, "z")
+    joint_terms = second_step(joint_parts, "seq")
+    joint_more = second_step(more_parts, "z")
+    joint_sum = jnp.concatenate([last_step(joint_terms), last_step(joint_more)], 1)
+    grad_qkv[0] = after(grad_qkv[0], joint_parts[0], more_parts[0])
+    mixture_sums = jnp.stack([jnp.sum(grad.astype(f32), 2) for grad in grad_qkv])
+    mixture_sums = mixture_sums.transpose(2, 1, 0, 3).reshape(-1)
+    grad_normed = joint_back(grad_qkv, joint_full)
     input_part, firstgain_grad, firstshift_grad = first_pull(grad_normed)
     input_grad = (grad_middle + input_part).astype(bf16).reshape(members, length, features)
 
@@ -459,7 +766,7 @@
         secondshift_grad,
     )
     packed = jnp.concatenate([g.reshape(devices, -1) for g in grads], 1)
-    packed = lax.psum_scatter(packed, EVERY, scatter_dimension=0, tiled=True)[0]
+    packed = scattered_small(packed)
     sums, first = [], 0
     for one in small:
         sums.append(packed[first : first + one.shape[0]])
@@ -484,11 +791,14 @@
 
 
 def solution(mesh):
-    tokens = P("dp", "seq", None)
+    ns, dp = mesh.devices.shape
+    split = Mesh(mesh.devices.reshape(ns, dp // 2, 2), EVERY)
+    tokens = P(("z", "core"), "seq", None)
     matrix = P(EVERY, None)
     vector = P(EVERY)
-    kinds = (tokens, tokens, P("dp", None), matrix, vector, vector, matrix, vector, vector, vector)
+    orders = P(("z", "core"), None)
+    kinds = (tokens, tokens, orders, matrix, vector, vector, matrix, vector, vector, vector)
     kinds += (matrix, vector, matrix, vector, vector, vector)
     in_specs = kinds
     out_specs = kinds[:2] + kinds[3:]
-    return jax.shard_map(body, mesh=mesh, in_specs=in_specs, out_specs=out_specs, check_vma=False)
+    return jax.shard_map(body, mesh=split, in_specs=in_specs, out_specs=out_specs, check_vma=False)

time: 786 us -> 583 us (0.74)
  blocking collectives: 122 us -> 0 us
  local copies, waits for them, and re-layouts: 92.3 us -> 48.7 us
  waiting for transfers between devices: 252 us -> 210 us
  matrix products: 93.5 us -> 52.1 us
  Pallas kernels: 91.7 us -> 123 us
  starting transfers between devices: 77.5 us -> 95.1 us
  other arithmetic: 45 us -> 30.4 us
  between operations: 2.2 us -> 15.2 us
    ppermute x24, waiting for transfers between devices: 202 us -> 92.8 us  [to_seq(): return lax.ppermute(value, 'seq', [(i, i ^ by) for i in range(count)])]
    unnamed x1 -> x0, blocking collectives: 79.4 us -> none
    all_to_all x4 -> x8, waiting for transfers between devices: 0.01 us -> 52.4 us  [over_seq(): return lax.all_to_all(value, 'seq', 0, 0, tiled=True)]
    all_gather x1 -> x0, blocking collectives: 42.9 us -> none  [body(): lax.all_gather(jnp.concatenate(small)[None], EVERY, axis=0, tiled=True)]
    pallas_call x4 -> x14, Pallas kernels: 27.6 us -> 61 us  [the longest x8 24.7 us: summed(): pl.pallas_call(kernel, name='summed', grid_spec=pltpu.PrefetchScalarGridS...]
    dot_general x4 -> x0, matrix products: 33.4 us -> none  [left_transposed(): lax.dot_general(left, right, (((0,), (0,)), ((), ())), preferred_element_...]
    convert_element_type x13 -> x0, local copies, waits for them, and re-layouts: 23.9 us -> none  [the longest x4 15.3 us: scattered(): other.astype(bf16)]
    convert_element_type x10 -> x5, other arithmetic: 26.5 us -> 11.1 us  [the longest x1 6.32 us: body(): (downward_mine.astype(f32) + downward_other.astype(f32)).astype(bf16)]
  transfers between devices with their start and end apart: 72 -> 73, of which waited for: 21 -> 27; matrix products, arithmetic and copies ran while one was open for 18% -> 15% of each run, Pallas kernels for 12% -> 19%
where the time goes in v2:
time: 583 us; the launch traced here: 574 us
  waiting for transfers between devices  210 us (36%)
  Pallas kernels  123 us (21%)
  starting transfers between devices  95.1 us (16%)
  matrix products  52.1 us (9%)
  local copies, waits for them, and re-layouts  48.7 us (8%)
  other arithmetic  30.4 us (5%)
  between operations  15.2 us (3%)
    ppermute x24, waiting for transfers between devices, to_seq(): return lax.ppermute(value, 'seq', [(i, i ^ by) for i in range(count)])  92.8 us
    ppermute x24, waiting for transfers between devices, to_z(): lax.ppermute(value, 'z', [(i, (i + by) % count) for i in range(count)])  56 us
    all_to_all x8, waiting for transfers between devices, over_seq(): return lax.all_to_all(value, 'seq', 0, 0, tiled=True)  52.4 us
    pallas_call x2, Pallas kernels, attention_backward(): pl.pallas_call(kernel, name='attention_backward', grid_spec=grid_spec, ou...  35.2 us
    all_to_all x8, starting transfers between devices, over_seq(): return lax.all_to_all(value, 'seq', 0, 0, tiled=True)  31.8 us
    ppermute x24, starting transfers between devices, to_z(): lax.ppermute(value, 'z', [(i, (i + by) % count) for i in range(count)])  31.5 us
    ppermute x24, starting transfers between devices, to_seq(): return lax.ppermute(value, 'seq', [(i, i ^ by) for i in range(count)])  29 us
    dot_general x3, matrix products, right_transposed(): lax.dot_general(left, right, (((1,), (1,)), ((), ())), preferred_element_...  27.4 us
  transfers between devices with their start and end apart: 73, of which 27 were waited for; matrix products, arithmetic and copies ran while one was open for 15% of the time, Pallas kernels for 19%

profile of v2, /device:TPU:0, one launch (start us, length us, event | category | flops | bytes accessed | tf_op | source)
XLA Modules:
  0.0 574.1 jit_solution(11416220584742958179)
XLA Ops:
  34.4 10.4 %collective-permute-done.1 = bf16[32,3072]{1,0:T(8,128)(2,1)S(1)} collective-permute-done((bf16[32,3072]{1,0:T(8,128)(2,1)}, bf16[32,3072]{1,0:T(8,128)(2,1)S(1)}, u32[]{:S(2)}, u32[]{:S(2)}) %collective-permute-start.1) | collective-permute-done | bytes 196640 | tf_op jit(solution)/shard_map/ppermute | solution.py:62
  49.0 16.2 %collective-permute-done.14.refs_10_ = bf16[4,32,1024]{2,1,0:T(8,128)(2,1)} collective-permute-done((bf16[4,32,1024]{2,1,0:T(8,128)(2,1)S(1)}, bf16[4,32,1024]{2,1,0:T(8,128)(2,1)}, u32[]{:S(2)}, u32[]{:S(2)}) %collective-permute-start.14) | collective-permute-done | bytes 262176 | tf_op jit(solution)/shard_map/ppermute | solution.py:62
  65.3 14.5 %collective-permute-done.16.refs_12_ = bf16[4,32,1024]{2,1,0:T(8,128)(2,1)S(1)} collective-permute-done((bf16[4,32,1024]{2,1,0:T(8,128)(2,1)S(1)}, bf16[4,32,1024]{2,1,0:T(8,128)(2,1)S(1)}, u32[]{:S(2)}, u32[]{:S(2)}) %collective-permute-start.16) | collective-permute-done | bytes 262176 | tf_op jit(solution)/shard_map/ppermute | solution.py:62
  81.6 9.0 %collective-permute-done.8.refs_6_ = bf16[4,32,3072]{2,1,0:T(8,128)(2,1)S(1)} collective-permute-done((bf16[4,32,3072]{2,1,0:T(8,128)(2,1)S(1)}, bf16[4,32,3072]{2,1,0:T(8,128)(2,1)S(1)}, u32[]{:S(2)}, u32[]{:S(2)}) %collective-permute-start.8) | collective-permute-done | bytes 786464 | tf_op jit(solution)/shard_map/ppermute | solution.py:57
  95.6 12.5 %joint_product.1 = (bf16[32,32,3072]{2,1,0:T(8,128)(2,1)S(1)}, bf16[32,32,1024]{2,1,0:T(8,128)(2,1)S(1)}, bf16[4,3,512,128]{3,2,1,0:T(8,128)(2,1)S(1)}, bf16[4,3,512,128]{3,2,1,0:T(8,128)(2,1)}) custom-call(s32[3]{0:T(128)S(1)} %pad_add_fusion.place, bf16[4,32,3072]{2,1,0:T(8,128)(2,1)S(1)} %pad_maximum_fusion.refs_0_, ...), custom_call_target="tpu_custom_call" | custom-call | flops 3221225472 | bytes 18874368 | tf_op jit(solution)/shard_map/joint_product/pallas_call | solution.py:388
  118.6 20.7 %all-to-all-done.2.q_ref.kv_ref.qkv_ref = bf16[4,3,512,128]{3,2,1,0:T(8,128)(2,1)S(1)} async-done(((bf16[4,3,512,128]{3,2,1,0:T(8,128)(2,1)}), bf16[4,3,512,128]{3,2,1,0:T(8,128)(2,1)S(1)}, u32[]{:S(2)}, u32[]{:S(2)}) %all-to-all-start.2) | async-done | bytes 1572896 | tf_op jit(solution)/shard_map/all_to_all | solution.py:308
  143.0 13.1 %attention_forward.3 = (bf16[4,512,128]{2,1,0:T(8,128)(2,1)S(1)}, f32[4,512,128]{2,1,0:T(8,128)S(1)}, f32[1,4,8,512]{3,2,1,0:T(8,128)S(1)}) custom-call(s32[4]{0:T(128)S(1)} %get-tuple-element.73.order_ref, f32[2]{0:T(128)S(1)} %get-tuple-element.175.slope_ref, bf16[4,3,512,128]{3,2,1,0:T(8,128)(2,1)S(1)} %all-to-all-done.2.q_ref.kv_ref.qkv_ref, ...), custom_call_target="tpu_custom_call" | custom-call | flops 32212254720 | bytes 3145728 | tf_op jit(solution)/shard_map/attention_forward/pallas_call | solution.py:493
  157.8 11.6 %all-to-all-done.q_ref.kv_ref.qkv_ref = bf16[4,3,512,128]{3,2,1,0:T(8,128)(2,1)S(1)} async-done(((bf16[4,3,512,128]{3,2,1,0:T(8,128)(2,1)}), bf16[4,3,512,128]{3,2,1,0:T(8,128)(2,1)S(1)}, u32[]{:S(2)}, u32[]{:S(2)}) %all-to-all-start) | async-done | bytes 1572896 | tf_op jit(solution)/shard_map/all_to_all | solution.py:308
  173.4 13.7 %attention_forward.2 = (bf16[4,512,128]{2,1,0:T(8,128)(2,1)}, f32[4,512,128]{2,1,0:T(8,128)S(1)}, f32[1,4,8,512]{3,2,1,0:T(8,128)S(1)}) custom-call(s32[4]{0:T(128)S(1)} %get-tuple-element.73.order_ref, f32[2]{0:T(128)S(1)} %get-tuple-element.174.slope_ref, bf16[4,3,512,128]{3,2,1,0:T(8,128)(2,1)S(1)} %all-to-all-done.q_ref.kv_ref.qkv_ref, ...), custom_call_target="tpu_custom_call" | custom-call | flops 32212254720 | bytes 3145728 | tf_op jit(solution)/shard_map/attention_forward/pallas_call | solution.py:493
  193.3 7.5 %all-to-all-done.1 = bf16[4,512,128]{2,1,0:T(8,128)(2,1)S(1)} async-done(((bf16[4,512,128]{2,1,0:T(8,128)(2,1)}), bf16[4,512,128]{2,1,0:T(8,128)(2,1)S(1)}, u32[]{:S(2)}, u32[]{:S(2)}) %all-to-all-start.1) | async-done | bytes 524320 | tf_op jit(solution)/shard_map/all_to_all | solution.py:308
  207.6 12.3 %multiply_convert_fusion = (bf16[512,4096]{1,0:T(8,128)(2,1)S(1)}, f32[512,4096]{1,0:T(8,128)}) fusion(f32[4096]{0:T(1024)S(1)} %slice_bitcast_fusion.2, bf16[512,1024]{1,0:T(8,128)(2,1)S(1)} %add_convert_fusion.3.left_ref, bf16[1024,4096]{1,0:T(8,128)(2,1)} %all-gather.3.cloned.1.call-done), kind=kOutput, calls=%fused_computation.11 | convolution fusion | flops 4315938816 | bytes 22036480 | tf_op jit(solution)/shard_map/dot_general | solution.py:32
  219.9 6.5 %halves.3 = (bf16[4,4,128,1024]{3,2,1,0:T(8,128)(2,1)S(1)}, bf16[4,4,128,1024]{3,2,1,0:T(8,128)(2,1)}) custom-call(s32[1]{0:T(128)} %bitcast.4.core_ref, bf16[512,4096]{1,0:T(8,128)(2,1)S(1)} %get-tuple-element.178.left_ref, bf16[512,1024]{1,0:T(8,128)(2,1)S(1)} %bitcast.223), custom_call_target="tpu_custom_call" | custom-call | flops 4294967296 | bytes 13631488 | tf_op jit(solution)/shard_map/halves/pallas_call | solution.py:131
  228.4 14.0 %convert_reduce_fusion = (f32[4096]{0:T(1024)}, bf16[512,4096]{1,0:T(8,128)(2,1)S(1)}) fusion(f32[512,4096]{1,0:T(8,128)} %get-tuple-element.179, f32[4096]{0:T(1024)S(1)} %slice_bitcast_fusion.2, bf16[512,1024]{1,0:T(8,128)(2,1)S(1)} %bitcast.224, bf16[4096,1024]{1,0:T(8,128)(2,1)} %all-gather.5.cloned.1.call-done), kind=kOutput, calls=%fused_computation.9 | convolution fusion | flops 4343197696 | bytes 22052864 | tf_op jit(solution)/shard_map/dot_general | solution.py:40
  248.7 6.4 %halves.4 = (bf16[4,4,32,4096]{3,2,1,0:T(8,128)(2,1)S(1)}, bf16[4,4,32,4096]{3,2,1,0:T(8,128)(2,1)}) custom-call(s32[1]{0:T(128)} %bitcast.4.core_ref, bf16[512,1024]{1,0:T(8,128)(2,1)S(1)} %add_convert_fusion.3.left_ref, bf16[512,4096]{1,0:T(8,128)(2,1)S(1)} %get-tuple-element.84.right_ref), custom_call_target="tpu_custom_call" | custom-call | flops 4294967296 | bytes 13631488 | tf_op jit(solution)/shard_map/halves/pallas_call | solution.py:131
  255.1 9.6 %multiply_reduce_fusion = (f32[1024]{0:T(1024)}, f32[512]{0:T(512)S(1)}, f32[1024]{0:T(1024)}, f32[512,1024]{1,0:T(8,128)S(1)}) fusion(f32[512,1024]{1,0:T(8,128)S(1)} %copy-done.45, f32[512]{0:T(512)S(1)} %fusion.37, f32[512]{0:T(512)S(1)} %broadcast_multiply_fusion, f32[1024]{0:T(1024)S(1)} %mul.188, ...), kind=kOutput, calls=%fused_computation.34 | convolution fusion | flops 4299159040 | bytes 16795648 | tf_op jit(solution)/shard_map/dot_general | solution.py:40
  301.7 9.2 %fusion.21 = bf16[1,512,1024]{2,1,0:T(8,128)(2,1)} fusion(f32[512,1024]{1,0:T(8,128)} %copy-done.44, bf16[512,4096]{1,0:T(8,128)(2,1)S(1)} %copy-done.35, bf16[4096,1024]{1,0:T(8,128)(2,1)} %all-gather.5.cloned.1.call-done, f32[1024]{0:T(1024)S(1)} %copy-done.66), kind=kOutput, calls=%fused_computation.42 | convolution fusion | flops 4296540160 | bytes 15732736 | tf_op jit(solution)/shard_map/dot_general | solution.py:32
  313.8 9.7 %summed.8 = (bf16[4,32,4096]{2,1,0:T(8,128)(2,1)S(1)}, bf16[4,32,4096]{2,1,0:T(8,128)(2,1)S(1)}, bf16[4,32,4096]{2,1,0:T(8,128)(2,1)S(1)}, bf16[4,32,4096]{2,1,0:T(8,128)(2,1)S(1)}) custom-call(s32[4]{0:T(128)S(1)} %iota_xor_fusion.order_ref, bf16[4,4,32,4096]{3,2,1,0:T(8,128)(2,1)S(1)} %copy-done.1, ...), custom_call_target="tpu_custom_call" | custom-call | bytes 12582912 | tf_op jit(solution)/shard_map/summed/pallas_call | solution.py:248
  335.4 17.1 %attention_backward.2 = bf16[4,3,512,128]{3,2,1,0:T(8,128)(2,1)S(1)} custom-call(s32[4]{0:T(128)S(1)} %get-tuple-element.73.order_ref, f32[2]{0:T(128)S(1)} %get-tuple-element.174.slope_ref, bf16[4,3,512,128]{3,2,1,0:T(8,128)(2,1)S(1)} %copy-done.13, bf16[4,512,128]{2,1,0:T(8,128)(2,1)S(1)} %all-to-all-done.4.grad_ref, f32[4,512,128]{2,1,0:T(8,128)S(1)} %copy-done.39, ...), custom_call_target="tpu_custom_call" | custom-call | flops 80530636800 | bytes 4718592 | tf_op jit(solution)/shard_map/attention_backward/pallas_call | solution.py:597
  353.7 36.6 %collective-permute-done.30 = bf16[4,32,4096]{2,1,0:T(8,128)(2,1)S(1)} collective-permute-done((bf16[4,32,4096]{2,1,0:T(8,128)(2,1)}, bf16[4,32,4096]{2,1,0:T(8,128)(2,1)S(1)}, u32[]{:S(2)}, u32[]{:S(2)}) %collective-permute-start.30) | collective-permute-done | bytes 1048608 | tf_op jit(solution)/shard_map/ppermute | solution.py:57
  390.3 28.8 %collective-permute-done.32 = bf16[4,32,4096]{2,1,0:T(8,128)(2,1)S(1)} collective-permute-done((bf16[4,32,4096]{2,1,0:T(8,128)(2,1)}, bf16[4,32,4096]{2,1,0:T(8,128)(2,1)S(1)}, u32[]{:S(2)}, u32[]{:S(2)}) %collective-permute-start.32) | collective-permute-done | bytes 1048608 | tf_op jit(solution)/shard_map/ppermute | solution.py:57
  429.8 18.1 %attention_backward.3 = bf16[4,3,512,128]{3,2,1,0:T(8,128)(2,1)S(1)} custom-call(s32[4]{0:T(128)S(1)} %get-tuple-element.73.order_ref, f32[2]{0:T(128)S(1)} %copy-done.21, bf16[4,3,512,128]{3,2,1,0:T(8,128)(2,1)S(1)} %copy-done.11, bf16[4,512,128]{2,1,0:T(8,128)(2,1)} %all-to-all-done.6.grad_ref, f32[4,512,128]{2,1,0:T(8,128)S(1)} %copy-done.37, ...), custom_call_target="tpu_custom_call" | custom-call | flops 80530636800 | bytes 4718592 | tf_op jit(solution)/shard_map/attention_backward/pallas_call | solution.py:597
  457.1 12.6 %all-to-all-done.7.refs_1_ = bf16[4,3,512,128]{3,2,1,0:T(8,128)(2,1)S(1)} async-done(((bf16[4,3,512,128]{3,2,1,0:T(8,128)(2,1)}), bf16[4,3,512,128]{3,2,1,0:T(8,128)(2,1)S(1)}, u32[]{:S(2)}, u32[]{:S(2)}) %all-to-all-start.7) | async-done | bytes 1572896 | tf_op jit(solution)/shard_map/all_to_all | solution.py:308
  500.9 6.8 %collective-permute-done.47 = bf16[4,32,1024]{2,1,0:T(8,128)(2,1)S(1)} collective-permute-done((bf16[4,32,1024]{2,1,0:T(8,128)(2,1)}, bf16[4,32,1024]{2,1,0:T(8,128)(2,1)S(1)}, u32[]{:S(2)}, u32[]{:S(2)}) %collective-permute-start.47) | collective-permute-done | bytes 262176 | tf_op jit(solution)/shard_map/ppermute | solution.py:62
  559.8 6.5 %collective-permute-done.50 = bf16[32,2048]{1,0:T(8,128)(2,1)S(1)} collective-permute-done((bf16[32,2048]{1,0:T(8,128)(2,1)S(1)}, bf16[32,2048]{1,0:T(8,128)(2,1)S(1)}, u32[]{:S(2)}, u32[]{:S(2)}) %collective-permute-start.50) | collective-permute-done | bytes 131104 | tf_op jit(solution)/shard_map/ppermute | solution.py:62
  (375 shorter events, 235.5 us)
Async XLA Ops:
  7.2 200.4 %all-gather.3.cloned.1.call-start = ((), (), s32[]{:S(2)}) async-start(), calls=%async_computation.9 | async-start | bytes 8650752 | tf_op jit(solution)/shard_map/all_gather | solution.py:670
  7.9 220.4 %all-gather.5.cloned.1.call-start = ((), (), s32[]{:S(2)}) async-start(), calls=%async_computation.10 | async-start | bytes 8650752 | tf_op jit(solution)/shard_map/all_gather | solution.py:671
  44.8 36.3 %collective-permute-start.4 = (bf16[4,32,3072]{2,1,0:T(8,128)(2,1)S(1)}, bf16[4,32,3072]{2,1,0:T(8,128)(2,1)S(1)}, u32[]{:S(2)}, u32[]{:S(2)}) collective-permute-start(bf16[4,32,3072]{2,1,0:T(8,128)(2,1)S(1)} %pad_maximum_fusion.refs_0_), channel_id=1, source_target_pairs={{0,8},{8,0},{16,24},{24,16},{1,9},{9,1},{17,25},{25,17},{2,10},{10... | collective-permute-start | bytes 2359304 | tf_op jit(solution)/shard_map/ppermute | solution.py:57
  46.2 35.0 %collective-permute-start.6 = (bf16[4,32,3072]{2,1,0:T(8,128)(2,1)S(1)}, bf16[4,32,3072]{2,1,0:T(8,128)(2,1)S(1)}, u32[]{:S(2)}, u32[]{:S(2)}) collective-permute-start(bf16[4,32,3072]{2,1,0:T(8,128)(2,1)S(1)} %pad_maximum_fusion.refs_0_), channel_id=1, source_target_pairs={{0,16},{8,24},{16,0},{24,8},{1,17},{9,25},{17,1},{25,9},{2,18},{10... | collective-permute-start | bytes 2359304 | tf_op jit(solution)/shard_map/ppermute | solution.py:57
  47.0 43.7 %collective-permute-start.8 = (bf16[4,32,3072]{2,1,0:T(8,128)(2,1)S(1)}, bf16[4,32,3072]{2,1,0:T(8,128)(2,1)S(1)}, u32[]{:S(2)}, u32[]{:S(2)}) collective-permute-start(bf16[4,32,3072]{2,1,0:T(8,128)(2,1)S(1)} %pad_maximum_fusion.refs_0_), channel_id=1, source_target_pairs={{0,24},{8,16},{16,8},{24,0},{1,25},{9,17},{17,9},{25,1},{2,26},{10... | collective-permute-start | bytes 2359304 | tf_op jit(solution)/shard_map/ppermute | solution.py:57
  48.9 30.8 %collective-permute-start.16 = (bf16[4,32,1024]{2,1,0:T(8,128)(2,1)S(1)}, bf16[4,32,1024]{2,1,0:T(8,128)(2,1)S(1)}, u32[]{:S(2)}, u32[]{:S(2)}) collective-permute-start(bf16[4,32,1024]{2,1,0:T(8,128)(2,1)S(1)} %pad_maximum_fusion.2.refs_8_), channel_id=1, source_target_pairs={{0,4},{2,6},{4,0},{6,2},{1,5},{3,7},{5,1},{7,3},{8,12},{10,14},{12... | collective-permute-start | bytes 786440 | tf_op jit(solution)/shard_map/ppermute | solution.py:62
  113.1 26.2 %all-to-all-start.2 = ((bf16[4,3,512,128]{3,2,1,0:T(8,128)(2,1)}), bf16[4,3,512,128]{3,2,1,0:T(8,128)(2,1)S(1)}, u32[]{:S(2)}, u32[]{:S(2)}) async-start(bf16[4,3,512,128]{3,2,1,0:T(8,128)(2,1)} %get-tuple-element.76), calls=%async_computation.2 | async-start | bytes 3145728 | tf_op jit(solution)/shard_map/all_to_all | solution.py:308
  139.4 30.0 %all-to-all-start = ((bf16[4,3,512,128]{3,2,1,0:T(8,128)(2,1)}), bf16[4,3,512,128]{3,2,1,0:T(8,128)(2,1)S(1)}, u32[]{:S(2)}, u32[]{:S(2)}) async-start(bf16[4,3,512,128]{3,2,1,0:T(8,128)(2,1)} %copy-done.14), calls=%async_computation | async-start | bytes 3145728 | tf_op jit(solution)/shard_map/all_to_all | solution.py:308
  264.7 46.9 %collective-permute-start.28 = (bf16[4,4,32,4096]{3,2,1,0:T(8,128)(2,1)}, bf16[4,4,32,4096]{3,2,1,0:T(8,128)(2,1)}, u32[]{:S(2)}, u32[]{:S(2)}) collective-permute-start(bf16[4,4,32,4096]{3,2,1,0:T(8,128)(2,1)} %get-tuple-element.85), channel_id=1, source_target_pairs={{0,1},{1,0},{2,3},{3,2},{4,5},{5,4},{6,7},{7,6},{8,9},{9,8},{10,11... | collective-permute-start | bytes 12582920 | tf_op jit(solution)/shard_map/ppermute | solution.py:52
  284.3 42.1 %all-to-all-start.4 = ((bf16[4,512,128]{2,1,0:T(8,128)(2,1)}), bf16[4,512,128]{2,1,0:T(8,128)(2,1)S(1)}, u32[]{:S(2)}, u32[]{:S(2)}) async-start(bf16[4,512,128]{2,1,0:T(8,128)(2,1)} %get-tuple-element.150), calls=%async_computation.4 | async-start | bytes 1048576 | tf_op jit(solution)/shard_map/all_to_all | solution.py:308
  287.8 167.5 %reduce-scatter.2.cloned.1.call-start = ((), (), s32[]{:S(2)}) async-start(), calls=%async_computation.11 | async-start | bytes 4456448 | tf_op jit(solution)/shard_map/reduce_scatter | solution.py:709
  326.5 98.2 %all-to-all-start.6 = ((bf16[4,512,128]{2,1,0:T(8,128)(2,1)}), bf16[4,512,128]{2,1,0:T(8,128)(2,1)}, u32[]{:S(2)}, u32[]{:S(2)}) async-start(bf16[4,512,128]{2,1,0:T(8,128)(2,1)} %get-tuple-element.149), calls=%async_computation.7 | async-start | bytes 1048576 | tf_op jit(solution)/shard_map/all_to_all | solution.py:308
  330.6 59.6 %collective-permute-start.30 = (bf16[4,32,4096]{2,1,0:T(8,128)(2,1)}, bf16[4,32,4096]{2,1,0:T(8,128)(2,1)S(1)}, u32[]{:S(2)}, u32[]{:S(2)}) collective-permute-start(bf16[4,32,4096]{2,1,0:T(8,128)(2,1)} %copy-done.24), channel_id=1, source_target_pairs={{0,8},{8,0},{16,24},{24,16},{1,9},{9,1},{17,25},{25,17},{2,10},{10... | collective-permute-start | bytes 3145736 | tf_op jit(solution)/shard_map/ppermute | solution.py:57
  332.6 57.7 %collective-permute-start.31 = (bf16[4,32,4096]{2,1,0:T(8,128)(2,1)}, bf16[4,32,4096]{2,1,0:T(8,128)(2,1)S(1)}, u32[]{:S(2)}, u32[]{:S(2)}) collective-permute-start(bf16[4,32,4096]{2,1,0:T(8,128)(2,1)} %copy-done.23), channel_id=1, source_target_pairs={{0,16},{8,24},{16,0},{24,8},{1,17},{9,25},{17,1},{25,9},{2,18},{10... | collective-permute-start | bytes 3145736 | tf_op jit(solution)/shard_map/ppermute | solution.py:57
  334.1 85.0 %collective-permute-start.32 = (bf16[4,32,4096]{2,1,0:T(8,128)(2,1)}, bf16[4,32,4096]{2,1,0:T(8,128)(2,1)S(1)}, u32[]{:S(2)}, u32[]{:S(2)}) collective-permute-start(bf16[4,32,4096]{2,1,0:T(8,128)(2,1)} %copy-done.22), channel_id=1, source_target_pairs={{0,24},{8,16},{16,8},{24,0},{1,25},{9,17},{17,9},{25,1},{2,26},{10... | collective-permute-start | bytes 3145736 | tf_op jit(solution)/shard_map/ppermute | solution.py:57
  422.3 31.0 %collective-permute-start.35 = (bf16[32,4096]{1,0:T(8,128)(2,1)}, bf16[32,4096]{1,0:T(8,128)(2,1)}, u32[]{:S(2)}, u32[]{:S(2)}) collective-permute-start(bf16[32,4096]{1,0:T(8,128)(2,1)} %bitcast.37), channel_id=1, source_target_pairs={{0,6},{2,0},{4,2},{6,4},{1,7},{3,1},{5,3},{7,5},{8,14},{10,8},{12,... | collective-permute-start | bytes 786440 | tf_op jit(solution)/shard_map/ppermute | solution.py:62
  424.1 29.2 %collective-permute-start.34 = (bf16[32,4096]{1,0:T(8,128)(2,1)}, bf16[32,4096]{1,0:T(8,128)(2,1)}, u32[]{:S(2)}, u32[]{:S(2)}) collective-permute-start(bf16[32,4096]{1,0:T(8,128)(2,1)} %bitcast.36), channel_id=1, source_target_pairs={{0,4},{2,6},{4,0},{6,2},{1,5},{3,7},{5,1},{7,3},{8,12},{10,14},{12... | collective-permute-start | bytes 786440 | tf_op jit(solution)/shard_map/ppermute | solution.py:62
  424.1 29.2 %collective-permute-start.33 = (bf16[32,4096]{1,0:T(8,128)(2,1)}, bf16[32,4096]{1,0:T(8,128)(2,1)}, u32[]{:S(2)}, u32[]{:S(2)}) collective-permute-start(bf16[32,4096]{1,0:T(8,128)(2,1)} %bitcast.35), channel_id=1, source_target_pairs={{0,2},{2,4},{4,6},{6,0},{1,3},{3,5},{5,7},{7,1},{8,10},{10,12},{12... | collective-permute-start | bytes 786440 | tf_op jit(solution)/shard_map/ppermute | solution.py:62
  424.7 24.4 %all-to-all-start.5 = ((bf16[4,3,512,128]{3,2,1,0:T(8,128)(2,1)}), bf16[4,3,512,128]{3,2,1,0:T(8,128)(2,1)S(1)}, u32[]{:S(2)}, u32[]{:S(2)}) async-start(bf16[4,3,512,128]{3,2,1,0:T(8,128)(2,1)} %copy-done.15), calls=%async_computation.5 | async-start | bytes 3145728 | tf_op jit(solution)/shard_map/all_to_all | solution.py:308
  491.3 25.5 %collective-permute-start.44 = (bf16[4,32,2048]{2,1,0:T(8,128)(2,1)}, bf16[4,32,2048]{2,1,0:T(8,128)(2,1)S(1)}, u32[]{:S(2)}, u32[]{:S(2)}) collective-permute-start(bf16[4,32,2048]{2,1,0:T(8,128)(2,1)} %get-tuple-element.115), channel_id=1, source_target_pairs={{0,16},{8,24},{16,0},{24,8},{1,17},{9,25},{17,1},{25,9},{2,18},{10... | collective-permute-start | bytes 1572872 | tf_op jit(solution)/shard_map/ppermute | solution.py:57
  491.9 25.2 %collective-permute-start.45 = (bf16[4,32,2048]{2,1,0:T(8,128)(2,1)}, bf16[4,32,2048]{2,1,0:T(8,128)(2,1)S(1)}, u32[]{:S(2)}, u32[]{:S(2)}) collective-permute-start(bf16[4,32,2048]{2,1,0:T(8,128)(2,1)} %get-tuple-element.116), channel_id=1, source_target_pairs={{0,24},{8,16},{16,8},{24,0},{1,25},{9,17},{17,9},{25,1},{2,26},{10... | collective-permute-start | bytes 1572872 | tf_op jit(solution)/shard_map/ppermute | solution.py:57
  508.9 29.7 %collective-permute-start.54 = (bf16[32,1024]{1,0:T(8,128)(2,1)}, bf16[32,1024]{1,0:T(8,128)(2,1)}, u32[]{:S(2)}, u32[]{:S(2)}) collective-permute-start(bf16[32,1024]{1,0:T(8,128)(2,1)} %bitcast.66), channel_id=1, source_target_pairs={{0,24},{8,16},{16,8},{24,0},{1,25},{9,17},{17,9},{25,1},{2,26},{10... | collective-permute-start | bytes 196616 | tf_op jit(solution)/shard_map/ppermute | solution.py:57
  510.3 28.3 %collective-permute-start.53 = (bf16[32,1024]{1,0:T(8,128)(2,1)}, bf16[32,1024]{1,0:T(8,128)(2,1)}, u32[]{:S(2)}, u32[]{:S(2)}) collective-permute-start(bf16[32,1024]{1,0:T(8,128)(2,1)} %bitcast.65), channel_id=1, source_target_pairs={{0,16},{8,24},{16,0},{24,8},{1,17},{9,25},{17,1},{25,9},{2,18},{10... | collective-permute-start | bytes 196616 | tf_op jit(solution)/shard_map/ppermute | solution.py:57
  511.8 26.8 %collective-permute-start.52 = (bf16[32,1024]{1,0:T(8,128)(2,1)S(1)}, bf16[32,1024]{1,0:T(8,128)(2,1)}, u32[]{:S(2)}, u32[]{:S(2)}) collective-permute-start(bf16[32,1024]{1,0:T(8,128)(2,1)S(1)} %bitcast.229), channel_id=1, source_target_pairs={{0,8},{8,0},{16,24},{24,16},{1,9},{9,1},{17,25},{25,17},{2,10},{10... | collective-permute-start | bytes 196616 | tf_op jit(solution)/shard_map/ppermute | solution.py:57
  (117 other events, 1181.5 us)
Sparse Core Ops, SparseCore 0:
  11.0 104.0 all-gather.2
  118.1 95.2 all-gather.4
  311.0 98.0 reduce-scatter.1

commit v3 on v2

--- a/solution.py
+++ b/solution.py
@@ -24,8 +24,13 @@
     return centered * lax.rsqrt(variance + epsilon) * scaling + shifting
 
 
-def gelu_tanh(values):
-    return jax.nn.gelu(values, approximate=True)
+def gelu_both(values):
+    slope = math.sqrt(2.0 / math.pi)
+    square = values * values
+    curve = jnp.tanh(slope * values * (1.0 + 0.044715 * square))
+    half = 0.5 * (1.0 + curve)
+    inner = slope * (1.0 + 3 * 0.044715 * square)
+    return values * half, half + 0.5 * values * (1.0 - curve * curve) * inner
 
 
 def matmul(left, right):
@@ -217,81 +222,71 @@
         name="joint_back",
         out_shape=jax.ShapeDtypeStruct((tokens, depth), f32),
         compiler_params=pltpu.CompilerParams(vmem_limit_bytes=24 << 20),
-        cost_estimate=pl.CostEstimate(
-            flops=2 * tokens * weight.size,
-            bytes_accessed=4 * weight.size + 4 * tokens * depth,
-            transcendentals=0,
-        ),
+        cost_estimate=pl.CostEstimate(flops=0, bytes_accessed=depth, transcendentals=0),
     )(*grads, weight)
 
 
-def summed(terms, order, axis=0, cut=None):
-    _, _, rows, columns = terms[0].shape
-    n, m = terms[0].shape[axis], terms[0].shape[1 - axis]
-    first, last = cut or (0, columns // 1024)
-    count = len(terms)
+def summed(terms, order, extra=()):
+    n, m, rows, columns = terms[0].shape
+    more = extra[0].shape[3] if extra else 0
+    count, both = len(terms), len(terms) + len(extra)
 
     def kernel(order_ref, *refs):
         for k in range(n):
-            result = refs[k * count][0, 0].astype(f32)
-            for j in range(1, count):
-                result = result + refs[k * count + j][0, 0].astype(f32)
-            refs[n * count + k][0] = result.astype(bf16)
-
-    def block(k):
-        def index(i, c, order):
-            return (order[k], i, 0, first + c) if axis == 0 else (i, order[k], 0, first + c)
-
-        return pl.BlockSpec((1, 1, rows, 1024), index)
-
-    size = 2 * n * m * rows * (last - first) * 1024
+            ins, out = refs[k * both : (k + 1) * both], refs[n * both + k]
+            for group, start, size in ((ins[:count], 0, columns), (ins[count:], columns, more)):
+                if size:
+                    result = group[0][0, 0].astype(f32)
+                    for ref in group[1:]:
+                        result = result + ref[0, 0].astype(f32)
+                    out[0, :, start : start + size] = result.astype(bf16)
+
+    def block(k, size):
+        return pl.BlockSpec((1, 1, rows, size), lambda i, order: (order[k], i, 0, 0))
+
+    in_specs = []
+    for k in range(n):
+        in_specs += [block(k, columns)] * count + [block(k, more)] * len(extra)
+    total = columns + more
     return pl.pallas_call(
         kernel,
         name="summed",
         grid_spec=pltpu.PrefetchScalarGridSpec(
             num_scalar_prefetch=1,
-            grid=(m, last - first),
-            in_specs=[block(k) for k in range(n) for _ in range(count)],
-            out_specs=[pl.BlockSpec((1, rows, 1024), lambda i, c, order: (i, 0, c))] * n,
-        ),
-        out_shape=[jax.ShapeDtypeStruct((m, rows, (last - first) * 1024), bf16)] * n,
+            grid=(m,),
+            in_specs=in_specs,
+            out_specs=[pl.BlockSpec((1, rows, total), lambda i, order: (i, 0, 0))] * n,
+        ),
+        out_shape=[jax.ShapeDtypeStruct((m, rows, total), bf16)] * n,
         compiler_params=pltpu.CompilerParams(vmem_limit_bytes=32 << 20),
         cost_estimate=pl.CostEstimate(
-            flops=0, bytes_accessed=(count + 1) * size, transcendentals=0
-        ),
-    )(order.astype(jnp.int32), *([*terms] * n))
-
-
-def first_step(mine, other, along, cut=None):
-    ns, nz = sizes()
+            flops=0, bytes_accessed=(count + 1) * 2 * n * m * rows * total, transcendentals=0
+        ),
+    )(order.astype(jnp.int32), *([*terms, *extra] * n))
+
+
+def seq_step(mine, other, extra=()):
+    ns = sizes()[0]
     if mine.shape[2] % 16:
-        if cut:
-            mine, other = (v[..., cut[0] * 1024 : cut[1] * 1024] for v in (mine, other))
-        return [(mine.astype(f32) + other.astype(f32)).astype(bf16)]
-    seq, z, _ = places()
-    if along == "seq":
-        parts = summed([mine, other], seq ^ jnp.arange(ns), 0, cut)
-        return [parts[0]] + [to_seq(parts[by], by) for by in range(1, ns)]
-    parts = summed([mine, other], (z + jnp.arange(nz)) % nz, 1, cut)
-    return [parts[0]] + [to_z(parts[by], by) for by in range(1, nz)]
-
-
-def second_sums(terms, along):
-    ns, nz = sizes()
+        chip = mine.astype(f32) + other.astype(f32)
+        if extra:
+            chip = jnp.concatenate([chip, extra[0].astype(f32) + extra[1].astype(f32)], 3)
+        return [chip.astype(bf16)]
+    parts = summed([mine, other], places()[0] ^ jnp.arange(ns), extra)
+    return [parts[0]] + [to_seq(parts[by], by) for by in range(1, ns)]
+
+
+def column_sums(terms):
     if len(terms) == 1:
         return terms
-    seq, z, _ = places()
-    order = (z + jnp.arange(nz)) % nz if along == "seq" else seq ^ jnp.arange(ns)
-    return summed([term[:, None] for term in terms], order)
-
-
-def second_step(parts, along):
-    ns, nz = sizes()
+    nz = sizes()[1]
+    return summed([term[:, None] for term in terms], (places()[1] + jnp.arange(nz)) % nz)
+
+
+def z_step(parts):
     if len(parts) == 1:
         return parts
-    if along == "seq":
-        return [parts[0][0]] + [to_z(parts[by][0], by) for by in range(1, nz)]
-    return [parts[0][0]] + [to_seq(parts[by][0], by) for by in range(1, ns)]
+    return [parts[0][0]] + [to_z(parts[by][0], by) for by in range(1, sizes()[1])]
 
 
 def last_step(terms):
@@ -339,7 +334,7 @@
         mixture = mixture.reshape(tokens, 3, ns, pairs, 128).transpose(3, 2, 1, 0, 4)
         return full, last, [mixture[pair] for pair in range(pairs)]
     one = jnp.stack(along_z(shard))
-    two = jnp.stack(along_seq(later))
+    two = after(jnp.stack(along_seq(later)), one)
     ones = with_core(along_seq(one))
     twos = with_core(along_z(two))
     owners = [owner_seq_outer(nz)] * len(ones) + [owner_z_outer(nz)] * len(twos)
@@ -693,7 +688,8 @@
     second, second_pull = jax.vjp(layer_norm, middle, gain_two, shift_two)
     second_low = second.astype(bf16)
     hidden = matmul(second_low, upward_full) + upward_add
-    active, gelu_pull = jax.vjp(gelu_tanh, hidden)
+    active, derivative = gelu_both(hidden)
+    derivative = derivative.astype(bf16)
     active_low = active.astype(bf16)
     result = matmul(active_low, downward_full) + downward_add
     output = (middle + result).astype(bf16).reshape(members, length, features)
@@ -703,7 +699,8 @@
     downward_mine, downward_other = halves(active_low, grad_result)
     downwardbias_grad = jnp.sum(grad_result_full, 0)
     downward_other = to_core(downward_other)
-    (grad_hidden,) = gelu_pull(right_transposed(after(grad_result, downward_mine), downward_full))
+    grad_active = right_transposed(after(grad_result, downward_mine), downward_full)
+    grad_hidden = grad_active * derivative.astype(f32)
     grad_hidden_low = grad_hidden.astype(bf16)
     downward_chip = (downward_mine.astype(f32) + downward_other.astype(f32)).astype(bf16)
     downward_sum = lax.psum_scatter(
@@ -723,31 +720,22 @@
     grad_attended = [over_seq(grad_attended[pair]) for pair in range(pairs)]
     projection_mine, projection_other = halves(attended_low, grad_branch)
     projection_other = to_core(projection_other)
-    upward_terms = first_step(upward_mine, upward_other, "seq")
-    projection_terms = first_step(projection_mine, projection_other, "seq")
-    grad_attended[0] = after(grad_attended[0], upward_terms[0], projection_terms[0])
+    upward_terms = seq_step(upward_mine, upward_other, (projection_mine, projection_other))
+    grad_attended[0] = after(grad_attended[0], upward_terms[0])
+    upward_parts = column_sums(upward_terms)
     grad_qkv = []
     for pair in range(pairs):
-        if pair == pairs - 1:
-            upward_parts = second_sums(upward_terms, "seq")
-            projection_parts = second_sums(projection_terms, "seq")
-            grad_attended[pair] = after(grad_attended[pair], upward_parts[0], projection_parts[0])
         low, full, logs = forward[pair]
         grad = attention_backward(qkv[pair], grad_attended[pair], full, logs, order, slopes[pair])
+        if pair == pairs - 1:
+            grad = after(grad, upward_parts[0], downward_sum)
         grad_qkv.append(over_seq(grad))
-    upward_sum = last_step(second_step(upward_parts, "seq"))
-    projection_sum = last_step(second_step(projection_parts, "seq"))
-    grad_qkv[0] = after(grad_qkv[0], upward_sum, projection_sum, downward_sum, output)
+    upward_sum = last_step(z_step(upward_parts))
+    upward_sum, projection_sum = upward_sum[:, :-features], upward_sum[:, -features:]
+    grad_qkv[0] = after(grad_qkv[0], upward_sum, output)
     joint_mine, joint_other = joint_halves(normed_low, grad_qkv)
-    joint_other = to_core(joint_other)
-    joint_terms = first_step(joint_mine, joint_other, "seq", (0, 2))
-    joint_more = first_step(joint_mine, joint_other, "z", (2, 3))
-    joint_parts = second_sums(joint_terms, "seq")
-    more_parts = second_sums(joint_more, "z")
-    joint_terms = second_step(joint_parts, "seq")
-    joint_more = second_step(more_parts, "z")
-    joint_sum = jnp.concatenate([last_step(joint_terms), last_step(joint_more)], 1)
-    grad_qkv[0] = after(grad_qkv[0], joint_parts[0], more_parts[0])
+    joint_terms = seq_step(joint_mine, to_core(joint_other))
+    grad_qkv[0] = after(grad_qkv[0], joint_terms[0])
     mixture_sums = jnp.stack([jnp.sum(grad.astype(f32), 2) for grad in grad_qkv])
     mixture_sums = mixture_sums.transpose(2, 1, 0, 3).reshape(-1)
     grad_normed = joint_back(grad_qkv, joint_full)
@@ -767,6 +755,8 @@
     )
     packed = jnp.concatenate([g.reshape(devices, -1) for g in grads], 1)
     packed = scattered_small(packed)
+    joint_terms[0] = after(joint_terms[0], packed, input_grad)
+    joint_sum = last_step(z_step(column_sums(joint_terms)))
     sums, first = [], 0
     for one in small:
         sums.append(packed[first : first + one.shape[0]])

time: 583 us -> 549 us (0.942)
  starting transfers between devices: 95.1 us -> 73.8 us
  Pallas kernels: 123 us -> 115 us
    ppermute x24 -> x18, starting transfers between devices: 31.5 us -> 16.5 us  [to_z(): lax.ppermute(value, 'z', [(i, (i + by) % count) for i in range(count)])]
    pallas_call x8 -> x4, Pallas kernels: 24.7 us -> 13.3 us  [summed(): pl.pallas_call(kernel, name='summed', grid_spec=pltpu.PrefetchScalarGridS...]
    concatenate x9, local copies, waits for them, and re-layouts: 9.88 us -> 0.91 us  [body(): packed = jnp.concatenate([g.reshape(devices, -1) for g in grads], 1)]
    ppermute x24 -> x18, waiting for transfers between devices: 92.8 us -> 99.9 us  [to_seq(): return lax.ppermute(value, 'seq', [(i, i ^ by) for i in range(count)])]
    ppermute x24 -> x18, starting transfers between devices: 29 us -> 22.1 us  [to_seq(): return lax.ppermute(value, 'seq', [(i, i ^ by) for i in range(count)])]
    ppermute x24 -> x18, waiting for transfers between devices: 56 us -> 57.1 us  [to_z(): lax.ppermute(value, 'z', [(i, (i + by) % count) for i in range(count)])]
    unnamed x137 -> x143, local copies, waits for them, and re-layouts: 25.6 us -> 26.5 us
  transfers between devices with their start and end apart: 73 -> 61, of which waited for: 27 -> 25; matrix products, arithmetic and copies ran while one was open for 15% -> 16% of each run, Pallas kernels for 19% -> 17%
where the time goes in v3:
time: 549 us; the launch traced here: 539 us
  waiting for transfers between devices  214 us (39%)
  Pallas kernels  115 us (21%)
  starting transfers between devices  73.8 us (13%)
  matrix products  50.6 us (9%)
  local copies, waits for them, and re-layouts  44.7 us (8%)
  other arithmetic  26 us (5%)
  between operations  15 us (3%)
    ppermute x18, waiting for transfers between devices, to_seq(): return lax.ppermute(value, 'seq', [(i, i ^ by) for i in range(count)])  99.9 us
    ppermute x18, waiting for transfers between devices, to_z(): lax.ppermute(value, 'z', [(i, (i + by) % count) for i in range(count)])  57.1 us
    all_to_all x8, waiting for transfers between devices, over_seq(): return lax.all_to_all(value, 'seq', 0, 0, tiled=True)  47.9 us
    pallas_call x2, Pallas kernels, attention_backward(): pl.pallas_call(kernel, name='attention_backward', grid_spec=grid_spec, ou...  35.2 us
    all_to_all x8, starting transfers between devices, over_seq(): return lax.all_to_all(value, 'seq', 0, 0, tiled=True)  32.4 us
    pallas_call x2, Pallas kernels, attention_forward(): pl.pallas_call(kernel, name='attention_forward', grid_spec=grid_spec, out...  26.8 us
    unnamed x143, local copies, waits for them, and re-layouts  26.5 us
    dot_general x4, matrix products, matmul(): return jnp.dot(left, right, preferred_element_type=f32)  26 us
  transfers between devices with their start and end apart: 61, of which 25 were waited for; matrix products, arithmetic and copies ran while one was open for 16% of the time, Pallas kernels for 17%

profile of v3, /device:TPU:0, one launch (start us, length us, event | category | flops | bytes accessed | tf_op | source)
XLA Modules:
  0.0 538.9 jit_solution(1618619247159408003)
XLA Ops:
  34.3 10.4 %collective-permute-done.1 = bf16[32,3072]{1,0:T(8,128)(2,1)S(1)} collective-permute-done((bf16[32,3072]{1,0:T(8,128)(2,1)}, bf16[32,3072]{1,0:T(8,128)(2,1)S(1)}, u32[]{:S(2)}, u32[]{:S(2)}) %collective-permute-start.1) | collective-permute-done | bytes 196640 | tf_op jit(solution)/shard_map/ppermute | solution.py:67
  50.1 14.5 %collective-permute-done.14.refs_10_ = bf16[4,32,1024]{2,1,0:T(8,128)(2,1)} collective-permute-done((bf16[4,32,1024]{2,1,0:T(8,128)(2,1)S(1)}, bf16[4,32,1024]{2,1,0:T(8,128)(2,1)}, u32[]{:S(2)}, u32[]{:S(2)}) %collective-permute-start.14) | collective-permute-done | bytes 262176 | tf_op jit(solution)/shard_map/ppermute | solution.py:67
  64.6 14.9 %collective-permute-done.16.refs_12_ = bf16[4,32,1024]{2,1,0:T(8,128)(2,1)S(1)} collective-permute-done((bf16[4,32,1024]{2,1,0:T(8,128)(2,1)S(1)}, bf16[4,32,1024]{2,1,0:T(8,128)(2,1)S(1)}, u32[]{:S(2)}, u32[]{:S(2)}) %collective-permute-start.16) | collective-permute-done | bytes 262176 | tf_op jit(solution)/shard_map/ppermute | solution.py:67
  81.7 7.4 %collective-permute-done.8.refs_6_ = bf16[4,32,3072]{2,1,0:T(8,128)(2,1)S(1)} collective-permute-done((bf16[4,32,3072]{2,1,0:T(8,128)(2,1)S(1)}, bf16[4,32,3072]{2,1,0:T(8,128)(2,1)S(1)}, u32[]{:S(2)}, u32[]{:S(2)}) %collective-permute-start.8) | collective-permute-done | bytes 786464 | tf_op jit(solution)/shard_map/ppermute | solution.py:62
  94.0 12.5 %joint_product.1 = (bf16[32,32,3072]{2,1,0:T(8,128)(2,1)S(1)}, bf16[32,32,1024]{2,1,0:T(8,128)(2,1)S(1)}, bf16[4,3,512,128]{3,2,1,0:T(8,128)(2,1)S(1)}, bf16[4,3,512,128]{3,2,1,0:T(8,128)(2,1)}) custom-call(s32[3]{0:T(128)S(1)} %pad_add_fusion.place, bf16[4,32,3072]{2,1,0:T(8,128)(2,1)S(1)} %pad_maximum_fusion.refs_0_, ...), custom_call_target="tpu_custom_call" | custom-call | flops 3221225472 | bytes 18874368 | tf_op jit(solution)/shard_map/joint_product/pallas_call | solution.py:383
  116.3 21.0 %all-to-all-done.2.q_ref.kv_ref.qkv_ref = bf16[4,3,512,128]{3,2,1,0:T(8,128)(2,1)S(1)} async-done(((bf16[4,3,512,128]{3,2,1,0:T(8,128)(2,1)}), bf16[4,3,512,128]{3,2,1,0:T(8,128)(2,1)S(1)}, u32[]{:S(2)}, u32[]{:S(2)}) %all-to-all-start.2) | async-done | bytes 1572896 | tf_op jit(solution)/shard_map/all_to_all | solution.py:303
  140.9 13.1 %attention_forward.3 = (bf16[4,512,128]{2,1,0:T(8,128)(2,1)S(1)}, f32[4,512,128]{2,1,0:T(8,128)S(1)}, f32[1,4,8,512]{3,2,1,0:T(8,128)S(1)}) custom-call(s32[4]{0:T(128)S(1)} %get-tuple-element.59.order_ref, f32[2]{0:T(128)S(1)} %get-tuple-element.145.slope_ref, bf16[4,3,512,128]{3,2,1,0:T(8,128)(2,1)S(1)} %all-to-all-done.2.q_ref.kv_ref.qkv_ref, ...), custom_call_target="tpu_custom_call" | custom-call | flops 32212254720 | bytes 3145728 | tf_op jit(solution)/shard_map/attention_forward/pallas_call | solution.py:488
  155.8 11.9 %all-to-all-done.q_ref.kv_ref.qkv_ref = bf16[4,3,512,128]{3,2,1,0:T(8,128)(2,1)S(1)} async-done(((bf16[4,3,512,128]{3,2,1,0:T(8,128)(2,1)}), bf16[4,3,512,128]{3,2,1,0:T(8,128)(2,1)S(1)}, u32[]{:S(2)}, u32[]{:S(2)}) %all-to-all-start) | async-done | bytes 1572896 | tf_op jit(solution)/shard_map/all_to_all | solution.py:303
  171.2 13.7 %attention_forward.2 = (bf16[4,512,128]{2,1,0:T(8,128)(2,1)}, f32[4,512,128]{2,1,0:T(8,128)S(1)}, f32[1,4,8,512]{3,2,1,0:T(8,128)S(1)}) custom-call(s32[4]{0:T(128)S(1)} %get-tuple-element.59.order_ref, f32[2]{0:T(128)S(1)} %get-tuple-element.144.slope_ref, bf16[4,3,512,128]{3,2,1,0:T(8,128)(2,1)S(1)} %all-to-all-done.q_ref.kv_ref.qkv_ref, ...), custom_call_target="tpu_custom_call" | custom-call | flops 32212254720 | bytes 3145728 | tf_op jit(solution)/shard_map/attention_forward/pallas_call | solution.py:488
  191.2 8.2 %all-to-all-done.1 = bf16[4,512,128]{2,1,0:T(8,128)(2,1)S(1)} async-done(((bf16[4,512,128]{2,1,0:T(8,128)(2,1)}), bf16[4,512,128]{2,1,0:T(8,128)(2,1)S(1)}, u32[]{:S(2)}, u32[]{:S(2)}) %all-to-all-start.1) | async-done | bytes 524320 | tf_op jit(solution)/shard_map/all_to_all | solution.py:303
  207.7 12.4 %multiply_convert_fusion.1 = (bf16[512,4096]{1,0:T(8,128)(2,1)S(1)}, f32[512,4096]{1,0:T(8,128)}) fusion(f32[4096]{0:T(1024)S(1)} %slice_bitcast_fusion.2, bf16[512,1024]{1,0:T(8,128)(2,1)S(1)} %add_convert_fusion.4.left_ref, bf16[1024,4096]{1,0:T(8,128)(2,1)} %all-gather.3.cloned.1.call-done), kind=kOutput, calls=%fused_computation.4 | convolution fusion | flops 4315938816 | bytes 22036480 | tf_op jit(solution)/shard_map/dot_general | solution.py:37
  220.1 6.5 %halves.3 = (bf16[4,4,128,1024]{3,2,1,0:T(8,128)(2,1)S(1)}, bf16[4,4,128,1024]{3,2,1,0:T(8,128)(2,1)}) custom-call(s32[1]{0:T(128)} %bitcast.4.core_ref, bf16[512,4096]{1,0:T(8,128)(2,1)S(1)} %get-tuple-element.148.left_ref, bf16[512,1024]{1,0:T(8,128)(2,1)S(1)} %bitcast.162), custom_call_target="tpu_custom_call" | custom-call | flops 4294967296 | bytes 13631488 | tf_op jit(solution)/shard_map/halves/pallas_call | solution.py:136
  228.6 13.3 %convert_reduce_fusion = (f32[4096]{0:T(1024)}, bf16[512,4096]{1,0:T(8,128)(2,1)S(1)}) fusion(f32[512,4096]{1,0:T(8,128)} %get-tuple-element.149, f32[4096]{0:T(1024)S(1)} %slice_bitcast_fusion.2, bf16[512,1024]{1,0:T(8,128)(2,1)S(1)} %bitcast.163, bf16[4096,1024]{1,0:T(8,128)(2,1)} %all-gather.5.cloned.1.call-done), kind=kOutput, calls=%fused_computation | convolution fusion | flops 4343197696 | bytes 22052864 | tf_op jit(solution)/shard_map/dot_general | solution.py:45
  248.2 6.4 %halves.4 = (bf16[4,4,32,4096]{3,2,1,0:T(8,128)(2,1)S(1)}, bf16[4,4,32,4096]{3,2,1,0:T(8,128)(2,1)}) custom-call(s32[1]{0:T(128)} %bitcast.4.core_ref, bf16[512,1024]{1,0:T(8,128)(2,1)S(1)} %add_convert_fusion.4.left_ref, bf16[512,4096]{1,0:T(8,128)(2,1)S(1)} %get-tuple-element.71.right_ref), custom_call_target="tpu_custom_call" | custom-call | flops 4294967296 | bytes 13631488 | tf_op jit(solution)/shard_map/halves/pallas_call | solution.py:136
  255.2 9.1 %multiply_reduce_fusion = (f32[1024]{0:T(1024)}, f32[512]{0:T(512)S(1)}, f32[1024]{0:T(1024)}, f32[512,1024]{1,0:T(8,128)S(1)}) fusion(f32[512,1024]{1,0:T(8,128)S(1)} %copy-done.44, f32[512]{0:T(512)S(1)} %fusion.26, f32[512]{0:T(512)S(1)} %broadcast_multiply_fusion, f32[1024]{0:T(1024)S(1)} %mul.189, ...), kind=kOutput, calls=%fused_computation.29 | convolution fusion | flops 4299159040 | bytes 16795648 | tf_op jit(solution)/shard_map/dot_general | solution.py:45
  303.3 18.1 %attention_backward.2 = bf16[4,3,512,128]{3,2,1,0:T(8,128)(2,1)S(1)} custom-call(s32[4]{0:T(128)S(1)} %get-tuple-element.59.order_ref, f32[2]{0:T(128)S(1)} %get-tuple-element.144.slope_ref, bf16[4,3,512,128]{3,2,1,0:T(8,128)(2,1)S(1)} %copy-done.15, bf16[4,512,128]{2,1,0:T(8,128)(2,1)} %all-to-all-done.4.grad_ref, f32[4,512,128]{2,1,0:T(8,128)S(1)} %copy-done.39, ...), custom_call_target="tpu_custom_call" | custom-call | flops 80530636800 | bytes 4718592 | tf_op jit(solution)/shard_map/attention_backward/pallas_call | solution.py:592
  329.5 17.1 %attention_backward.3 = bf16[4,3,512,128]{3,2,1,0:T(8,128)(2,1)S(1)} custom-call(s32[4]{0:T(128)S(1)} %get-tuple-element.59.order_ref, f32[2]{0:T(128)S(1)} %copy-done.23, bf16[4,3,512,128]{3,2,1,0:T(8,128)(2,1)S(1)} %copy-done.13, bf16[4,512,128]{2,1,0:T(8,128)(2,1)S(1)} %all-to-all-done.6.grad_ref, f32[4,512,128]{2,1,0:T(8,128)S(1)} %copy-done.37, ...), custom_call_target="tpu_custom_call" | custom-call | flops 80530636800 | bytes 4718592 | tf_op jit(solution)/shard_map/attention_backward/pallas_call | solution.py:592
  346.6 21.6 %collective-permute-done.30 = bf16[4,32,5120]{2,1,0:T(8,128)(2,1)} collective-permute-done((bf16[4,32,5120]{2,1,0:T(8,128)(2,1)}, bf16[4,32,5120]{2,1,0:T(8,128)(2,1)}, u32[]{:S(2)}, u32[]{:S(2)}) %collective-permute-start.30) | collective-permute-done | bytes 1310752 | tf_op jit(solution)/shard_map/ppermute | solution.py:62
  368.2 42.8 %collective-permute-done.31 = bf16[4,32,5120]{2,1,0:T(8,128)(2,1)} collective-permute-done((bf16[4,32,5120]{2,1,0:T(8,128)(2,1)}, bf16[4,32,5120]{2,1,0:T(8,128)(2,1)}, u32[]{:S(2)}, u32[]{:S(2)}) %collective-permute-start.31) | collective-permute-done | bytes 1310752 | tf_op jit(solution)/shard_map/ppermute | solution.py:62
  423.9 10.8 %fusion.14 = bf16[1,512,1024]{2,1,0:T(8,128)(2,1)} fusion(f32[512,1024]{1,0:T(8,128)} %copy-done.43, bf16[512,4096]{1,0:T(8,128)(2,1)} %copy-done.35, bf16[4096,1024]{1,0:T(8,128)(2,1)} %all-gather.5.cloned.1.call-done, f32[1024]{0:T(1024)S(1)} %copy-done.67), kind=kOutput, calls=%fused_computation.37 | convolution fusion | flops 4296540160 | bytes 15732736 | tf_op jit(solution)/shard_map/dot_general | solution.py:37
  445.7 6.6 %joint_halves.1 = (bf16[4,4,32,3072]{3,2,1,0:T(8,128)(2,1)S(1)}, bf16[4,4,32,3072]{3,2,1,0:T(8,128)(2,1)}) custom-call(s32[1]{0:T(128)} %bitcast.4.core_ref, bf16[512,1024]{1,0:T(8,128)(2,1)S(1)} %copy-done.20, bf16[4,3,512,128]{3,2,1,0:T(8,128)(2,1)S(1)} %copy-done.3, bf16[4,3,512,128]{3,2,1,0:T(8,128)(2,1)} %all-to-all-done.7.refs_1_), custom_call_target="tpu_custom_call" | custom-call | flops 3221225472 | bytes 10485760 | tf_op jit(solution)/shard_map/joint_halves/pallas_call | solution.py:185
  490.9 7.5 %collective-permute-done.44 = bf16[4,32,3072]{2,1,0:T(8,128)(2,1)S(1)} collective-permute-done((bf16[4,32,3072]{2,1,0:T(8,128)(2,1)}, bf16[4,32,3072]{2,1,0:T(8,128)(2,1)S(1)}, u32[]{:S(2)}, u32[]{:S(2)}) %collective-permute-start.44) | collective-permute-done | bytes 786464 | tf_op jit(solution)/shard_map/ppermute | solution.py:62
  498.4 16.3 %collective-permute-done.45 = bf16[4,32,3072]{2,1,0:T(8,128)(2,1)S(1)} collective-permute-done((bf16[4,32,3072]{2,1,0:T(8,128)(2,1)}, bf16[4,32,3072]{2,1,0:T(8,128)(2,1)S(1)}, u32[]{:S(2)}, u32[]{:S(2)}) %collective-permute-start.45) | collective-permute-done | bytes 786464 | tf_op jit(solution)/shard_map/ppermute | solution.py:62
  524.4 6.9 %collective-permute-done.48 = bf16[32,3072]{1,0:T(8,128)(2,1)S(1)} collective-permute-done((bf16[32,3072]{1,0:T(8,128)(2,1)S(1)}, bf16[32,3072]{1,0:T(8,128)(2,1)S(1)}, u32[]{:S(2)}, u32[]{:S(2)}) %collective-permute-start.48) | collective-permute-done | bytes 196640 | tf_op jit(solution)/shard_map/ppermute | solution.py:67
  (353 shorter events, 200.9 us)
Async XLA Ops:
  7.2 200.5 %all-gather.3.cloned.1.call-start = ((), (), s32[]{:S(2)}) async-start(), calls=%async_computation.9 | async-start | bytes 8650752 | tf_op jit(solution)/shard_map/all_gather | solution.py:665
  7.9 220.6 %all-gather.5.cloned.1.call-start = ((), (), s32[]{:S(2)}) async-start(), calls=%async_computation.10 | async-start | bytes 8650752 | tf_op jit(solution)/shard_map/all_gather | solution.py:666
  15.8 18.5 %collective-permute-start.2 = (bf16[32,3072]{1,0:T(8,128)(2,1)}, bf16[32,3072]{1,0:T(8,128)(2,1)S(1)}, u32[]{:S(2)}, u32[]{:S(2)}) collective-permute-start(bf16[32,3072]{1,0:T(8,128)(2,1)} %param.19), channel_id=1, source_target_pairs={{0,6},{2,0},{4,2},{6,4},{1,7},{3,1},{5,3},{7,5},{8,14},{10,8},{12,... | collective-permute-start | bytes 589832 | tf_op jit(solution)/shard_map/ppermute | solution.py:67
  44.8 36.3 %collective-permute-start.4 = (bf16[4,32,3072]{2,1,0:T(8,128)(2,1)S(1)}, bf16[4,32,3072]{2,1,0:T(8,128)(2,1)S(1)}, u32[]{:S(2)}, u32[]{:S(2)}) collective-permute-start(bf16[4,32,3072]{2,1,0:T(8,128)(2,1)S(1)} %pad_maximum_fusion.refs_0_), channel_id=1, source_target_pairs={{0,8},{8,0},{16,24},{24,16},{1,9},{9,1},{17,25},{25,17},{2,10},{10... | collective-permute-start | bytes 2359304 | tf_op jit(solution)/shard_map/ppermute | solution.py:62
  46.2 35.4 %collective-permute-start.6 = (bf16[4,32,3072]{2,1,0:T(8,128)(2,1)S(1)}, bf16[4,32,3072]{2,1,0:T(8,128)(2,1)S(1)}, u32[]{:S(2)}, u32[]{:S(2)}) collective-permute-start(bf16[4,32,3072]{2,1,0:T(8,128)(2,1)S(1)} %pad_maximum_fusion.refs_0_), channel_id=1, source_target_pairs={{0,16},{8,24},{16,0},{24,8},{1,17},{9,25},{17,1},{25,9},{2,18},{10... | collective-permute-start | bytes 2359304 | tf_op jit(solution)/shard_map/ppermute | solution.py:62
  47.0 42.2 %collective-permute-start.8 = (bf16[4,32,3072]{2,1,0:T(8,128)(2,1)S(1)}, bf16[4,32,3072]{2,1,0:T(8,128)(2,1)S(1)}, u32[]{:S(2)}, u32[]{:S(2)}) collective-permute-start(bf16[4,32,3072]{2,1,0:T(8,128)(2,1)S(1)} %pad_maximum_fusion.refs_0_), channel_id=1, source_target_pairs={{0,24},{8,16},{16,8},{24,0},{1,25},{9,17},{17,9},{25,1},{2,26},{10... | collective-permute-start | bytes 2359304 | tf_op jit(solution)/shard_map/ppermute | solution.py:62
  50.1 29.4 %collective-permute-start.16 = (bf16[4,32,1024]{2,1,0:T(8,128)(2,1)S(1)}, bf16[4,32,1024]{2,1,0:T(8,128)(2,1)S(1)}, u32[]{:S(2)}, u32[]{:S(2)}) collective-permute-start(bf16[4,32,1024]{2,1,0:T(8,128)(2,1)S(1)} %pad_maximum_fusion.1.refs_8_), channel_id=1, source_target_pairs={{0,4},{2,6},{4,0},{6,2},{1,5},{3,7},{5,1},{7,3},{8,12},{10,14},{12... | collective-permute-start | bytes 786440 | tf_op jit(solution)/shard_map/ppermute | solution.py:67
  111.7 25.6 %all-to-all-start.2 = ((bf16[4,3,512,128]{3,2,1,0:T(8,128)(2,1)}), bf16[4,3,512,128]{3,2,1,0:T(8,128)(2,1)S(1)}, u32[]{:S(2)}, u32[]{:S(2)}) async-start(bf16[4,3,512,128]{3,2,1,0:T(8,128)(2,1)} %get-tuple-element.63), calls=%async_computation.2 | async-start | bytes 3145728 | tf_op jit(solution)/shard_map/all_to_all | solution.py:303
  137.3 30.3 %all-to-all-start = ((bf16[4,3,512,128]{3,2,1,0:T(8,128)(2,1)}), bf16[4,3,512,128]{3,2,1,0:T(8,128)(2,1)S(1)}, u32[]{:S(2)}, u32[]{:S(2)}) async-start(bf16[4,3,512,128]{3,2,1,0:T(8,128)(2,1)} %copy-done.17), calls=%async_computation | async-start | bytes 3145728 | tf_op jit(solution)/shard_map/all_to_all | solution.py:303
  167.7 18.2 %all-to-all-start.3 = ((bf16[4,512,128]{2,1,0:T(8,128)(2,1)}), bf16[4,512,128]{2,1,0:T(8,128)(2,1)S(1)}, u32[]{:S(2)}, u32[]{:S(2)}) async-start(bf16[4,512,128]{2,1,0:T(8,128)(2,1)} %copy-done.21), calls=%async_computation.3 | async-start | bytes 1048576 | tf_op jit(solution)/shard_map/all_to_all | solution.py:303
  254.7 28.3 %collective-permute-start.28 = (bf16[4,4,32,4096]{3,2,1,0:T(8,128)(2,1)}, bf16[4,4,32,4096]{3,2,1,0:T(8,128)(2,1)}, u32[]{:S(2)}, u32[]{:S(2)}) collective-permute-start(bf16[4,4,32,4096]{3,2,1,0:T(8,128)(2,1)} %get-tuple-element.72), channel_id=1, source_target_pairs={{0,1},{1,0},{2,3},{3,2},{4,5},{5,4},{6,7},{7,6},{8,9},{9,8},{10,11... | collective-permute-start | bytes 12582920 | tf_op jit(solution)/shard_map/ppermute | solution.py:57
  282.2 134.7 %reduce-scatter.2.cloned.1.call-start = ((), (), s32[]{:S(2)}) async-start(), calls=%async_computation.11 | async-start | bytes 4456448 | tf_op jit(solution)/shard_map/reduce_scatter | solution.py:706
  292.5 30.0 %all-to-all-start.6 = ((bf16[4,512,128]{2,1,0:T(8,128)(2,1)}), bf16[4,512,128]{2,1,0:T(8,128)(2,1)S(1)}, u32[]{:S(2)}, u32[]{:S(2)}) async-start(bf16[4,512,128]{2,1,0:T(8,128)(2,1)} %get-tuple-element.119), calls=%async_computation.6 | async-start | bytes 1048576 | tf_op jit(solution)/shard_map/all_to_all | solution.py:303
  297.0 71.2 %collective-permute-start.30 = (bf16[4,32,5120]{2,1,0:T(8,128)(2,1)}, bf16[4,32,5120]{2,1,0:T(8,128)(2,1)}, u32[]{:S(2)}, u32[]{:S(2)}) collective-permute-start(bf16[4,32,5120]{2,1,0:T(8,128)(2,1)} %copy-done.26), channel_id=1, source_target_pairs={{0,8},{8,0},{16,24},{24,16},{1,9},{9,1},{17,25},{25,17},{2,10},{10... | collective-permute-start | bytes 3932168 | tf_op jit(solution)/shard_map/ppermute | solution.py:62
  299.1 111.9 %collective-permute-start.31 = (bf16[4,32,5120]{2,1,0:T(8,128)(2,1)}, bf16[4,32,5120]{2,1,0:T(8,128)(2,1)}, u32[]{:S(2)}, u32[]{:S(2)}) collective-permute-start(bf16[4,32,5120]{2,1,0:T(8,128)(2,1)} %copy-done.25), channel_id=1, source_target_pairs={{0,16},{8,24},{16,0},{24,8},{1,17},{9,25},{17,1},{25,9},{2,18},{10... | collective-permute-start | bytes 3932168 | tf_op jit(solution)/shard_map/ppermute | solution.py:62
  300.5 110.4 %collective-permute-start.32 = (bf16[4,32,5120]{2,1,0:T(8,128)(2,1)}, bf16[4,32,5120]{2,1,0:T(8,128)(2,1)}, u32[]{:S(2)}, u32[]{:S(2)}) collective-permute-start(bf16[4,32,5120]{2,1,0:T(8,128)(2,1)} %copy-done.24), channel_id=1, source_target_pairs={{0,24},{8,16},{16,8},{24,0},{1,25},{9,17},{17,9},{25,1},{2,26},{10... | collective-permute-start | bytes 3932168 | tf_op jit(solution)/shard_map/ppermute | solution.py:62
  322.5 96.8 %all-to-all-start.5 = ((bf16[4,3,512,128]{3,2,1,0:T(8,128)(2,1)}), bf16[4,3,512,128]{3,2,1,0:T(8,128)(2,1)S(1)}, u32[]{:S(2)}, u32[]{:S(2)}) async-start(bf16[4,3,512,128]{3,2,1,0:T(8,128)(2,1)} %copy-done.18), calls=%async_computation.5 | async-start | bytes 3145728 | tf_op jit(solution)/shard_map/all_to_all | solution.py:303
  414.8 19.9 %collective-permute-start.35 = (bf16[32,5120]{1,0:T(8,128)(2,1)}, bf16[32,5120]{1,0:T(8,128)(2,1)S(1)}, u32[]{:S(2)}, u32[]{:S(2)}) collective-permute-start(bf16[32,5120]{1,0:T(8,128)(2,1)} %bitcast.37), channel_id=1, source_target_pairs={{0,6},{2,0},{4,2},{6,4},{1,7},{3,1},{5,3},{7,5},{8,14},{10,8},{12,... | collective-permute-start | bytes 983048 | tf_op jit(solution)/shard_map/ppermute | solution.py:67
  414.9 19.8 %collective-permute-start.34 = (bf16[32,5120]{1,0:T(8,128)(2,1)}, bf16[32,5120]{1,0:T(8,128)(2,1)S(1)}, u32[]{:S(2)}, u32[]{:S(2)}) collective-permute-start(bf16[32,5120]{1,0:T(8,128)(2,1)} %bitcast.36), channel_id=1, source_target_pairs={{0,4},{2,6},{4,0},{6,2},{1,5},{3,7},{5,1},{7,3},{8,12},{10,14},{12... | collective-permute-start | bytes 983048 | tf_op jit(solution)/shard_map/ppermute | solution.py:67
  415.0 19.7 %collective-permute-start.33 = (bf16[32,5120]{1,0:T(8,128)(2,1)}, bf16[32,5120]{1,0:T(8,128)(2,1)}, u32[]{:S(2)}, u32[]{:S(2)}) collective-permute-start(bf16[32,5120]{1,0:T(8,128)(2,1)} %bitcast.35), channel_id=1, source_target_pairs={{0,2},{2,4},{4,6},{6,0},{1,3},{3,5},{5,7},{7,1},{8,10},{10,12},{12... | collective-permute-start | bytes 983048 | tf_op jit(solution)/shard_map/ppermute | solution.py:67
  419.3 23.8 %all-to-all-start.7 = ((bf16[4,3,512,128]{3,2,1,0:T(8,128)(2,1)}), bf16[4,3,512,128]{3,2,1,0:T(8,128)(2,1)}, u32[]{:S(2)}, u32[]{:S(2)}) async-start(bf16[4,3,512,128]{3,2,1,0:T(8,128)(2,1)} %copy-done.16), calls=%async_computation.8 | async-start | bytes 3145728 | tf_op jit(solution)/shard_map/all_to_all | solution.py:303
  477.8 20.7 %collective-permute-start.44 = (bf16[4,32,3072]{2,1,0:T(8,128)(2,1)}, bf16[4,32,3072]{2,1,0:T(8,128)(2,1)S(1)}, u32[]{:S(2)}, u32[]{:S(2)}) collective-permute-start(bf16[4,32,3072]{2,1,0:T(8,128)(2,1)} %copy-done.29), channel_id=1, source_target_pairs={{0,8},{8,0},{16,24},{24,16},{1,9},{9,1},{17,25},{25,17},{2,10},{10... | collective-permute-start | bytes 2359304 | tf_op jit(solution)/shard_map/ppermute | solution.py:62
  479.2 35.6 %collective-permute-start.45 = (bf16[4,32,3072]{2,1,0:T(8,128)(2,1)}, bf16[4,32,3072]{2,1,0:T(8,128)(2,1)S(1)}, u32[]{:S(2)}, u32[]{:S(2)}) collective-permute-start(bf16[4,32,3072]{2,1,0:T(8,128)(2,1)} %copy-done.28), channel_id=1, source_target_pairs={{0,16},{8,24},{16,0},{24,8},{1,17},{9,25},{17,1},{25,9},{2,18},{10... | collective-permute-start | bytes 2359304 | tf_op jit(solution)/shard_map/ppermute | solution.py:62
  479.8 35.0 %collective-permute-start.46 = (bf16[4,32,3072]{2,1,0:T(8,128)(2,1)}, bf16[4,32,3072]{2,1,0:T(8,128)(2,1)S(1)}, u32[]{:S(2)}, u32[]{:S(2)}) collective-permute-start(bf16[4,32,3072]{2,1,0:T(8,128)(2,1)} %copy-done.27), channel_id=1, source_target_pairs={{0,24},{8,16},{16,8},{24,0},{1,25},{9,17},{17,9},{25,1},{2,26},{10... | collective-permute-start | bytes 2359304 | tf_op jit(solution)/shard_map/ppermute | solution.py:62
  (108 other events, 1057.2 us)
Sparse Core Ops, SparseCore 0:
  11.0 105.5 all-gather.2
  119.6 92.5 all-gather.4
  285.3 98.1 reduce-scatter.1
